TPU v7x, 32 devices: a whole 2x2x4 slice. The times are simulated.
32 devices in a mesh: pix: 8 (over z, y), head: 4 (over x, core).
Axes of the slice: x: 2, y: 2, z: 4, core: 2. Of those that a mesh axis runs over, the one named last changes fastest.
Arguments:
- queries: bfloat16 [4096, 1024], P('pix', 'head'), may hold values from -6 to 6
- keys: bfloat16 [4096, 1024], P('pix', 'head'), may hold values from -6 to 6
- values: bfloat16 [4096, 1024], P('pix', 'head'), may hold values from -24 to 24
- coarse_keys: bfloat16 [64, 1024], P('pix', 'head'), may hold values from -6 to 6
- coarse_values: bfloat16 [64, 1024], P('pix', 'head'), may hold values from -24 to 24
- neighbors: int32 [32, 4], P('pix'), may hold values from 0 to 31, as said below
- pool_map: int32 [4096], P('pix'), may hold values from 0 to 63, as said below
- coarse_mask: int32 [32, 8], P('pix'), may hold values 0 or 1
- w_out: bfloat16 [1024, 1024], P('head'), may hold values from -0.1875 to 0.1875
- grad_mixed: bfloat16 [4096, 1024], P('pix', 'head'), may hold values from -48 to 48
Outputs:
- mixed: bfloat16 [4096, 1024], P('pix', 'head')
- grad_queries: bfloat16 [4096, 1024], P('pix', 'head')
- grad_keys: bfloat16 [4096, 1024], P('pix', 'head')
- grad_values: bfloat16 [4096, 1024], P('pix', 'head')
- grad_coarse_keys: float32 [64, 1024], P('pix', 'head')
- grad_coarse_values: float32 [64, 1024], P('pix', 'head')
- grad_w_out: float32 [1024, 1024], P('head')
Inputs may be any that keep to these rules, and one draw needn't show every extreme that they name: `neighbors`: row b starts with b itself, followed by 4 - 1 different blocks b + o with 1 <= |o| <= 2; where b + o falls outside 0 to 31, b - o stands in its place, so that entries may repeat near the two ends. `pool_map`: the fine pixels of slab s (rows s * 512 to (s + 1) * 512 - 1) map into coarse rows s * 8 to (s + 1) * 8 - 1, and the first 8 pixels of each slab name each of those rows once.
All inputs are finite; a program needn't handle non-finite values. No bound on the sum of `coarse_mask` on one device may be relied on, other than what follows from the above.
Results may differ from a plain program's by a relative error of at most 0.018.
Values may be sent and summed in bfloat16 or wider, within the bound.
No kernel may reach another device: no remote copies, remote signals or barrier semaphores. Data moves between devices by JAX's collectives and lax.ppermute only.
A program may use at most 64 MiB of HBM per device.

v0:
```python
import math

import jax
import jax.numpy as jnp
from jax import lax
from jax.sharding import PartitionSpec as P

HDIM = 64
BLK = 128
NBR = 4
HB = 2
CBLK = 8


def with_halo(cells, sides, width):
    for axis, dim in sides:
        count = lax.axis_size(axis)
        ends = count - 1
        head = lax.slice_in_dim(cells, 0, width, axis=dim)
        tail = lax.slice_in_dim(cells, cells.shape[dim] - width, cells.shape[dim], axis=dim)
        cells = jnp.concatenate(
            [
                lax.ppermute(tail, axis, [(i, (i + 1) % count) for i in range(ends)]),
                cells,
                lax.ppermute(head, axis, [((i + 1) % count, i) for i in range(ends)]),
            ],
            axis=dim,
        )
    return cells


def from_behind(value, axis, by):
    peers = lax.axis_size(axis)
    pairs = [(i, i + by) for i in range(peers) if 0 <= i + by < peers]
    return lax.ppermute(value, axis, pairs)


def head_split(array, head_dim):
    return array.reshape(array.shape[:-1] + (array.shape[-1] // head_dim, head_dim))


def coarse_terms(
    query, grad_out, maxima, totals, dterm, panel_keys, panel_values, allowed_rows, score_scale
):
    scores = score_scale * jnp.einsum(
        "nbhd,rhd->nhbr", query, panel_keys, preferred_element_type=jnp.float32
    )
    scores = jnp.where(allowed_rows[:, None, None, :], scores, -jnp.inf)
    weights = jnp.exp(scores - maxima[..., None]) / totals[..., None]
    dweights = jnp.einsum(
        "nbhd,rhd->nhbr", grad_out, panel_values, preferred_element_type=jnp.float32
    )
    dscores = (weights * (dweights - dterm[..., None])).astype(jnp.bfloat16)
    return (weights.astype(jnp.bfloat16), dscores)


def on_device(
    queries,
    keys,
    values,
    coarse_keys,
    coarse_values,
    neighbors,
    pool_map,
    coarse_mask,
    w_out,
    grad_mixed,
):
    tok_rows, width = queries.shape
    coarse_rows = coarse_keys.shape[0]
    head_dim = HDIM
    heads = width // head_dim
    score_scale = head_dim ** (-0.5)
    local_blocks = tok_rows // BLK
    slab_index = lax.axis_index("pix")
    local_map = pool_map - slab_index * coarse_rows
    member = local_map[None, :] == jnp.arange(coarse_rows, dtype=jnp.int32)[:, None]
    counts = jnp.sum(member.astype(jnp.float32), axis=1)
    sums = jnp.dot(
        member.astype(jnp.bfloat16),
        jnp.concatenate([keys, values], 1),
        preferred_element_type=jnp.float32,
    )
    means = sums / counts[:, None]
    panel_k = (means[:, :width] + coarse_keys.astype(jnp.float32)).astype(jnp.bfloat16)
    panel_v = (means[:, width:] + coarse_values.astype(jnp.float32)).astype(jnp.bfloat16)
    panel = lax.all_gather(jnp.stack([panel_k, panel_v]), "pix", axis=1, tiled=True)
    total_rows = panel.shape[1]
    panel_keys = head_split(panel[0], head_dim)
    panel_values = head_split(panel[1], head_dim)
    rim_rows = HB * BLK
    fine_kv = with_halo(jnp.stack([keys, values]), (("pix", 1),), rim_rows)
    fine_kv = fine_kv.reshape(2, local_blocks + 2 * HB, BLK, heads, head_dim)
    group_blocks = math.gcd(tok_rows, 512) // BLK
    group_count = local_blocks // group_blocks
    listed = (neighbors - slab_index * local_blocks + HB).reshape(group_count, group_blocks, NBR)
    allowed = jnp.repeat(coarse_mask > 0, CBLK, axis=1).reshape(
        group_count, group_blocks, total_rows
    )
    query_groups = head_split(queries, head_dim).reshape(
        group_count, group_blocks, BLK, heads, head_dim
    )

    def fine_pieces(picks):
        fine_keys = fine_kv[0][picks].reshape(group_blocks, NBR * BLK, heads, head_dim)
        fine_values = fine_kv[1][picks].reshape(group_blocks, NBR * BLK, heads, head_dim)
        return (fine_keys, fine_values)

    def forward_group(inputs):
        query, picks, allowed_rows = inputs
        fine_keys, fine_values = fine_pieces(picks)
        fine_scores = score_scale * jnp.einsum(
            "nbhd,nmhd->nhbm", query, fine_keys, preferred_element_type=jnp.float32
        )
        coarse_scores = score_scale * jnp.einsum(
            "nbhd,rhd->nhbr", query, panel_keys, preferred_element_type=jnp.float32
        )
        coarse_scores = jnp.where(allowed_rows[:, None, None, :], coarse_scores, -jnp.inf)
        maxima = jnp.maximum(jnp.max(fine_scores, -1), jnp.max(coarse_scores, -1))
        fine_exp = jnp.exp(fine_scores - maxima[..., None])
        coarse_exp = jnp.exp(coarse_scores - maxima[..., None])
        totals = jnp.sum(fine_exp, -1) + jnp.sum(coarse_exp, -1)
        fine_wb = (fine_exp / totals[..., None]).astype(jnp.bfloat16)
        coarse_wb = (coarse_exp / totals[..., None]).astype(jnp.bfloat16)
        attn_sum = jnp.einsum(
            "nhbm,nmhd->nbhd", fine_wb, fine_values, preferred_element_type=jnp.float32
        )
        attn_sum = attn_sum + jnp.einsum(
            "nhbr,rhd->nbhd", coarse_wb, panel_values, preferred_element_type=jnp.float32
        )
        return (attn_sum.astype(jnp.bfloat16), maxima, totals)

    attn_groups, maxima_all, totals_all = lax.map(forward_group, (query_groups, listed, allowed))
    attn_rows = attn_groups.reshape(tok_rows, width)
    partial_value = jnp.dot(attn_rows, w_out, preferred_element_type=jnp.float32)
    mixed = lax.psum_scatter(partial_value, "head", scatter_dimension=1, tiled=True).astype(
        jnp.bfloat16
    )
    grad_full = lax.all_gather(grad_mixed, "head", axis=1, tiled=True)
    grad_attn = jnp.einsum(
        "tc,wc->tw", grad_full, w_out, preferred_element_type=jnp.float32
    ).astype(jnp.bfloat16)
    wout_term = jnp.einsum("tw,tc->wc", attn_rows, grad_full, preferred_element_type=jnp.float32)
    grad_w_out = lax.psum(wout_term, "pix") * (tok_rows * lax.axis_size("pix")) ** (-0.5)
    grad_groups = head_split(grad_attn, head_dim).reshape(
        group_count, group_blocks, BLK, heads, head_dim
    )

    def backward_group(carry, inputs):
        key_grads, value_grads, coarse_grads = carry
        query, grad_out, attn_block, picks, allowed_rows, maxima, totals = inputs
        fine_keys, fine_values = fine_pieces(picks)
        dterm = jnp.einsum(
            "nbhd,nbhd->nhb", grad_out.astype(jnp.float32), attn_block.astype(jnp.float32)
        )
        fine_scores = score_scale * jnp.einsum(
            "nbhd,nmhd->nhbm", query, fine_keys, preferred_element_type=jnp.float32
        )
        fine_w = jnp.exp(fine_scores - maxima[..., None]) / totals[..., None]
        fine_dw = jnp.einsum(
            "nbhd,nmhd->nhbm", grad_out, fine_values, preferred_element_type=jnp.float32
        )
        fine_ds = (fine_w * (fine_dw - dterm[..., None])).astype(jnp.bfloat16)
        fine_wb = fine_w.astype(jnp.bfloat16)
        coarse_wb, coarse_ds = coarse_terms(
            query,
            grad_out,
            maxima,
            totals,
            dterm,
            panel_keys,
            panel_values,
            allowed_rows,
            score_scale,
        )
        grad_query = jnp.einsum(
            "nhbm,nmhd->nbhd", fine_ds, fine_keys, preferred_element_type=jnp.float32
        )
        grad_query = grad_query + jnp.einsum(
            "nhbr,rhd->nbhd", coarse_ds, panel_keys, preferred_element_type=jnp.float32
        )
        grad_query = (score_scale * grad_query).astype(jnp.bfloat16)
        flat = picks.reshape(-1)
        key_part = score_scale * jnp.einsum(
            "nhbm,nbhd->nmhd", fine_ds, query, preferred_element_type=jnp.float32
        )
        value_part = jnp.einsum(
            "nhbm,nbhd->nmhd", fine_wb, grad_out, preferred_element_type=jnp.float32
        )
        key_grads = key_grads.at[flat].add(key_part.reshape(group_blocks * NBR, BLK, width))
        value_grads = value_grads.at[flat].add(value_part.reshape(group_blocks * NBR, BLK, width))
        return ((key_grads, value_grads, coarse_grads), (grad_query, dterm))

    coarse_start = jnp.zeros((1,), jnp.float32)
    ext_zeros = jnp.zeros((local_blocks + 2 * HB, BLK, width), jnp.float32)
    finals, outputs = lax.scan(
        backward_group,
        (ext_zeros, ext_zeros, coarse_start),
        (query_groups, grad_groups, attn_groups, listed, allowed, maxima_all, totals_all),
    )
    key_grads, value_grads, coarse_grads = finals
    grad_queries = outputs[0].reshape(tok_rows, width)
    dterm_all = outputs[1]

    def add_group(running, inputs):
        query, grad_out, allowed_rows, maxima, totals, dterm = inputs
        coarse_wb, coarse_ds = coarse_terms(
            query,
            grad_out,
            maxima,
            totals,
            dterm,
            panel_keys,
            panel_values,
            allowed_rows,
            score_scale,
        )
        coarse_key_part = score_scale * jnp.einsum(
            "nhbr,nbhd->rhd", coarse_ds, query, preferred_element_type=jnp.float32
        )
        coarse_value_part = jnp.einsum(
            "nhbr,nbhd->rhd", coarse_wb, grad_out, preferred_element_type=jnp.float32
        )
        update = jnp.concatenate(
            [
                coarse_key_part.reshape(lax.axis_size("pix") * coarse_rows, width),
                coarse_value_part.reshape(lax.axis_size("pix") * coarse_rows, width),
            ],
            1,
        )
        return (running + update, None)

    result, unused = lax.scan(
        add_group,
        jnp.zeros((lax.axis_size("pix") * coarse_rows, 2 * width), jnp.float32),
        (query_groups, grad_groups, allowed, maxima_all, totals_all, dterm_all),
    )
    coarse_own = lax.psum_scatter(result, "pix", scatter_dimension=0, tiled=True)
    both_grads = jnp.stack([key_grads, value_grads])
    from_above = from_behind(both_grads[:, :HB], "pix", -1)
    from_below = from_behind(
        both_grads[:, local_blocks + HB :].astype(jnp.bfloat16), "pix", 1
    ).astype(jnp.float32)
    own_grads = both_grads[:, HB : HB + local_blocks]
    own_grads = own_grads.at[:, local_blocks - HB :].add(from_above)
    own_grads = own_grads.at[:, :HB].add(from_below)
    own_grads = own_grads.reshape(2, tok_rows, width)
    per_row = coarse_own / counts[:, None]
    pooled_back = jnp.dot(member.astype(jnp.float32).T, per_row, precision=lax.Precision.HIGHEST)
    grad_keys = (own_grads[0] + pooled_back[:, :width]).astype(jnp.bfloat16)
    grad_values = (own_grads[1] + pooled_back[:, width:]).astype(jnp.bfloat16)
    return (
        mixed,
        grad_queries,
        grad_keys,
        grad_values,
        coarse_own[:, :width],
        coarse_own[:, width:],
        grad_w_out,
    )


def solution(mesh):
    in_specs = (
        P("pix", "head"),
        P("pix", "head"),
        P("pix", "head"),
        P("pix", "head"),
        P("pix", "head"),
        P("pix", None),
        P("pix"),
        P("pix", None),
        P("head", None),
        P("pix", "head"),
    )
    out_specs = (
        P("pix", "head"),
        P("pix", "head"),
        P("pix", "head"),
        P("pix", "head"),
        P("pix", "head"),
        P("pix", "head"),
        P("head", None),
    )
    return jax.shard_map(
        on_device, mesh=mesh, in_specs=in_specs, out_specs=out_specs, check_vma=False
    )
```

profile of v0, /device:TPU:0, one launch (start us, length us, event | category | flops | bytes accessed | tf_op | source)
XLA Modules:
  0.0 259.5 jit_solution(12877071800469402210)
XLA Ops:
  7.3 1.2 fusion.36
  8.5 4.9 %collective-permute-start = (bf16[2,256,256]{2,1,0:T(8,128)(2,1)S(1)}, bf16[2,256,256]{2,1,0:T(8,128)(2,1)S(1)}, u32[]{:S(2)}, u32[]{:S(2)}) collective-permute-start(bf16[2,256,256]{2,1,0:T(8,128)(2,1)S(1)} %get-tuple-element.177), channel_id=1, source_target_pairs={{0,4},{4,8},{8,12},{12,16},{16,20},{20,24},{24,28},{1,5},{5,9},{9,... | collective-permute-start | bytes 786440 | tf_op jit(solution)/shard_map/ppermute | solution.py:23
  13.4 1.3 collective-permute-start.1
  14.8 0.7 broadcast_subtract_fusion
  15.6 1.2 convolution_divide_fusion
  16.9 33.7 %all_gather.6 = bf16[2,64,256]{2,1,0:T(8,128)(2,1)S(1)} all-gather(bf16[2,8,256]{2,1,0:T(8,128)(2,1)S(1)} %pad_maximum_fusion.4), channel_id=1, replica_groups=mesh['pix'=8,'head'=4] {'pix'}, dimensions={1}, use_global_device_ids=true | all-gather | bytes 73728 | tf_op jit(solution)/shard_map/all_gather | solution.py:87
  51.9 0.7 copy.226
  52.7 0.8 fusion.76
  53.6 0.9 fusion.73
  55.4 0.7 gather_fusion.1
  57.4 0.9 bitcast_reduce_fusion
  58.5 0.7 fusion.2
  59.2 1.1 copy-done.1
  61.9 0.7 gather_fusion
  63.4 1.2 reshape.197
  64.7 1.0 convolution_bitcast_fusion.4
  65.7 1.8 convolution_convert_fusion
  68.0 4.2 %multiply_reduce_fusion = (f32[4,4,128]{2,1,0:T(4,128)S(1)}, bf16[4,128,4,64]{1,3,2,0:T(8,128)(2,1)}) fusion(f32[4,4,128,64]{2,0,3,1:T(4,128)S(1)} %bitcast_convert_fusion, f32[4,128,4,64]{1,3,2,0:T(8,128)} %convolution_bitcast_fusion.4, f32[4,4,128]{2,1,0:T(4,128)S(1)} %copy-done.19, f32[4,4,128]{2,1,0:T(4,128)S(1)} %copy_maximum_fusion, ...), kind=kOutput, calls=%fused_computation.65 | convolution fusion | flops 139065344 | bytes 6578176 | tf_op jit(solution)/shard_map/while/body/eval_jaxpr/nhbm,nmhd->nbhd/dot_general | solution.py:125
  73.8 1.2 copy.228
  74.9 1.4 fusion.37
  76.8 1.9 fusion.39
  78.7 4.5 %convolution_bitcast_fusion = f32[4,512,4,64]{1,3,2,0:T(8,128)} fusion(bf16[4,128,4,64]{1,0,3,2:T(4,128)(2,1)S(1)} %squeeze.61, f32[4,4,512,128]{3,2,1,0:T(8,128)} %copy-done.1, f32[4,4,128]{2,1,0:T(4,128)S(1)} %copy-done.19, f32[4,4,128]{2,1,0:T(4,128)S(1)} %copy_maximum_fusion), kind=kOutput, calls=%fused_computation.17 | convolution fusion | flops 138412032 | bytes 6569984 | tf_op jit(solution)/shard_map/while/body/eval_jaxpr/nhbm,nbhd->nmhd/dot_general | solution.py:187
  83.2 4.9 %copy.279 = f32[4,512,4,64]{3,2,1,0:T(4,128)} copy(f32[4,512,4,64]{1,3,2,0:T(8,128)} %convolution_bitcast_fusion) | data formatting | bytes 4194304 | tf_op jit(solution)/shard_map/while/body/eval_jaxpr/reshape | solution.py:191
  88.1 5.4 %reshape.257 = f32[16,128,256]{2,1,0:T(8,128)} reshape(f32[4,512,4,64]{3,2,1,0:T(4,128)} %copy.279) | data formatting | bytes 4194304 | tf_op jit(solution)/shard_map/while/body/eval_jaxpr/reshape | solution.py:191
  93.5 3.8 %multiply_convert_fusion = bf16[4,4,128,512]{2,3,1,0:T(8,128)(2,1)S(1)} fusion(f32[4,4,128]{2,1,0:T(4,128)S(1)} %get-tuple-element.191, bf16[4,512,4,64]{1,0,3,2:T(4,128)(2,1)S(1)} %copy-done.9, bf16[4,128,4,64]{1,0,3,2:T(4,128)(2,1)S(1)} %squeeze.61, f32[4,4,128]{2,1,0:T(4,128)S(1)} %copy-done.19, f32[4,4,128]{2,1,0:T(4,128)S(1)} %copy_maximum_fusion, ...), kind=kOutput, calls=%fused_computation.7 | convolution fusion | flops 140509184 | bytes 7626752 | tf_op jit(solution)/shard_map/while/body/eval_jaxpr/nbhd,nmhd->nhbm/dot_general | solution.py:160
  97.3 1.4 copy-done.4
  98.7 0.9 multiply_bitcast_fusion
  99.5 3.1 %copy.278 = f32[4,512,4,64]{3,2,1,0:T(4,128)} copy(f32[4,512,4,64]{1,3,2,0:T(8,128)S(1)} %multiply_bitcast_fusion) | data formatting | bytes 4194304 | tf_op jit(solution)/shard_map/while/body/eval_jaxpr/reshape | solution.py:190
  102.7 5.3 %reshape.256 = f32[16,128,256]{2,1,0:T(8,128)} reshape(f32[4,512,4,64]{3,2,1,0:T(4,128)} %copy.278) | data formatting | bytes 4194304 | tf_op jit(solution)/shard_map/while/body/eval_jaxpr/reshape | solution.py:190
  108.1 3.5 %scatter_fusion.1 = f32[8,128,256]{2,1,0:T(8,128)S(1)} fusion(f32[8,128,256]{2,1,0:T(8,128)S(1)} %broadcast_in_dim.100.clone.1, s32[16]{0:T(128)S(1)} %fusion.68, f32[16,128,256]{2,1,0:T(8,128)} %reshape.257), kind=kCustom, calls=%fused_computation.3 | custom fusion | flops 524288 | bytes 6291520 | tf_op jit(solution)/shard_map/while/body/eval_jaxpr/scatter-add | solution.py:191
  111.7 3.5 %scatter_fusion = f32[8,128,256]{2,1,0:T(8,128)S(1)} fusion(f32[8,128,256]{2,1,0:T(8,128)S(1)} %broadcast_in_dim.100.clone, s32[16]{0:T(128)S(1)} %fusion.68, f32[16,128,256]{2,1,0:T(8,128)} %reshape.256), kind=kCustom, calls=%fused_computation.2 | custom fusion | flops 524288 | bytes 6291520 | tf_op jit(solution)/shard_map/while/body/eval_jaxpr/scatter-add | solution.py:190
  115.2 0.7 fusion.29
  115.9 2.4 collective-permute-start.3
  118.3 0.8 fusion.23
  119.1 1.8 collective-permute-start.2
  120.9 1.1 fusion.15
  123.2 1.0 reshape.255
  124.2 9.8 %reduce-scatter.5.cloned.1.call-done = f32[8,512]{1,0:T(8,128)} async-done(((f32[64,512]{1,0:T(8,128)}), f32[8,512]{1,0:T(8,128)}) %reduce-scatter.5.cloned.1.call-update) | async-done | bytes 16400 | tf_op jit(solution)/shard_map/reduce_scatter | solution.py:238
  134.1 1.4 fusion.59
  135.4 1.3 fusion.75
  136.7 1.9 fusion.26
  138.6 2.0 fusion.30
  140.6 1.3 fusion.72
  141.9 0.9 fusion.27
  142.8 74.7 %all-reduce.2.cloned.1.call-done = f32[256,1024]{1,0:T(8,128)} async-done(((f32[256,1024]{1,0:T(8,128)}), f32[256,1024]{1,0:T(8,128)}) %all-reduce.2.cloned.1.call-update) | async-done | bytes 1048592 | tf_op jit(solution)/shard_map/psum | solution.py:144
  217.6 2.3 broadcast_multiply_fusion
  219.9 31.3 %reduce-scatter.3.cloned.1.call-done = f32[512,256]{1,0:T(8,128)} async-done(((f32[512,1024]{1,0:T(8,128)}), f32[512,256]{1,0:T(8,128)}) %reduce-scatter.3.cloned.1.call-update) | async-done | bytes 524304 | tf_op jit(solution)/shard_map/reduce_scatter | solution.py:136
  251.2 1.8 convert_element_type.75
  (122 shorter events, 9.9 us)
Async XLA Ops:
  7.2 58.6 %copy-start = (bf16[256,1024]{1,0:T(8,128)(2,1)S(1)}, bf16[256,1024]{1,0:T(8,128)(2,1)}, u32[]{:S(2)}) copy-start(bf16[256,1024]{1,0:T(8,128)(2,1)} %param.22) | copy-start | bytes 1572868
  7.2 9.7 %copy-start.26 = (bf16[8,256]{1,0:T(8,128)(2,1)S(1)}, bf16[8,256]{1,0:T(8,128)(2,1)}, u32[]{:S(2)}) copy-start(bf16[8,256]{1,0:T(8,128)(2,1)} %param.17) | copy-start | bytes 12292
  7.2 9.7 %copy-start.27 = (bf16[8,256]{1,0:T(8,128)(2,1)S(1)}, bf16[8,256]{1,0:T(8,128)(2,1)}, u32[]{:S(2)}) copy-start(bf16[8,256]{1,0:T(8,128)(2,1)} %param.18) | copy-start | bytes 12292
  7.2 43.4 %copy-start.30 = (s32[4,8]{1,0:T(4,128)S(1)}, s32[4,8]{1,0:T(4,128)}, u32[]{:S(2)}) copy-start(s32[4,8]{1,0:T(4,128)} %param.21) | copy-start | bytes 388
  7.2 43.4 %copy-start.31 = (s32[4,4]{1,0:T(4,128)S(1)}, s32[4,4]{1,0:T(4,128)}, u32[]{:S(2)}) copy-start(s32[4,4]{1,0:T(4,128)} %param.19) | copy-start | bytes 196
  7.2 44.2 %copy-start.14 = (bf16[512,256]{1,0:T(8,128)(2,1)S(1)}, bf16[512,256]{1,0:T(8,128)(2,1)}, u32[]{:S(2)}) copy-start(bf16[512,256]{1,0:T(8,128)(2,1)} %param.14) | copy-start | bytes 786436
  7.2 58.5 %all-gather.2.cloned.1.call-start = ((), (), s32[]{:S(2)}) async-start(), calls=%async_computation.3 | async-start | bytes 1310720 | tf_op jit(solution)/shard_map/all_gather | solution.py:139
  7.3 46.2 %copy-start.12 = (bf16[512,256]{1,0:T(8,128)(2,1)S(1)}, bf16[512,256]{1,0:T(8,128)(2,1)}, u32[]{:S(2)}) copy-start(bf16[512,256]{1,0:T(8,128)(2,1)} %param.15) | copy-start | bytes 786436
  7.3 46.2 %copy-start.13 = (bf16[512,256]{1,0:T(8,128)(2,1)S(1)}, bf16[512,256]{1,0:T(8,128)(2,1)}, u32[]{:S(2)}) copy-start(bf16[512,256]{1,0:T(8,128)(2,1)} %param.16) | copy-start | bytes 786436
  8.5 45.0 %collective-permute-start = (bf16[2,256,256]{2,1,0:T(8,128)(2,1)S(1)}, bf16[2,256,256]{2,1,0:T(8,128)(2,1)S(1)}, u32[]{:S(2)}, u32[]{:S(2)}) collective-permute-start(bf16[2,256,256]{2,1,0:T(8,128)(2,1)S(1)} %get-tuple-element.177), channel_id=1, source_target_pairs={{0,4},{4,8},{8,12},{12,16},{16,20},{20,24},{24,28},{1,5},{5,9},{9,... | collective-permute-start | bytes 786440 | tf_op jit(solution)/shard_map/ppermute | solution.py:23
  13.4 40.1 %collective-permute-start.1 = (bf16[2,256,256]{2,1,0:T(8,128)(2,1)S(1)}, bf16[2,256,256]{2,1,0:T(8,128)(2,1)S(1)}, u32[]{:S(2)}, u32[]{:S(2)}) collective-permute-start(bf16[2,256,256]{2,1,0:T(8,128)(2,1)S(1)} %get-tuple-element.178), channel_id=1, source_target_pairs={{4,0},{8,4},{12,8},{16,12},{20,16},{24,20},{28,24},{5,1},{9,5},{13... | collective-permute-start | bytes 786440 | tf_op jit(solution)/shard_map/ppermute | solution.py:25
  14.8 119.3 %reduce-scatter.5.cloned.1.call-start = ((), (), s32[]{:S(2)}) async-start(), calls=%async_computation.4 | async-start | bytes 147456 | tf_op jit(solution)/shard_map/reduce_scatter | solution.py:238
  15.5 1.4 copy-start.20
  15.6 1.3 copy-start.28
  51.3 4.1 %copy-start.22 = (s32[1024]{0:T(1024)}, s32[1024]{0:T(1024)S(1)}, u32[]{:S(2)}) copy-start(s32[1024]{0:T(1024)S(1)} %pad_clamp_fusion) | copy-start | bytes 12292
  57.3 1.0 copy-start.2
  57.4 1.0 copy-start.24
  58.4 1.9 copy-start.1
  58.5 2.4 copy-start.6
  60.3 1.6 copy-start.23
  60.3 1.6 copy-start.18
  63.4 1.2 copy-start.16
  63.4 1.3 copy-start.15
  65.7 2.3 copy-start.8
  65.7 2.3 copy-start.19
  68.0 4.2 %copy-start.17 = (f32[4,4,128]{2,0,1:T(4,128)S(1)}, f32[4,4,128]{2,0,1:T(4,128)}, u32[]{:S(2)}) copy-start(f32[4,4,128]{2,0,1:T(4,128)} %copy.225) | copy-start | bytes 24580
  72.2 2.7 %copy-start.7 = (bf16[512,1024]{1,0:T(8,128)(2,1)S(1)}, bf16[512,1024]{1,0:T(8,128)(2,1)}, u32[]{:S(2)}) copy-start(bf16[512,1024]{1,0:T(8,128)(2,1)} %all-gather.2.cloned.1.call-done) | copy-start | bytes 3145732
  72.5 1.3 copy-start.10
  73.7 3.0 %copy-start.25 = (s32[4,4]{1,0:T(4,128)S(1)}, s32[4,4]{1,0:T(4,128)}, u32[]{:S(2)}) copy-start(s32[4,4]{1,0:T(4,128)} %get-tuple-element.185) | copy-start | bytes 196
  73.7 143.9 %all-reduce.2.cloned.1.call-start = ((), (), s32[]{:S(2)}) async-start(), calls=%async_computation.5 | async-start | bytes 2097152 | tf_op jit(solution)/shard_map/psum | solution.py:144
  76.4 174.8 %reduce-scatter.3.cloned.1.call-start = ((), (), s32[]{:S(2)}) async-start(), calls=%async_computation.2 | async-start | bytes 2621440 | tf_op jit(solution)/shard_map/reduce_scatter | solution.py:136
  88.1 5.4 %copy-start.9 = (bf16[4,512,4,64]{1,0,3,2:T(4,128)(2,1)S(1)}, bf16[4,512,4,64]{1,0,3,2:T(4,128)(2,1)}, u32[]{:S(2)}) copy-start(bf16[4,512,4,64]{1,0,3,2:T(4,128)(2,1)} %reshape.197) | copy-start | bytes 3145732
  97.3 1.4 copy-start.4
  115.9 22.7 %collective-permute-start.3 = (bf16[2,2,128,256]{3,2,1,0:T(8,128)(2,1)}, bf16[2,2,128,256]{3,2,1,0:T(8,128)(2,1)}, u32[]{:S(2)}, u32[]{:S(2)}) collective-permute-start(bf16[2,2,128,256]{3,2,1,0:T(8,128)(2,1)} %fusion.29), channel_id=1, source_target_pairs={{0,4},{4,8},{8,12},{12,16},{16,20},{20,24},{24,28},{1,5},{5,9},{9,... | collective-permute-start | bytes 786440 | tf_op jit(solution)/shard_map/ppermute | solution.py:35
  118.3 3.7 %copy-start.11 = (bf16[4,4,128,64]{2,3,0,1:T(8,128)(2,1)S(1)}, bf16[4,4,128,64]{2,3,0,1:T(8,128)(2,1)}, u32[]{:S(2)}) copy-start(bf16[4,4,128,64]{2,3,0,1:T(8,128)(2,1)} %copy-done.10) | copy-start | bytes 786436
  119.1 3.1 %copy-start.3 = (bf16[4,512,4,64]{1,0,3,2:T(4,128)(2,1)S(1)}, bf16[4,512,4,64]{1,0,3,2:T(4,128)(2,1)}, u32[]{:S(2)}) copy-start(bf16[4,512,4,64]{1,0,3,2:T(4,128)(2,1)} %copy-done.2) | copy-start | bytes 3145732
  119.1 3.1 %copy-start.5 = (bf16[4,4,128,512]{2,3,1,0:T(8,128)(2,1)S(1)}, bf16[4,4,128,512]{2,3,1,0:T(8,128)(2,1)}, u32[]{:S(2)}) copy-start(bf16[4,4,128,512]{2,3,1,0:T(8,128)(2,1)} %copy-done.4) | copy-start | bytes 6291460
  119.1 17.6 %collective-permute-start.2 = (f32[2,2,128,256]{3,2,1,0:T(8,128)}, f32[2,2,128,256]{3,2,1,0:T(8,128)}, u32[]{:S(2)}, u32[]{:S(2)}) collective-permute-start(f32[2,2,128,256]{3,2,1,0:T(8,128)} %fusion.23), channel_id=1, source_target_pairs={{4,0},{8,4},{12,8},{16,12},{20,16},{24,20},{28,24},{5,1},{9,5},{13... | collective-permute-start | bytes 1572872 | tf_op jit(solution)/shard_map/ppermute | solution.py:35
  122.2 11.8 %copy-start.21 = (s32[512]{0:T(512)S(1)}, s32[512]{0:T(512)}, u32[]{:S(2)}) copy-start(s32[512]{0:T(512)} %copy-done.20) | copy-start | bytes 6148
  122.2 11.8 %copy-start.29 = (f32[8]{0:T(128)S(1)}, f32[8]{0:T(128)}, u32[]{:S(2)}) copy-start(f32[8]{0:T(128)} %copy-done.28) | copy-start | bytes 100
Sparse Core Ops, SparseCore 0:
  14.9 19.2 all-gather.1
  73.8 60.1 reduce-scatter.4
  137.6 79.9 all-reduce.1
  220.1 31.0 reduce-scatter.2
where the time goes:
time: 260 us; the launch traced here: 259 us
  waiting for transfers between devices  116 us (45%)
  local copies, waits for them, and re-layouts  36.7 us (14%)
  blocking collectives  33.7 us (13%)
  matrix products  25.2 us (10%)
  other arithmetic  22.9 us (9%)
  between operations  14.4 us (6%)
  starting transfers between devices  10.7 us (4%)
    psum x1, waiting for transfers between devices, on_device(): lax.psum(wout_term, 'pix') * (tok_rows * lax.axis_size('pix')) ** (-0.5)  74.7 us
    all_gather x1, blocking collectives, on_device(): lax.all_gather(jnp.stack([panel_k, panel_v]), 'pix', axis=1, tiled=True)  33.7 us
    reduce_scatter x1, waiting for transfers between devices, on_device(): lax.psum_scatter(partial_value, 'head', scatter_dimension=1, tiled=True)  31.3 us
    reshape x2, local copies, waits for them, and re-layouts, backward_group(): value_part.reshape(group_blocks * NBR, BLK, width)  10.3 us
    reduce_scatter x1, waiting for transfers between devices, on_device(): lax.psum_scatter(result, 'pix', scatter_dimension=0, tiled=True)  9.83 us
    reshape x2, local copies, waits for them, and re-layouts, backward_group(): key_part.reshape(group_blocks * NBR, BLK, width)  8.48 us
  transfers between devices with their start and end apart: 8, of which 3 were waited for; matrix products, arithmetic and copies ran while one was open for 27% of the time, Pallas kernels for 0%

commit v1 on v0

v1 whole, which is shorter than its diff:
```python
import functools
import math

import jax
import jax.numpy as jnp
from jax import lax
from jax.experimental import pallas as pl
from jax.experimental.pallas import tpu as pltpu
from jax.sharding import PartitionSpec as P

HDIM = 64
BLK = 128
NBR = 4
HB = 2
CBLK = 8
RIM = HB * BLK
SCALE = HDIM ** (-0.5)
LOG2E = math.log2(math.e)
BF = jnp.bfloat16
F32 = jnp.float32
VMEM = pl.BlockSpec(memory_space=pltpu.VMEM)
SMEM = pl.BlockSpec(memory_space=pltpu.SMEM)


def mm(a, b):
    return jnp.dot(a, b, preferred_element_type=F32)


def mm_t(a, b):
    return lax.dot_general(a, b, (((1,), (1,)), ((), ())), preferred_element_type=F32)


def t_mm(a, b):
    return lax.dot_general(a, b, (((0,), (0,)), ((), ())), preferred_element_type=F32)


def bit_list(count):
    return [1 << i for i in range(count.bit_length() - 1)]


def swap(value, axis, bit):
    return lax.ppermute(value, axis, [(i, i ^ bit) for i in range(lax.axis_size(axis))])


def reversed_bits(index, levels):
    out = 0
    for level in range(levels):
        out = out * 2 + ((index >> level) & 1)
    return out


def call(body, outs, scratch=(), smem=(), count=0, flops=0, bytes_accessed=0):
    return pl.pallas_call(
        body,
        out_shape=[jax.ShapeDtypeStruct(s, t) for s, t in outs],
        in_specs=[SMEM if i in smem else VMEM for i in range(count)],
        out_specs=[VMEM] * len(outs),
        scratch_shapes=list(scratch),
        compiler_params=pltpu.CompilerParams(vmem_limit_bytes=48 * 1024 * 1024),
        cost_estimate=pl.CostEstimate(
            flops=flops, bytes_accessed=bytes_accessed, transcendentals=0
        ),
    )


def membership(pool_ref, rows):
    me = lax.axis_index("pix")
    local = pool_ref[...] - me * rows
    count = pool_ref.shape[1]
    return local == lax.broadcasted_iota(jnp.int32, (rows, count), 0)


def prep_kernel(k_ref, v_ref, ck_ref, cv_ref, pool_ref, lo_ref, hi_ref, panel_ref):
    tok = k_ref.shape[0]
    lo_ref[0:RIM] = k_ref[0:RIM]
    lo_ref[RIM:] = v_ref[0:RIM]
    hi_ref[0:RIM] = k_ref[tok - RIM :]
    hi_ref[RIM:] = v_ref[tok - RIM :]
    member = membership(pool_ref, ck_ref.shape[0]).astype(F32)
    counts = jnp.sum(member, axis=1, keepdims=True)
    member = member.astype(BF)
    panel_k = mm(member, k_ref[...]) / counts + ck_ref[...].astype(F32)
    panel_v = mm(member, v_ref[...]) / counts + cv_ref[...].astype(F32)
    panel_ref[...] = jnp.concatenate([panel_k, panel_v], 0).astype(BF)


def grad_kernel(*refs):
    pieces, w_ref, go_ref = refs[:-2], refs[-2], refs[-1]
    me = lax.axis_index("head")
    width = w_ref.shape[0]
    total = None
    for j, ref in enumerate(pieces):
        w = w_ref[:, pl.ds(pl.multiple_of((me ^ j) * width, width), width)]
        part = mm_t(ref[...], w)
        total = part if total is None else total + part
    go_ref[...] = total.astype(BF)


def head_masks(width, rows):
    lane = lax.broadcasted_iota(jnp.int32, (rows, width), 1)
    return [(lane >= h * HDIM) & (lane < (h + 1) * HDIM) for h in range(width // HDIM)]


def stacked(block, masks):
    zero = jnp.zeros_like(block)
    return jnp.concatenate([jnp.where(m, block, zero) for m in masks], 0)


def unstacked(tall, masks):
    rows = tall.shape[0] // len(masks)
    out = tall[0:rows]
    for h in range(1, len(masks)):
        out = jnp.where(masks[h], tall[h * rows : (h + 1) * rows], out)
    return out


def extend(ext_k, ext_v, k_ref, v_ref, prev_ref, next_ref):
    tok = k_ref.shape[0]
    ext_k[0:RIM] = prev_ref[0:RIM]
    ext_v[0:RIM] = prev_ref[RIM:]
    ext_k[RIM : RIM + tok] = k_ref[...]
    ext_v[RIM : RIM + tok] = v_ref[...]
    ext_k[RIM + tok :] = next_ref[0:RIM]
    ext_v[RIM + tok :] = next_ref[RIM:]


def panel_parts(panel_ref, rows):
    width = panel_ref.shape[1]
    slots = panel_ref.shape[0] // (2 * rows)
    both = panel_ref[...].astype(F32).reshape(slots, 2 * rows, width)
    keys = both[:, :rows].reshape(slots * rows, width).astype(BF)
    values = both[:, rows:].reshape(slots * rows, width).astype(BF)
    return keys, values


def picks(nbr_ref, block, blocks):
    me = lax.axis_index("pix")
    starts = []
    for n in range(NBR):
        index = nbr_ref[block, n] - me * blocks + HB
        starts.append(pl.multiple_of(index * BLK, BLK))
    return starts


def gathered(ext, starts, panel):
    return jnp.concatenate([ext[pl.ds(s, BLK), :] for s in starts] + [panel], 0)


def forward_kernel(rows, levels, pieces_count, *refs):
    (nbr_ref, mask_ref, q_ref, k_ref, v_ref, prev_ref, next_ref, panel_ref, w_ref) = refs[:9]
    pieces = refs[9 : 9 + pieces_count]
    (attn_ref, p_ref, mix_keep, mix_send, gw_keep, gw_send, ext_k, ext_v, gw_all) = refs[
        9 + pieces_count :
    ]
    tok, width = q_ref.shape
    blocks = tok // BLK
    me = lax.axis_index("pix")
    me_head = lax.axis_index("head")
    extend(ext_k, ext_v, k_ref, v_ref, prev_ref, next_ref)
    panel_k, panel_v = panel_parts(panel_ref, rows)
    coarse = panel_k.shape[0]
    cols = mask_ref.shape[1]
    row = lax.broadcasted_iota(jnp.int32, (cols, coarse), 1)
    owner_row = ((row // rows) ^ me) * rows + row % rows
    pick = (owner_row // CBLK) == lax.broadcasted_iota(jnp.int32, (cols, coarse), 0)
    allowed = mm((mask_ref[...] > 0).astype(BF), pick.astype(BF))
    masks = head_masks(width, BLK)
    for b in range(blocks):
        starts = picks(nbr_ref, b, blocks)
        q_tall = stacked(q_ref[b * BLK : (b + 1) * BLK], masks)
        scores = mm_t(q_tall, gathered(ext_k, starts, panel_k)) * (SCALE * LOG2E)
        fine = scores[:, : NBR * BLK]
        lo = jnp.where(allowed[b : b + 1] > 0.5, scores[:, NBR * BLK :], -jnp.inf)
        top = jnp.maximum(
            jnp.max(fine, axis=1, keepdims=True), jnp.max(lo, axis=1, keepdims=True)
        )
        fine = jnp.exp2(fine - top)
        lo = jnp.exp2(lo - top)
        total = jnp.sum(fine, axis=1, keepdims=True) + jnp.sum(lo, axis=1, keepdims=True)
        scale = 1.0 / total
        weights = jnp.concatenate([fine * scale, lo * scale], 1).astype(BF)
        p_ref[b] = weights
        out = mm(weights, gathered(ext_v, starts, panel_v))
        attn_ref[b * BLK : (b + 1) * BLK] = unstacked(out, masks).astype(BF)
    attn = attn_ref[...]
    for j in range(pieces_count):
        w = w_ref[:, pl.ds(pl.multiple_of((me_head ^ j) * width, width), width)]
        part = mm(attn, w).astype(BF)
        target = mix_send if j & 1 else mix_keep
        target[(j >> 1) * tok : ((j >> 1) + 1) * tok] = part
    chunk = width >> levels
    mine = reversed_bits(me, levels)
    for j in range(pieces_count):
        part = t_mm(attn, pieces[j][...]).astype(BF)
        lanes = pl.ds(pl.multiple_of((me_head ^ j) * width, width), width)
        for c in range(1 << levels):
            place = pl.ds(pl.multiple_of((c ^ mine) * chunk, chunk), chunk)
            gw_all[place, lanes] = part[c * chunk : (c + 1) * chunk]
    gw_keep[...] = gw_all[: width // 2]
    gw_send[...] = gw_all[width // 2 :]


def backward_kernel(rows, *refs):
    (nbr_ref, q_ref, k_ref, v_ref, prev_ref, next_ref, panel_ref, go_ref, attn_ref, p_ref) = refs[
        :10
    ]
    (dq_ref, own_ref, to_prev, to_next, coarse_ref, ext_k, ext_v, sum_k, sum_v) = refs[10:]
    tok, width = q_ref.shape
    blocks = tok // BLK
    extend(ext_k, ext_v, k_ref, v_ref, prev_ref, next_ref)
    panel_k, panel_v = panel_parts(panel_ref, rows)
    coarse = panel_k.shape[0]
    masks = head_masks(width, BLK)
    sum_k[...] = jnp.zeros_like(sum_k)
    sum_v[...] = jnp.zeros_like(sum_v)
    coarse_k = jnp.zeros((coarse, width), F32)
    coarse_v = jnp.zeros((coarse, width), F32)
    heads = len(masks)
    for b in range(blocks):
        span = slice(b * BLK, (b + 1) * BLK)
        starts = picks(nbr_ref, b, blocks)
        q_tall = stacked(q_ref[span], masks)
        g_tall = stacked(go_ref[span], masks)
        attn = attn_ref[span].astype(F32)
        dterm = jnp.sum(
            g_tall.astype(F32) * jnp.concatenate([attn] * heads, 0), axis=1, keepdims=True
        )
        weights = p_ref[b]
        slope = mm_t(g_tall, gathered(ext_v, starts, panel_v))
        ds = (weights.astype(F32) * (slope - dterm)).astype(BF)
        dq = unstacked(mm(ds, gathered(ext_k, starts, panel_k)), masks)
        dq_ref[span] = (SCALE * dq).astype(BF)
        dk = SCALE * t_mm(ds, q_tall)
        dv = t_mm(weights, g_tall)
        for n in range(NBR):
            place = pl.ds(starts[n], BLK)
            sum_k[place, :] += dk[n * BLK : (n + 1) * BLK]
            sum_v[place, :] += dv[n * BLK : (n + 1) * BLK]
        coarse_k = coarse_k + dk[NBR * BLK :]
        coarse_v = coarse_v + dv[NBR * BLK :]
    own_ref[0:tok] = sum_k[RIM : RIM + tok]
    own_ref[tok:] = sum_v[RIM : RIM + tok]
    to_prev[0:RIM] = sum_k[0:RIM].astype(BF)
    to_prev[RIM:] = sum_v[0:RIM].astype(BF)
    to_next[0:RIM] = sum_k[RIM + tok :].astype(BF)
    to_next[RIM:] = sum_v[RIM + tok :].astype(BF)
    for j in range(coarse // rows):
        coarse_ref[2 * j * rows : (2 * j + 1) * rows] = coarse_k[j * rows : (j + 1) * rows]
        coarse_ref[(2 * j + 1) * rows : (2 * j + 2) * rows] = coarse_v[j * rows : (j + 1) * rows]


def finish_kernel(own_ref, below_ref, above_ref, coarse_ref, pool_ref, gk_ref, gv_ref, ck_ref, cv_ref):
    tok, width = gk_ref.shape
    rows = ck_ref.shape[0]
    member = membership(pool_ref, rows).astype(F32)
    counts = jnp.sum(member, axis=1, keepdims=True)
    member = member.astype(BF)
    ck_ref[...] = coarse_ref[0:rows]
    cv_ref[...] = coarse_ref[rows:]
    member = jnp.concatenate([member, member], 0)
    for which, out in ((0, gk_ref), (1, gv_ref)):
        per_row = coarse_ref[which * rows : (which + 1) * rows] / counts
        high = per_row.astype(BF)
        low = (per_row - high.astype(F32)).astype(BF)
        pooled = t_mm(member, jnp.concatenate([high, low], 0))
        grads = own_ref[which * tok : (which + 1) * tok] + pooled
        half = slice(which * RIM, (which + 1) * RIM)
        head = grads[0:RIM] + below_ref[half].astype(F32)
        tail = grads[tok - RIM :] + above_ref[half].astype(F32)
        if tok >= 2 * RIM:
            out[0:RIM] = head.astype(BF)
            if tok > 2 * RIM:
                out[RIM : tok - RIM] = grads[RIM : tok - RIM].astype(BF)
            out[tok - RIM :] = tail.astype(BF)


def gw_kernel(levels, factor, in_ref, out_ref):
    me = lax.axis_index("pix")
    width = out_ref.shape[0]
    chunk = width >> levels
    mine = reversed_bits(me, levels)
    for c in range(1 << levels):
        place = pl.ds(pl.multiple_of((c ^ mine) * chunk, chunk), chunk)
        out_ref[c * chunk : (c + 1) * chunk] = in_ref[place, :].astype(F32) * factor


def on_device(
    queries,
    keys,
    values,
    coarse_keys,
    coarse_values,
    neighbors,
    pool_map,
    coarse_mask,
    w_out,
    grad_mixed,
):
    tok, width = queries.shape
    rows = coarse_keys.shape[0]
    pix = lax.axis_size("pix")
    head = lax.axis_size("head")
    blocks = tok // BLK
    coarse = pix * rows
    d_model = head * width
    bits = bit_list(pix)
    head_bits = bit_list(head)
    levels = min(2, len(bits))
    heads = width // HDIM
    forward_pairs = [(i, i + 1) for i in range(pix - 1)]
    backward_pairs = [(i + 1, i) for i in range(pix - 1)]
    pool_row = pool_map.reshape(1, tok)

    order = [grad_mixed]
    index = [0]
    for bit in reversed(head_bits):
        order = order + [swap(piece, "head", bit) for piece in order]
        index = index + [i ^ bit for i in index]
    grads = [order[index.index(j)] for j in range(head)]

    lo, hi, panel = call(
        prep_kernel,
        [((2 * RIM, width), BF), ((2 * RIM, width), BF), ((2 * rows, width), BF)],
        count=5,
        flops=4 * rows * tok * width,
        bytes_accessed=4 * tok * width * 2,
    )(keys, values, coarse_keys, coarse_values, pool_row)
    prev = lax.ppermute(hi, "pix", forward_pairs)
    nxt = lax.ppermute(lo, "pix", backward_pairs)
    for bit in bits:
        panel = jnp.concatenate([panel, swap(panel, "pix", bit)], 0)

    (grad_attn,) = call(
        grad_kernel,
        [((tok, width), BF)],
        count=head + 1,
        flops=2 * tok * width * d_model,
        bytes_accessed=(2 * tok * d_model + width * d_model) * 2,
    )(*grads, w_out)

    keys_each = NBR * BLK + coarse
    tall = heads * BLK
    product = 2 * tall * keys_each * width
    attn, weights, mix_keep, mix_send, gw_keep, gw_send = call(
        functools.partial(forward_kernel, rows, levels, head),
        [
            ((tok, width), BF),
            ((blocks, tall, keys_each), BF),
            ((head // 2 * tok, width), BF),
            ((head // 2 * tok, width), BF),
            ((width // 2, d_model), BF),
            ((width // 2, d_model), BF),
        ],
        scratch=[
            pltpu.VMEM((tok + 2 * RIM, width), BF),
            pltpu.VMEM((tok + 2 * RIM, width), BF),
            pltpu.VMEM((width, d_model), BF),
        ],
        smem=(0,),
        count=9 + head,
        flops=2 * blocks * product + 4 * tok * width * d_model,
        bytes_accessed=10_000_000,
    )(neighbors, coarse_mask, queries, keys, values, prev, nxt, panel, w_out, *grads)

    kept, sent = mix_keep, mix_send
    for bit in head_bits:
        total = kept.astype(F32) + swap(sent, "head", bit).astype(F32)
        if kept.shape[0] > tok:
            half = kept.shape[0] // 2
            kept, sent = total[:half], total[half:].astype(BF)
    mixed = total.astype(BF)

    kept, sent = gw_keep, gw_send
    for level, bit in enumerate(bits):
        if level >= levels:
            sent = kept.astype(BF)
        total = kept.astype(F32) + swap(sent, "pix", bit).astype(F32)
        if level + 1 < levels:
            half = total.shape[0] // 2
            kept, sent = total[:half], total[half:].astype(BF)
        else:
            kept = total
    part = kept.astype(BF)
    for bit in reversed(bits[:levels]):
        part = jnp.concatenate([part, swap(part, "pix", bit)], 0)
    (grad_w_out,) = call(
        functools.partial(gw_kernel, levels, (tok * pix) ** (-0.5)),
        [((width, d_model), F32)],
        count=1,
        flops=0,
        bytes_accessed=6 * width * d_model,
    )(part)

    grad_queries, own, to_prev, to_next, coarse_grads = call(
        functools.partial(backward_kernel, rows),
        [
            ((tok, width), BF),
            ((2 * tok, width), F32),
            ((2 * RIM, width), BF),
            ((2 * RIM, width), BF),
            ((2 * coarse, width), F32),
        ],
        scratch=[
            pltpu.VMEM((tok + 2 * RIM, width), BF),
            pltpu.VMEM((tok + 2 * RIM, width), BF),
            pltpu.VMEM((tok + 2 * RIM, width), F32),
            pltpu.VMEM((tok + 2 * RIM, width), F32),
        ],
        smem=(0,),
        count=10,
        flops=4 * blocks * product,
        bytes_accessed=10_000_000,
    )(neighbors, queries, keys, values, prev, nxt, panel, grad_attn, attn, weights)

    above = lax.ppermute(to_prev, "pix", backward_pairs)
    below = lax.ppermute(to_next, "pix", forward_pairs)
    for bit in reversed(bits):
        half = coarse_grads.shape[0] // 2
        coarse_grads = coarse_grads[:half] + swap(coarse_grads[half:], "pix", bit)

    grad_keys, grad_values, grad_ck, grad_cv = call(
        finish_kernel,
        [((tok, width), BF), ((tok, width), BF), ((rows, width), F32), ((rows, width), F32)],
        count=5,
        flops=8 * rows * tok * width,
        bytes_accessed=16 * tok * width,
    )(own, below, above, coarse_grads, pool_row)
    return (mixed, grad_queries, grad_keys, grad_values, grad_ck, grad_cv, grad_w_out)


def solution(mesh):
    in_specs = (
        P("pix", "head"),
        P("pix", "head"),
        P("pix", "head"),
        P("pix", "head"),
        P("pix", "head"),
        P("pix", None),
        P("pix"),
        P("pix", None),
        P("head", None),
        P("pix", "head"),
    )
    out_specs = (
        P("pix", "head"),
        P("pix", "head"),
        P("pix", "head"),
        P("pix", "head"),
        P("pix", "head"),
        P("pix", "head"),
        P("head", None),
    )
    return jax.shard_map(
        on_device, mesh=mesh, in_specs=in_specs, out_specs=out_specs, check_vma=False
    )
```

time: 260 us -> 90.1 us (0.35)
  waiting for transfers between devices: 116 us -> 33.2 us
  blocking collectives: 33.7 us -> 0 us
  local copies, waits for them, and re-layouts: 36.7 us -> 8.33 us
  matrix products: 25.2 us -> 0 us
  other arithmetic: 22.9 us -> 1.1 us
  starting transfers between devices: 10.7 us -> 32.3 us
  Pallas kernels: 0 us -> 13.8 us
  between operations: 14.4 us -> 0.88 us
    psum x1 -> x0, waiting for transfers between devices: 74.7 us -> none  [on_device(): lax.psum(wout_term, 'pix') * (tok_rows * lax.axis_size('pix')) ** (-0.5)]
    reduce_scatter x2 -> x0, waiting for transfers between devices: 41.1 us -> none  [the longest x1 31.3 us: on_device(): lax.psum_scatter(partial_value, 'head', scatter_dimension=1, tiled=True)]
    all_gather x1 -> x0, blocking collectives: 33.7 us -> none  [on_device(): lax.all_gather(jnp.stack([panel_k, panel_v]), 'pix', axis=1, tiled=True)]
    ppermute x4 -> x20, waiting for transfers between devices: 0.01 us -> 33.2 us  [the longest x16 33.2 us: swap(): lax.ppermute(value, axis, [(i, i ^ bit) for i in range(lax.axis_size(axis...]
    dot_general x17 -> x0, matrix products: 25.2 us -> none  [the longest x1 4.52 us: backward_group(): jnp.einsum('nhbm,nbhd->nmhd', fine_wb, grad_out, preferred_element_type=j...]
    ppermute x4 -> x20, starting transfers between devices: 10.3 us -> 32.3 us  [the longest x16 23.3 us: swap(): lax.ppermute(value, axis, [(i, i ^ bit) for i in range(lax.axis_size(axis...]
    reshape x9 -> x0, local copies, waits for them, and re-layouts: 20.7 us -> none  [the longest x2 10.3 us: backward_group(): value_part.reshape(group_blocks * NBR, BLK, width)]
    pallas_call x0 -> x6, Pallas kernels: none -> 13.8 us  [the longest x1 5.56 us: on_device(): call(functools.partial(backward_kernel, rows), [((tok, width), BF), ((2 *...]
  transfers between devices with their start and end apart: 8 -> 20, of which waited for: 3 -> 9; matrix products, arithmetic and copies ran while one was open for 27% -> 1% of each run, Pallas kernels for 0% -> 8%
where the time goes in v1:
time: 90.1 us; the launch traced here: 89.6 us
  waiting for transfers between devices  33.2 us (37%)
  starting transfers between devices  32.3 us (36%)
  Pallas kernels  13.8 us (15%)
  local copies, waits for them, and re-layouts  8.33 us (9%)
  other arithmetic  1.1 us (1%)
    ppermute x16, waiting for transfers between devices, swap(): lax.ppermute(value, axis, [(i, i ^ bit) for i in range(lax.axis_size(axis...  33.2 us
    ppermute x16, starting transfers between devices, swap(): lax.ppermute(value, axis, [(i, i ^ bit) for i in range(lax.axis_size(axis...  23.3 us
    unnamed x29, local copies, waits for them, and re-layouts  8.27 us
    pallas_call x1, Pallas kernels, on_device(): call(functools.partial(backward_kernel, rows), [((tok, width), BF), ((2 *...  5.56 us
    pallas_call x1, Pallas kernels, on_device(): call(functools.partial(forward_kernel, rows, levels, head), [((tok, width...  5.31 us
    ppermute x1, starting transfers between devices, on_device(): prev = lax.ppermute(hi, 'pix', forward_pairs)  3.44 us
    ppermute x1, starting transfers between devices, on_device(): below = lax.ppermute(to_next, 'pix', forward_pairs)  2.98 us
  transfers between devices with their start and end apart: 20, of which 9 were waited for; matrix products, arithmetic and copies ran while one was open for 1% of the time, Pallas kernels for 8%

profile of v1, /device:TPU:0, one launch (start us, length us, event | category | flops | bytes accessed | tf_op | source)
XLA Modules:
  0.0 89.6 jit_solution(15365975527852624525)
XLA Ops:
  0.6 0.5 collective-permute-start.5
  1.2 2.6 %collective-permute-start.6 = (bf16[512,256]{1,0:T(8,128)(2,1)}, bf16[512,256]{1,0:T(8,128)(2,1)S(1)}, u32[]{:S(2)}, u32[]{:S(2)}) collective-permute-start(bf16[512,256]{1,0:T(8,128)(2,1)} %refs_0_.4), channel_id=1, source_target_pairs={{0,2},{1,3},{2,0},{3,1},{4,6},{5,7},{6,4},{7,5},{8,10},{9,11},{10,... | collective-permute-start | bytes 786440 | tf_op jit(solution)/shard_map/ppermute | solution.py:42
  3.7 0.9 %copy-done.3 = bf16[512,256]{1,0:T(8,128)(2,1)S(1)} copy-done((bf16[512,256]{1,0:T(8,128)(2,1)S(1)}, bf16[512,256]{1,0:T(8,128)(2,1)}, u32[]{:S(2)}) %copy-start.3) | copy-done | bytes 262168
  4.7 0.9 %copy-done.4 = bf16[512,256]{1,0:T(8,128)(2,1)S(1)} copy-done((bf16[512,256]{1,0:T(8,128)(2,1)S(1)}, bf16[512,256]{1,0:T(8,128)(2,1)}, u32[]{:S(2)}) %copy-start.4) | copy-done | bytes 262168
  5.6 0.7 copy-done.5
  6.3 0.7 copy-done.7
  7.0 0.7 copy-done.8
  7.7 0.2 shard_map.153
  7.9 3.4 %collective-permute-start = (bf16[512,256]{1,0:T(8,128)(2,1)S(1)}, bf16[512,256]{1,0:T(8,128)(2,1)S(1)}, u32[]{:S(2)}, u32[]{:S(2)}) collective-permute-start(bf16[512,256]{1,0:T(8,128)(2,1)S(1)} %get-tuple-element.25), channel_id=1, source_target_pairs={{0,4},{4,8},{8,12},{12,16},{16,20},{20,24},{24,28},{1,5},{5,9},{9,... | collective-permute-start | bytes 786440 | tf_op jit(solution)/shard_map/ppermute | solution.py:328
  11.3 1.3 %collective-permute-start.1 = (bf16[512,256]{1,0:T(8,128)(2,1)S(1)}, bf16[512,256]{1,0:T(8,128)(2,1)S(1)}, u32[]{:S(2)}, u32[]{:S(2)}) collective-permute-start(bf16[512,256]{1,0:T(8,128)(2,1)S(1)} %get-tuple-element.26), channel_id=1, source_target_pairs={{4,0},{8,4},{12,8},{16,12},{20,16},{24,20},{28,24},{5,1},{9,5},{13... | collective-permute-start | bytes 786440 | tf_op jit(solution)/shard_map/ppermute | solution.py:329
  12.6 2.7 %collective-permute-start.2 = (bf16[16,256]{1,0:T(8,128)(2,1)S(1)}, bf16[16,256]{1,0:T(8,128)(2,1)S(1)}, u32[]{:S(2)}, u32[]{:S(2)}) collective-permute-start(bf16[16,256]{1,0:T(8,128)(2,1)S(1)} %get-tuple-element.27), channel_id=1, source_target_pairs={{0,4},{4,0},{8,12},{12,8},{16,20},{20,16},{24,28},{28,24},{1,5},{5... | collective-permute-start | bytes 24584 | tf_op jit(solution)/shard_map/ppermute | solution.py:42
  15.3 7.6 %collective-permute-done.2 = bf16[16,256]{1,0:T(8,128)(2,1)S(1)} collective-permute-done((bf16[16,256]{1,0:T(8,128)(2,1)S(1)}, bf16[16,256]{1,0:T(8,128)(2,1)S(1)}, u32[]{:S(2)}, u32[]{:S(2)}) %collective-permute-start.2) | collective-permute-done | bytes 8224 | tf_op jit(solution)/shard_map/ppermute | solution.py:42
  23.0 3.4 %collective-permute-start.3 = (bf16[32,256]{1,0:T(8,128)(2,1)S(1)}, bf16[32,256]{1,0:T(8,128)(2,1)S(1)}, u32[]{:S(2)}, u32[]{:S(2)}) collective-permute-start(bf16[32,256]{1,0:T(8,128)(2,1)S(1)} %pad_maximum_fusion.3), channel_id=1, source_target_pairs={{0,8},{4,12},{8,0},{12,4},{16,24},{20,28},{24,16},{28,20},{1,9},{5... | collective-permute-start | bytes 49160 | tf_op jit(solution)/shard_map/ppermute | solution.py:42
  26.4 1.7 %collective-permute-done.3 = bf16[32,256]{1,0:T(8,128)(2,1)S(1)} collective-permute-done((bf16[32,256]{1,0:T(8,128)(2,1)S(1)}, bf16[32,256]{1,0:T(8,128)(2,1)S(1)}, u32[]{:S(2)}, u32[]{:S(2)}) %collective-permute-start.3) | collective-permute-done | bytes 16416 | tf_op jit(solution)/shard_map/ppermute | solution.py:42
  28.1 3.0 %collective-permute-start.4 = (bf16[64,256]{1,0:T(8,128)(2,1)S(1)}, bf16[64,256]{1,0:T(8,128)(2,1)S(1)}, u32[]{:S(2)}, u32[]{:S(2)}) collective-permute-start(bf16[64,256]{1,0:T(8,128)(2,1)S(1)} %pad_maximum_fusion.2), channel_id=1, source_target_pairs={{0,16},{4,20},{8,24},{12,28},{16,0},{20,4},{24,8},{28,12},{1,17},{... | collective-permute-start | bytes 98312 | tf_op jit(solution)/shard_map/ppermute | solution.py:42
  31.2 1.9 %collective-permute-done.4 = bf16[64,256]{1,0:T(8,128)(2,1)S(1)} collective-permute-done((bf16[64,256]{1,0:T(8,128)(2,1)S(1)}, bf16[64,256]{1,0:T(8,128)(2,1)S(1)}, u32[]{:S(2)}, u32[]{:S(2)}) %collective-permute-start.4) | collective-permute-done | bytes 32800 | tf_op jit(solution)/shard_map/ppermute | solution.py:42
  33.1 1.0 %copy-done = bf16[256,1024]{1,0:T(8,128)(2,1)S(1)} copy-done((bf16[256,1024]{1,0:T(8,128)(2,1)S(1)}, bf16[256,1024]{1,0:T(8,128)(2,1)}, u32[]{:S(2)}) %copy-start) | copy-done | bytes 524312
  34.1 0.9 %copy-done.2 = bf16[512,256]{1,0:T(8,128)(2,1)S(1)} copy-done((bf16[512,256]{1,0:T(8,128)(2,1)S(1)}, bf16[512,256]{1,0:T(8,128)(2,1)}, u32[]{:S(2)}) %copy-start.2) | copy-done | bytes 262168
  35.1 0.9 %copy-done.9 = bf16[512,256]{1,0:T(8,128)(2,1)S(1)} copy-done((bf16[512,256]{1,0:T(8,128)(2,1)S(1)}, bf16[512,256]{1,0:T(8,128)(2,1)}, u32[]{:S(2)}) %copy-start.9) | copy-done | bytes 262168
  36.0 0.7 copy-done.11
  36.7 0.7 copy-done.12
  37.4 5.3 %shard_map.154 = (bf16[512,256]{1,0:T(8,128)(2,1)S(1)}, bf16[4,512,576]{2,1,0:T(8,128)(2,1)}, bf16[1024,256]{1,0:T(8,128)(2,1)S(1)}, bf16[1024,256]{1,0:T(8,128)...) custom-call(s32[4,4]{1,0:T(4,128)S(1)} %copy-done.12, s32[4,8]{1,0:T(4,128)S(1)} %copy-done.11, ...), custom_call_target="tpu_custom_call" | custom-call | flops 1744830464 | bytes 10000000 | tf_op jit(solution)/shard_map/pallas_call | solution.py:344
  42.7 1.0 %collective-permute-start.15 = (bf16[128,1024]{1,0:T(8,128)(2,1)S(1)}, bf16[128,1024]{1,0:T(8,128)(2,1)S(1)}, u32[]{:S(2)}, u32[]{:S(2)}) collective-permute-start(bf16[128,1024]{1,0:T(8,128)(2,1)S(1)} %get-tuple-element.42), channel_id=1, source_target_pairs={{0,4},{4,0},{8,12},{12,8},{16,20},{20,16},{24,28},{28,24},{1,5},{5... | collective-permute-start | bytes 786440 | tf_op jit(solution)/shard_map/ppermute | solution.py:42
  43.7 0.5 shard_map.155.refs_7_
  44.2 5.6 %shard_map.156 = (bf16[512,256]{1,0:T(8,128)(2,1)}, f32[1024,256]{1,0:T(8,128)S(1)}, bf16[512,256]{1,0:T(8,128)(2,1)S(1)}, bf16[512,256]{1,0:T(8,128)(2,1)S(1)}, f32[128,256]{1,0:T(8,128)S(1)}) custom-call(s32[4,4]{1,0:T(4,128)S(1)} %copy-done.12, bf16[512,256]{1,0:T(8,128)(2,1)S(1)} %copy-done.10, bf16[512,256]{1,0:T(8,128)(2,1)S(1)} %copy-done.3, ...), custom_call_target="tpu_custom_call" | custom-call | flops 2415919104 | bytes 10000000 | tf_op jit(solution)/shard_map/pallas_call | solution.py:394
  49.7 3.0 %collective-permute-start.10 = (bf16[512,256]{1,0:T(8,128)(2,1)S(1)}, bf16[512,256]{1,0:T(8,128)(2,1)S(1)}, u32[]{:S(2)}, u32[]{:S(2)}) collective-permute-start(bf16[512,256]{1,0:T(8,128)(2,1)S(1)} %get-tuple-element.34), channel_id=1, source_target_pairs={{0,4},{4,8},{8,12},{12,16},{16,20},{20,24},{24,28},{1,5},{5,9},{9,... | collective-permute-start | bytes 786440 | tf_op jit(solution)/shard_map/ppermute | solution.py:416
  52.7 1.3 %collective-permute-start.11 = (bf16[512,256]{1,0:T(8,128)(2,1)S(1)}, bf16[512,256]{1,0:T(8,128)(2,1)S(1)}, u32[]{:S(2)}, u32[]{:S(2)}) collective-permute-start(bf16[512,256]{1,0:T(8,128)(2,1)S(1)} %get-tuple-element.35), channel_id=1, source_target_pairs={{4,0},{8,4},{12,8},{16,12},{20,16},{24,20},{28,24},{5,1},{9,5},{13... | collective-permute-start | bytes 786440 | tf_op jit(solution)/shard_map/ppermute | solution.py:415
  54.0 5.1 %collective-permute-start.12 = (f32[64,256]{1,0:T(8,128)S(1)}, f32[64,256]{1,0:T(8,128)S(1)}, u32[]{:S(2)}, u32[]{:S(2)}) collective-permute-start(f32[64,256]{1,0:T(8,128)S(1)} %slice.35), channel_id=1, source_target_pairs={{0,16},{4,20},{8,24},{12,28},{16,0},{20,4},{24,8},{28,12},{1,17},{... | collective-permute-start | bytes 196616 | tf_op jit(solution)/shard_map/ppermute | solution.py:42
  59.1 0.1 convert_add_fusion.1
  59.2 0.0 copy-start.6
  59.2 1.3 %collective-permute-start.16 = (bf16[64,1024]{1,0:T(8,128)(2,1)S(1)}, bf16[64,1024]{1,0:T(8,128)(2,1)S(1)}, u32[]{:S(2)}, u32[]{:S(2)}) collective-permute-start(bf16[64,1024]{1,0:T(8,128)(2,1)S(1)} %slice.64), channel_id=1, source_target_pairs={{0,8},{4,12},{8,0},{12,4},{16,24},{20,28},{24,16},{28,20},{1,9},{5... | collective-permute-start | bytes 393224 | tf_op jit(solution)/shard_map/ppermute | solution.py:42
  60.5 7.9 %collective-permute-done.12 = f32[64,256]{1,0:T(8,128)S(1)} collective-permute-done((f32[64,256]{1,0:T(8,128)S(1)}, f32[64,256]{1,0:T(8,128)S(1)}, u32[]{:S(2)}, u32[]{:S(2)}) %collective-permute-start.12) | collective-permute-done | bytes 65568 | tf_op jit(solution)/shard_map/ppermute | solution.py:42
  68.4 0.5 collective-permute-start.13
  68.9 2.4 %collective-permute-start.17 = (bf16[64,1024]{1,0:T(8,128)(2,1)S(1)}, bf16[64,1024]{1,0:T(8,128)(2,1)S(1)}, u32[]{:S(2)}, u32[]{:S(2)}) collective-permute-start(bf16[64,1024]{1,0:T(8,128)(2,1)S(1)} %fusion.1), channel_id=1, source_target_pairs={{0,16},{4,20},{8,24},{12,28},{16,0},{20,4},{24,8},{28,12},{1,17},{... | collective-permute-start | bytes 393224 | tf_op jit(solution)/shard_map/ppermute | solution.py:42
  71.4 1.0 %collective-permute-done.13 = f32[32,256]{1,0:T(8,128)S(1)} collective-permute-done((f32[32,256]{1,0:T(8,128)S(1)}, f32[32,256]{1,0:T(8,128)S(1)}, u32[]{:S(2)}, u32[]{:S(2)}) %collective-permute-start.13) | collective-permute-done | bytes 32800 | tf_op jit(solution)/shard_map/ppermute | solution.py:42
  72.4 0.1 collective-permute-start.14
  72.5 4.5 %collective-permute-done.17 = bf16[64,1024]{1,0:T(8,128)(2,1)S(1)} collective-permute-done((bf16[64,1024]{1,0:T(8,128)(2,1)S(1)}, bf16[64,1024]{1,0:T(8,128)(2,1)S(1)}, u32[]{:S(2)}, u32[]{:S(2)}) %collective-permute-start.17) | collective-permute-done | bytes 131104 | tf_op jit(solution)/shard_map/ppermute | solution.py:42
  77.0 0.1 add_convert_fusion
  77.0 0.1 collective-permute-start.18
  77.1 0.1 convert_add_fusion
  77.3 0.6 collective-permute-start.9
  77.8 4.2 %collective-permute-done.18 = bf16[64,1024]{1,0:T(8,128)(2,1)S(1)} collective-permute-done((bf16[64,1024]{1,0:T(8,128)(2,1)S(1)}, bf16[64,1024]{1,0:T(8,128)(2,1)S(1)}, u32[]{:S(2)}, u32[]{:S(2)}) %collective-permute-start.18) | collective-permute-done | bytes 131104 | tf_op jit(solution)/shard_map/ppermute | solution.py:42
  82.1 0.1 collective-permute-start.19
  82.2 1.2 %shard_map.157 = (bf16[512,256]{1,0:T(8,128)(2,1)}, bf16[512,256]{1,0:T(8,128)(2,1)}, f32[8,256]{1,0:T(8,128)}, f32[8,256]{1,0:T(8,128)}) custom-call(f32[1024,256]{1,0:T(8,128)S(1)} %get-tuple-element.33.own_ref, bf16[512,256]{1,0:T(8,128)(2,1)S(1)} %collective-permute-done.10.below_ref, bf16[512,256]{1,0:T(8,128)(2,1)S(1)} %collective-permute-done.11.above_ref, ...), custom_call_target="tpu_custom_call" | custom-call | flops 8388608 | bytes 2097152 | tf_op jit(solution)/shard_map/pallas_call | solution.py:421
  83.4 1.5 %collective-permute-done.9 = bf16[512,256]{1,0:T(8,128)(2,1)S(1)} collective-permute-done((bf16[512,256]{1,0:T(8,128)(2,1)S(1)}, bf16[512,256]{1,0:T(8,128)(2,1)S(1)}, u32[]{:S(2)}, u32[]{:S(2)}) %collective-permute-start.9) | collective-permute-done | bytes 262176 | tf_op jit(solution)/shard_map/ppermute | solution.py:42
  84.8 0.8 fusion
  85.6 2.9 %collective-permute-done.19 = bf16[128,1024]{1,0:T(8,128)(2,1)S(1)} collective-permute-done((bf16[128,1024]{1,0:T(8,128)(2,1)S(1)}, bf16[128,1024]{1,0:T(8,128)(2,1)S(1)}, u32[]{:S(2)}, u32[]{:S(2)}) %collective-permute-start.19) | collective-permute-done | bytes 262176 | tf_op jit(solution)/shard_map/ppermute | solution.py:42
  88.5 1.1 %shard_map.158 = f32[256,1024]{1,0:T(8,128)} custom-call(bf16[256,1024]{1,0:T(8,128)(2,1)S(1)} %pad_maximum_fusion.in_ref), custom_call_target="tpu_custom_call" | custom-call | bytes 1572864 | tf_op jit(solution)/shard_map/pallas_call | solution.py:386
  (45 shorter events, 0.2 us)
Async XLA Ops:
  0.6 32.4 %collective-permute-start.5 = (bf16[512,256]{1,0:T(8,128)(2,1)}, bf16[512,256]{1,0:T(8,128)(2,1)S(1)}, u32[]{:S(2)}, u32[]{:S(2)}) collective-permute-start(bf16[512,256]{1,0:T(8,128)(2,1)} %refs_0_.4), channel_id=1, source_target_pairs={{0,1},{1,0},{2,3},{3,2},{4,5},{5,4},{6,7},{7,6},{8,9},{9,8},{10,11... | collective-permute-start | bytes 786440 | tf_op jit(solution)/shard_map/ppermute | solution.py:42
  1.2 25.3 %collective-permute-start.6 = (bf16[512,256]{1,0:T(8,128)(2,1)}, bf16[512,256]{1,0:T(8,128)(2,1)S(1)}, u32[]{:S(2)}, u32[]{:S(2)}) collective-permute-start(bf16[512,256]{1,0:T(8,128)(2,1)} %refs_0_.4), channel_id=1, source_target_pairs={{0,2},{1,3},{2,0},{3,1},{4,6},{5,7},{6,4},{7,5},{8,10},{9,11},{10,... | collective-permute-start | bytes 786440 | tf_op jit(solution)/shard_map/ppermute | solution.py:42
  3.7 0.9 %copy-start.3 = (bf16[512,256]{1,0:T(8,128)(2,1)S(1)}, bf16[512,256]{1,0:T(8,128)(2,1)}, u32[]{:S(2)}) copy-start(bf16[512,256]{1,0:T(8,128)(2,1)} %refs_2_.3) | copy-start | bytes 786436
  4.7 0.9 %copy-start.4 = (bf16[512,256]{1,0:T(8,128)(2,1)S(1)}, bf16[512,256]{1,0:T(8,128)(2,1)}, u32[]{:S(2)}) copy-start(bf16[512,256]{1,0:T(8,128)(2,1)} %refs_3_.3) | copy-start | bytes 786436
  5.6 0.7 copy-start.5
  6.3 0.7 copy-start.7
  7.0 0.7 copy-start.8
  7.9 25.2 %collective-permute-start = (bf16[512,256]{1,0:T(8,128)(2,1)S(1)}, bf16[512,256]{1,0:T(8,128)(2,1)S(1)}, u32[]{:S(2)}, u32[]{:S(2)}) collective-permute-start(bf16[512,256]{1,0:T(8,128)(2,1)S(1)} %get-tuple-element.25), channel_id=1, source_target_pairs={{0,4},{4,8},{8,12},{12,16},{16,20},{20,24},{24,28},{1,5},{5,9},{9,... | collective-permute-start | bytes 786440 | tf_op jit(solution)/shard_map/ppermute | solution.py:328
  11.3 21.8 %collective-permute-start.1 = (bf16[512,256]{1,0:T(8,128)(2,1)S(1)}, bf16[512,256]{1,0:T(8,128)(2,1)S(1)}, u32[]{:S(2)}, u32[]{:S(2)}) collective-permute-start(bf16[512,256]{1,0:T(8,128)(2,1)S(1)} %get-tuple-element.26), channel_id=1, source_target_pairs={{4,0},{8,4},{12,8},{16,12},{20,16},{24,20},{28,24},{5,1},{9,5},{13... | collective-permute-start | bytes 786440 | tf_op jit(solution)/shard_map/ppermute | solution.py:329
  12.6 10.4 %collective-permute-start.2 = (bf16[16,256]{1,0:T(8,128)(2,1)S(1)}, bf16[16,256]{1,0:T(8,128)(2,1)S(1)}, u32[]{:S(2)}, u32[]{:S(2)}) collective-permute-start(bf16[16,256]{1,0:T(8,128)(2,1)S(1)} %get-tuple-element.27), channel_id=1, source_target_pairs={{0,4},{4,0},{8,12},{12,8},{16,20},{20,16},{24,28},{28,24},{1,5},{5... | collective-permute-start | bytes 24584 | tf_op jit(solution)/shard_map/ppermute | solution.py:42
  23.0 5.2 %collective-permute-start.3 = (bf16[32,256]{1,0:T(8,128)(2,1)S(1)}, bf16[32,256]{1,0:T(8,128)(2,1)S(1)}, u32[]{:S(2)}, u32[]{:S(2)}) collective-permute-start(bf16[32,256]{1,0:T(8,128)(2,1)S(1)} %pad_maximum_fusion.3), channel_id=1, source_target_pairs={{0,8},{4,12},{8,0},{12,4},{16,24},{20,28},{24,16},{28,20},{1,9},{5... | collective-permute-start | bytes 49160 | tf_op jit(solution)/shard_map/ppermute | solution.py:42
  26.4 6.7 %collective-permute-start.7 = (bf16[512,256]{1,0:T(8,128)(2,1)S(1)}, bf16[512,256]{1,0:T(8,128)(2,1)S(1)}, u32[]{:S(2)}, u32[]{:S(2)}) collective-permute-start(bf16[512,256]{1,0:T(8,128)(2,1)S(1)} %collective-permute-done.6.refs_11_.refs_2_), channel_id=1, source_target_pairs={{0,1},{1,0},{2,3},{3,2},{4,5},{5,4},{6,7},{7,6},{8,9},{9,8},{10,11... | collective-permute-start | bytes 786440 | tf_op jit(solution)/shard_map/ppermute | solution.py:42
  28.1 4.9 %collective-permute-start.4 = (bf16[64,256]{1,0:T(8,128)(2,1)S(1)}, bf16[64,256]{1,0:T(8,128)(2,1)S(1)}, u32[]{:S(2)}, u32[]{:S(2)}) collective-permute-start(bf16[64,256]{1,0:T(8,128)(2,1)S(1)} %pad_maximum_fusion.2), channel_id=1, source_target_pairs={{0,16},{4,20},{8,24},{12,28},{16,0},{20,4},{24,8},{28,12},{1,17},{... | collective-permute-start | bytes 98312 | tf_op jit(solution)/shard_map/ppermute | solution.py:42
  33.1 1.0 %copy-start = (bf16[256,1024]{1,0:T(8,128)(2,1)S(1)}, bf16[256,1024]{1,0:T(8,128)(2,1)}, u32[]{:S(2)}) copy-start(bf16[256,1024]{1,0:T(8,128)(2,1)} %refs_4_.3) | copy-start | bytes 1572868
  34.1 0.9 %copy-start.2 = (bf16[512,256]{1,0:T(8,128)(2,1)S(1)}, bf16[512,256]{1,0:T(8,128)(2,1)}, u32[]{:S(2)}) copy-start(bf16[512,256]{1,0:T(8,128)(2,1)} %refs_0_.4) | copy-start | bytes 786436
  35.1 0.9 %copy-start.9 = (bf16[512,256]{1,0:T(8,128)(2,1)S(1)}, bf16[512,256]{1,0:T(8,128)(2,1)}, u32[]{:S(2)}) copy-start(bf16[512,256]{1,0:T(8,128)(2,1)} %refs_1_.3) | copy-start | bytes 786436
  36.0 0.7 copy-start.11
  36.7 0.7 copy-start.12
  37.4 6.3 %copy-start.1 = (bf16[256,1024]{1,0:T(8,128)(2,1)S(1)}, bf16[256,1024]{1,0:T(8,128)(2,1)}, u32[]{:S(2)}) copy-start(bf16[256,1024]{1,0:T(8,128)(2,1)} %refs_4_.3) | copy-start | bytes 1572868
  37.4 6.8 %copy-start.10 = (bf16[512,256]{1,0:T(8,128)(2,1)S(1)}, bf16[512,256]{1,0:T(8,128)(2,1)}, u32[]{:S(2)}) copy-start(bf16[512,256]{1,0:T(8,128)(2,1)} %refs_1_.3) | copy-start | bytes 786436
  42.7 16.4 %collective-permute-start.15 = (bf16[128,1024]{1,0:T(8,128)(2,1)S(1)}, bf16[128,1024]{1,0:T(8,128)(2,1)S(1)}, u32[]{:S(2)}, u32[]{:S(2)}) collective-permute-start(bf16[128,1024]{1,0:T(8,128)(2,1)S(1)} %get-tuple-element.42), channel_id=1, source_target_pairs={{0,4},{4,0},{8,12},{12,8},{16,20},{20,16},{24,28},{28,24},{1,5},{5... | collective-permute-start | bytes 786440 | tf_op jit(solution)/shard_map/ppermute | solution.py:42
  43.7 33.4 %collective-permute-start.8 = (bf16[1024,256]{1,0:T(8,128)(2,1)S(1)}, bf16[1024,256]{1,0:T(8,128)(2,1)S(1)}, u32[]{:S(2)}, u32[]{:S(2)}) collective-permute-start(bf16[1024,256]{1,0:T(8,128)(2,1)S(1)} %get-tuple-element.29), channel_id=1, source_target_pairs={{0,1},{1,0},{2,3},{3,2},{4,5},{5,4},{6,7},{7,6},{8,9},{9,8},{10,11... | collective-permute-start | bytes 1572872 | tf_op jit(solution)/shard_map/ppermute | solution.py:42
  49.7 32.4 %collective-permute-start.10 = (bf16[512,256]{1,0:T(8,128)(2,1)S(1)}, bf16[512,256]{1,0:T(8,128)(2,1)S(1)}, u32[]{:S(2)}, u32[]{:S(2)}) collective-permute-start(bf16[512,256]{1,0:T(8,128)(2,1)S(1)} %get-tuple-element.34), channel_id=1, source_target_pairs={{0,4},{4,8},{8,12},{12,16},{16,20},{20,24},{24,28},{1,5},{5,9},{9,... | collective-permute-start | bytes 786440 | tf_op jit(solution)/shard_map/ppermute | solution.py:416
  52.7 29.5 %collective-permute-start.11 = (bf16[512,256]{1,0:T(8,128)(2,1)S(1)}, bf16[512,256]{1,0:T(8,128)(2,1)S(1)}, u32[]{:S(2)}, u32[]{:S(2)}) collective-permute-start(bf16[512,256]{1,0:T(8,128)(2,1)S(1)} %get-tuple-element.35), channel_id=1, source_target_pairs={{4,0},{8,4},{12,8},{16,12},{20,16},{24,20},{28,24},{5,1},{9,5},{13... | collective-permute-start | bytes 786440 | tf_op jit(solution)/shard_map/ppermute | solution.py:415
  54.0 14.4 %collective-permute-start.12 = (f32[64,256]{1,0:T(8,128)S(1)}, f32[64,256]{1,0:T(8,128)S(1)}, u32[]{:S(2)}, u32[]{:S(2)}) collective-permute-start(f32[64,256]{1,0:T(8,128)S(1)} %slice.35), channel_id=1, source_target_pairs={{0,16},{4,20},{8,24},{12,28},{16,0},{20,4},{24,8},{28,12},{1,17},{... | collective-permute-start | bytes 196616 | tf_op jit(solution)/shard_map/ppermute | solution.py:42
  59.2 23.0 %copy-start.6 = (s32[512]{0:T(512)S(1)}, s32[512]{0:T(512)}, u32[]{:S(2)}) copy-start(s32[512]{0:T(512)} %param.16) | copy-start | bytes 6148
  59.2 9.7 %collective-permute-start.16 = (bf16[64,1024]{1,0:T(8,128)(2,1)S(1)}, bf16[64,1024]{1,0:T(8,128)(2,1)S(1)}, u32[]{:S(2)}, u32[]{:S(2)}) collective-permute-start(bf16[64,1024]{1,0:T(8,128)(2,1)S(1)} %slice.64), channel_id=1, source_target_pairs={{0,8},{4,12},{8,0},{12,4},{16,24},{20,28},{24,16},{28,20},{1,9},{5... | collective-permute-start | bytes 393224 | tf_op jit(solution)/shard_map/ppermute | solution.py:42
  68.4 4.0 %collective-permute-start.13 = (f32[32,256]{1,0:T(8,128)S(1)}, f32[32,256]{1,0:T(8,128)S(1)}, u32[]{:S(2)}, u32[]{:S(2)}) collective-permute-start(f32[32,256]{1,0:T(8,128)S(1)} %slice.45), channel_id=1, source_target_pairs={{0,8},{4,12},{8,0},{12,4},{16,24},{20,28},{24,16},{28,20},{1,9},{5... | collective-permute-start | bytes 98312 | tf_op jit(solution)/shard_map/ppermute | solution.py:42
  68.9 8.0 %collective-permute-start.17 = (bf16[64,1024]{1,0:T(8,128)(2,1)S(1)}, bf16[64,1024]{1,0:T(8,128)(2,1)S(1)}, u32[]{:S(2)}, u32[]{:S(2)}) collective-permute-start(bf16[64,1024]{1,0:T(8,128)(2,1)S(1)} %fusion.1), channel_id=1, source_target_pairs={{0,16},{4,20},{8,24},{12,28},{16,0},{20,4},{24,8},{28,12},{1,17},{... | collective-permute-start | bytes 393224 | tf_op jit(solution)/shard_map/ppermute | solution.py:42
  72.4 9.7 %collective-permute-start.14 = (f32[16,256]{1,0:T(8,128)S(1)}, f32[16,256]{1,0:T(8,128)S(1)}, u32[]{:S(2)}, u32[]{:S(2)}) collective-permute-start(f32[16,256]{1,0:T(8,128)S(1)} %slice.47), channel_id=1, source_target_pairs={{0,4},{4,0},{8,12},{12,8},{16,20},{20,16},{24,28},{28,24},{1,5},{5... | collective-permute-start | bytes 49160 | tf_op jit(solution)/shard_map/ppermute | solution.py:42
  77.0 5.0 %collective-permute-start.18 = (bf16[64,1024]{1,0:T(8,128)(2,1)S(1)}, bf16[64,1024]{1,0:T(8,128)(2,1)S(1)}, u32[]{:S(2)}, u32[]{:S(2)}) collective-permute-start(bf16[64,1024]{1,0:T(8,128)(2,1)S(1)} %add_convert_fusion), channel_id=1, source_target_pairs={{0,8},{4,12},{8,0},{12,4},{16,24},{20,28},{24,16},{28,20},{1,9},{5... | collective-permute-start | bytes 393224 | tf_op jit(solution)/shard_map/ppermute | solution.py:42
  77.3 7.6 %collective-permute-start.9 = (bf16[512,256]{1,0:T(8,128)(2,1)S(1)}, bf16[512,256]{1,0:T(8,128)(2,1)S(1)}, u32[]{:S(2)}, u32[]{:S(2)}) collective-permute-start(bf16[512,256]{1,0:T(8,128)(2,1)S(1)} %slice.63), channel_id=1, source_target_pairs={{0,2},{1,3},{2,0},{3,1},{4,6},{5,7},{6,4},{7,5},{8,10},{9,11},{10,... | collective-permute-start | bytes 786440 | tf_op jit(solution)/shard_map/ppermute | solution.py:42
  82.1 6.4 %collective-permute-start.19 = (bf16[128,1024]{1,0:T(8,128)(2,1)S(1)}, bf16[128,1024]{1,0:T(8,128)(2,1)S(1)}, u32[]{:S(2)}, u32[]{:S(2)}) collective-permute-start(bf16[128,1024]{1,0:T(8,128)(2,1)S(1)} %pad_maximum_fusion.1), channel_id=1, source_target_pairs={{0,4},{4,0},{8,12},{12,8},{16,20},{20,16},{24,28},{28,24},{1,5},{5... | collective-permute-start | bytes 786440 | tf_op jit(solution)/shard_map/ppermute | solution.py:42

commit v2 on v1

v2 whole, which is shorter than its diff:
```python
import functools
import math

import jax
import jax.numpy as jnp
from jax import lax
from jax.experimental import pallas as pl
from jax.experimental.pallas import tpu as pltpu
from jax.sharding import PartitionSpec as P

HDIM = 64
BLK = 128
NBR = 4
HB = 2
CBLK = 8
RIM = HB * BLK
SCALE = HDIM ** (-0.5)
LOG2E = math.log2(math.e)
BF = jnp.bfloat16
F32 = jnp.float32
VMEM = pl.BlockSpec(memory_space=pltpu.VMEM)
HBM = pl.BlockSpec(memory_space=pltpu.HBM)


def mm(a, b):
    return jnp.dot(a, b, preferred_element_type=F32)


def mm_t(a, b):
    return lax.dot_general(a, b, (((1,), (1,)), ((), ())), preferred_element_type=F32)


def t_mm(a, b):
    return lax.dot_general(a, b, (((0,), (0,)), ((), ())), preferred_element_type=F32)


def bit_list(count):
    return [1 << i for i in range(count.bit_length() - 1)]


def swap(value, axis, bit):
    return lax.ppermute(value, axis, [(i, i ^ bit) for i in range(lax.axis_size(axis))])


def exchange(value, pairs):
    return lax.ppermute(value, "pix", pairs + [(b, a) for a, b in pairs])


def near_pairs(count):
    return [(i, i + 1) for i in range(0, count, 2)]


def far_pairs(count):
    return [(i, i + 1) for i in range(1, count - 1, 2)]


def gather_parts(value, bits):
    offsets = [0]
    for bit in bits:
        offsets = offsets + [o + bit for o in offsets]
    return [value if o == 0 else swap(value, "pix", o) for o in offsets]


def gather_bits(value, bits):
    return jnp.concatenate(gather_parts(value, bits), 0)


def cut(lines, height, width, count):
    across = lines.shape[1] // width
    cells = []
    for t in range(count):
        top, left = t // across * height, t % across * width
        cells.append(lines[top : top + height, left : left + width])
    return cells


def reversed_bits(index, levels):
    out = 0
    for level in range(levels):
        out = out * 2 + ((index >> level) & 1)
    return out


def call(body, outs, specs, out_specs=None, scratch=(), flops=0, bytes_accessed=0):
    return pl.pallas_call(
        body,
        out_shape=[jax.ShapeDtypeStruct(s, t) for s, t in outs],
        in_specs=list(specs),
        out_specs=[VMEM] * len(outs) if out_specs is None else list(out_specs),
        scratch_shapes=list(scratch),
        compiler_params=pltpu.CompilerParams(vmem_limit_bytes=48 * 1024 * 1024),
        cost_estimate=pl.CostEstimate(
            flops=flops, bytes_accessed=bytes_accessed, transcendentals=0
        ),
    )


def membership(pool_ref, rows):
    me = lax.axis_index("pix")
    local = pool_ref[...] - me * rows
    count = pool_ref.shape[1]
    return local == lax.broadcasted_iota(jnp.int32, (rows, count), 0)


def prep_kernel(
    k_hbm, v_hbm, ck_hbm, cv_hbm, pool_hbm, mask_hbm,
    k_ref, v_ref, near_ref, far_ref, panel_ref, pool_ref, mask_ref,
    ck_ref, cv_ref, sems,
):
    tok = k_ref.shape[0]
    odd = lax.axis_index("pix") & 1
    near = pl.ds(pl.multiple_of((1 - odd) * (tok - RIM), RIM), RIM)
    far = pl.ds(pl.multiple_of(odd * (tok - RIM), RIM), RIM)
    pairs = [
        (pool_hbm, pool_ref),
        (k_hbm, k_ref),
        (v_hbm, v_ref),
        (ck_hbm, ck_ref),
        (cv_hbm, cv_ref),
        (k_hbm.at[near], near_ref.at[pl.ds(0, RIM)]),
        (v_hbm.at[near], near_ref.at[pl.ds(RIM, RIM)]),
        (k_hbm.at[far], far_ref.at[pl.ds(0, RIM)]),
        (v_hbm.at[far], far_ref.at[pl.ds(RIM, RIM)]),
        (mask_hbm, mask_ref),
    ]
    copies = [pltpu.make_async_copy(x, y, sems.at[i]) for i, (x, y) in enumerate(pairs)]
    for copy in copies:
        copy.start()
    for copy in copies[:5]:
        copy.wait()
    member = membership(pool_ref, ck_ref.shape[0]).astype(F32)
    counts = jnp.sum(member, axis=1, keepdims=True)
    member = member.astype(BF)
    panel_k = mm(member, k_ref[...]) / counts + ck_ref[...].astype(F32)
    panel_v = mm(member, v_ref[...]) / counts + cv_ref[...].astype(F32)
    panel_ref[...] = jnp.concatenate([panel_k, panel_v], 0).astype(BF)
    for copy in copies[5:]:
        copy.wait()


def grad_kernel(gm_hbm, q_hbm, w_hbm, *refs):
    pieces = refs[:-5]
    go_ref, gm_ref, q_ref, w_ref, sems = refs[-5:]
    copies = [
        pltpu.make_async_copy(x, y, sems.at[i])
        for i, (x, y) in enumerate([(w_hbm, w_ref), (gm_hbm, gm_ref), (q_hbm, q_ref)])
    ]
    for copy in copies:
        copy.start()
    me = lax.axis_index("head")
    width = w_ref.shape[0]
    copies[0].wait()
    copies[1].wait()
    total = None
    for j, ref in enumerate((gm_ref,) + pieces):
        w = w_ref[:, pl.ds(pl.multiple_of((me ^ j) * width, width), width)]
        part = mm_t(ref[...], w)
        total = part if total is None else total + part
    go_ref[...] = total.astype(BF)
    copies[2].wait()


def head_masks(width, rows):
    lane = lax.broadcasted_iota(jnp.int32, (rows, width), 1)
    return [(lane >= h * HDIM) & (lane < (h + 1) * HDIM) for h in range(width // HDIM)]


def stacked(block, masks):
    zero = jnp.zeros_like(block)
    return jnp.concatenate([jnp.where(m, block, zero) for m in masks], 0)


def unstacked(tall, masks):
    rows = tall.shape[0] // len(masks)
    out = tall[0:rows]
    for h in range(1, len(masks)):
        out = jnp.where(masks[h], tall[h * rows : (h + 1) * rows], out)
    return out


def extend(ext_k, ext_v, k_ref, v_ref, near_ref, far_ref):
    tok = k_ref.shape[0]
    odd = lax.axis_index("pix") & 1
    ext_k[RIM : RIM + tok] = k_ref[...]
    ext_v[RIM : RIM + tok] = v_ref[...]
    near = pl.ds(pl.multiple_of((1 - odd) * (tok + RIM), RIM), RIM)
    far = pl.ds(pl.multiple_of(odd * (tok + RIM), RIM), RIM)
    ext_k[near, :] = near_ref[0:RIM]
    ext_v[near, :] = near_ref[RIM:]
    ext_k[far, :] = far_ref[0:RIM]
    ext_v[far, :] = far_ref[RIM:]


def panel_parts(panel_ref, rows):
    width = panel_ref.shape[1]
    slots = panel_ref.shape[0] // (2 * rows)
    both = panel_ref[...].astype(F32).reshape(slots, 2 * rows, width)
    keys = both[:, :rows].reshape(slots * rows, width).astype(BF)
    values = both[:, rows:].reshape(slots * rows, width).astype(BF)
    return keys, values


def picks(nbr_ref, block, blocks):
    me = lax.axis_index("pix")
    starts = []
    for n in range(NBR):
        index = nbr_ref[block, n] - me * blocks + HB
        starts.append(pl.multiple_of(index * BLK, BLK))
    return starts


def gathered(ext, starts, panel):
    return jnp.concatenate([ext[pl.ds(s, BLK), :] for s in starts] + [panel], 0)


def forward_kernel(rows, levels, *refs):
    (nbr_hbm, mask_ref, q_ref, k_ref, v_ref, near_ref, far_ref, panel_ref, w_ref, go_ref) = refs[
        :10
    ]
    outs = len(refs) - 13
    pieces = refs[10:outs]
    (attn_ref, p_hbm, mix_keep, mix_send, gw_keep, gw_send) = refs[outs : outs + 6]
    (nbr_ref, ext_k, ext_v, gw_all, p_ref, nbr_sem, p_sems) = refs[outs + 6 :]
    tok, width = q_ref.shape
    blocks = tok // BLK
    fetch = pltpu.make_async_copy(nbr_hbm, nbr_ref, nbr_sem)
    fetch.start()
    me = lax.axis_index("pix")
    me_head = lax.axis_index("head")
    extend(ext_k, ext_v, k_ref, v_ref, near_ref, far_ref)
    panel_k, panel_v = panel_parts(panel_ref, rows)
    coarse = panel_k.shape[0]
    cols = mask_ref.shape[1]
    row = lax.broadcasted_iota(jnp.int32, (cols, coarse), 1)
    owner_row = ((row // rows) ^ me) * rows + row % rows
    pick = (owner_row // CBLK) == lax.broadcasted_iota(jnp.int32, (cols, coarse), 0)
    allowed = mm((mask_ref[...] > 0).astype(BF), pick.astype(BF))
    masks = head_masks(width, BLK)
    heads = len(masks)
    coarse_k = jnp.zeros((coarse, width), F32)
    coarse_v = jnp.zeros((coarse, width), F32)
    fetch.wait()
    stores = []
    for b in range(blocks):
        span = slice(b * BLK, (b + 1) * BLK)
        starts = picks(nbr_ref, b, blocks)
        q_tall = stacked(q_ref[span], masks)
        scores = mm_t(q_tall, gathered(ext_k, starts, panel_k)) * (SCALE * LOG2E)
        fine = scores[:, : NBR * BLK]
        lo = jnp.where(allowed[b : b + 1] > 0.5, scores[:, NBR * BLK :], -jnp.inf)
        top = jnp.maximum(
            jnp.max(fine, axis=1, keepdims=True), jnp.max(lo, axis=1, keepdims=True)
        )
        fine = jnp.exp2(fine - top)
        lo = jnp.exp2(lo - top)
        total = jnp.sum(fine, axis=1, keepdims=True) + jnp.sum(lo, axis=1, keepdims=True)
        scale = 1.0 / total
        coarse_w = (lo * scale).astype(BF)
        weights = jnp.concatenate([(fine * scale).astype(BF), coarse_w], 1)
        p_ref[b] = weights
        store = pltpu.make_async_copy(p_ref.at[b], p_hbm.at[b], p_sems.at[b])
        store.start()
        stores.append(store)
        attn = unstacked(mm(weights, gathered(ext_v, starts, panel_v)), masks).astype(BF)
        attn_ref[span] = attn
        g_tall = stacked(go_ref[span], masks)
        dterm = row_terms(g_tall, attn, heads)
        coarse_ds = coarse_w.astype(F32) * (mm_t(g_tall, panel_v) - dterm)
        coarse_k = coarse_k + t_mm(coarse_ds.astype(BF), q_tall)
        coarse_v = coarse_v + t_mm(coarse_w, g_tall)
    coarse_k = coarse_k * SCALE
    attn = attn_ref[...]
    for j, piece in enumerate(pieces):
        lanes = pl.ds(pl.multiple_of((me_head ^ j) * width, width), width)
        part = mm(attn, w_ref[:, lanes]).astype(BF)
        target = mix_send if j & 1 else mix_keep
        target[(j >> 1) * tok : ((j >> 1) + 1) * tok] = part
    chunk = width >> levels
    mine = reversed_bits(me, levels)
    for j, piece in enumerate(pieces):
        part = t_mm(attn, piece[...]).astype(BF)
        lanes = pl.ds(pl.multiple_of((me_head ^ j) * width, width), width)
        for c in range(1 << levels):
            place = pl.ds(pl.multiple_of((c ^ mine) * chunk, chunk), chunk)
            gw_all[place, lanes] = part[c * chunk : (c + 1) * chunk]
    segment = gw_keep.shape[0] * 2 >> levels
    across = gw_all.shape[1] // width
    if (coarse // rows) >> levels < across:
        for target in (gw_keep, gw_send):
            target[...] = jnp.zeros_like(target)
    for s in range(1 << levels):
        target = gw_keep if s < (1 << levels) // 2 else gw_send
        base = (s % ((1 << levels) // 2)) * segment
        target[base : base + chunk] = gw_all[s * chunk : (s + 1) * chunk]
    for j in range(coarse // rows):
        s = reversed_bits(j, levels)
        t = j >> levels
        target = gw_keep if s < (1 << levels) // 2 else gw_send
        base = (s % ((1 << levels) // 2)) * segment + chunk + (t // across) * 2 * rows
        lanes = slice((t % across) * width, (t % across + 1) * width)
        both = [coarse_k[j * rows : (j + 1) * rows], coarse_v[j * rows : (j + 1) * rows]]
        target[base : base + 2 * rows, lanes] = jnp.concatenate(both, 0).astype(BF)
    for store in stores:
        store.wait()


def row_terms(g_tall, attn, heads):
    tall = jnp.concatenate([attn.astype(F32)] * heads, 0)
    return jnp.sum(g_tall.astype(F32) * tall, axis=1, keepdims=True)


def backward_kernel(rows, *refs):
    (nbr_hbm, q_ref, k_ref, v_ref, near_ref, far_ref, panel_ref, go_ref, attn_ref, p_hbm) = refs[
        :10
    ]
    (dq_ref, own_ref, to_near, to_far) = refs[10:14]
    (nbr_ref, ext_k, ext_v, sum_k, sum_v, p_ref, nbr_sem, p_sems) = refs[14:]
    tok, width = q_ref.shape
    blocks = tok // BLK
    fetch = pltpu.make_async_copy(nbr_hbm, nbr_ref, nbr_sem)
    fetch.start()
    loads = [
        pltpu.make_async_copy(p_hbm.at[b], p_ref.at[b], p_sems.at[b]) for b in range(blocks)
    ]
    for load in loads:
        load.start()
    odd = lax.axis_index("pix") & 1
    extend(ext_k, ext_v, k_ref, v_ref, near_ref, far_ref)
    panel_k, panel_v = panel_parts(panel_ref, rows)
    masks = head_masks(width, BLK)
    sum_k[...] = jnp.zeros_like(sum_k)
    sum_v[...] = jnp.zeros_like(sum_v)
    heads = len(masks)
    fetch.wait()
    for b in range(blocks):
        span = slice(b * BLK, (b + 1) * BLK)
        starts = picks(nbr_ref, b, blocks)
        q_tall = stacked(q_ref[span], masks)
        g_tall = stacked(go_ref[span], masks)
        dterm = row_terms(g_tall, attn_ref[span], heads)
        slope = mm_t(g_tall, gathered(ext_v, starts, panel_v))
        loads[b].wait()
        weights = p_ref[b]
        ds = (weights.astype(F32) * (slope - dterm)).astype(BF)
        dq = unstacked(mm(ds, gathered(ext_k, starts, panel_k)), masks)
        dq_ref[span] = (SCALE * dq).astype(BF)
        dk = SCALE * t_mm(ds[:, : NBR * BLK], q_tall)
        dv = t_mm(weights[:, : NBR * BLK], g_tall)
        for n in range(NBR):
            place = pl.ds(starts[n], BLK)
            sum_k[place, :] += dk[n * BLK : (n + 1) * BLK]
            sum_v[place, :] += dv[n * BLK : (n + 1) * BLK]
    own_ref[0:tok] = sum_k[RIM : RIM + tok]
    own_ref[tok:] = sum_v[RIM : RIM + tok]
    near = pl.ds(pl.multiple_of((1 - odd) * (tok + RIM), RIM), RIM)
    far = pl.ds(pl.multiple_of(odd * (tok + RIM), RIM), RIM)
    to_near[0:RIM] = sum_k[near, :].astype(BF)
    to_near[RIM:] = sum_v[near, :].astype(BF)
    to_far[0:RIM] = sum_k[far, :].astype(BF)
    to_far[RIM:] = sum_v[far, :].astype(BF)


def finish_kernel(
    own_ref, near_ref, far_ref, coarse_ref, pool_ref, gk_ref, gv_ref, ck_ref, cv_ref, acc_ref
):
    tok, width = gk_ref.shape
    rows = ck_ref.shape[0]
    odd = lax.axis_index("pix") & 1
    member = membership(pool_ref, rows).astype(F32)
    counts = jnp.sum(member, axis=1, keepdims=True)
    member = member.astype(BF)
    ck_ref[...] = coarse_ref[0:rows]
    cv_ref[...] = coarse_ref[rows:]
    member = jnp.concatenate([member, member], 0)
    near = pl.ds(pl.multiple_of((1 - odd) * (tok - RIM), RIM), RIM)
    far = pl.ds(pl.multiple_of(odd * (tok - RIM), RIM), RIM)
    for which, out in ((0, gk_ref), (1, gv_ref)):
        per_row = coarse_ref[which * rows : (which + 1) * rows] / counts
        high = per_row.astype(BF)
        low = (per_row - high.astype(F32)).astype(BF)
        pooled = t_mm(member, jnp.concatenate([high, low], 0))
        acc_ref[...] = own_ref[which * tok : (which + 1) * tok] + pooled
        half = slice(which * RIM, (which + 1) * RIM)
        acc_ref[near, :] += near_ref[half].astype(F32)
        acc_ref[far, :] += far_ref[half].astype(F32)
        out[...] = acc_ref[...].astype(BF)


def gw_kernel(levels, factor, *refs):
    out_ref = refs[-1]
    me = lax.axis_index("pix")
    chunk = out_ref.shape[0] >> levels
    mine = reversed_bits(me, levels)
    for slot, ref in enumerate(refs[:-1]):
        place = pl.ds(pl.multiple_of((slot ^ mine) * chunk, chunk), chunk)
        out_ref[place, :] = ref[...].astype(F32) * factor


def on_device(
    queries,
    keys,
    values,
    coarse_keys,
    coarse_values,
    neighbors,
    pool_map,
    coarse_mask,
    w_out,
    grad_mixed,
):
    tok, width = queries.shape
    rows = coarse_keys.shape[0]
    pix = lax.axis_size("pix")
    head = lax.axis_size("head")
    blocks = tok // BLK
    coarse = pix * rows
    d_model = head * width
    bits = bit_list(pix)
    head_bits = bit_list(head)
    levels = min(2, len(bits))
    heads = width // HDIM
    pool_row = pool_map.reshape(1, tok)
    keys_hbm, values_hbm, ck_hbm, cv_hbm, pool_hbm, mask_hbm, nbr_hbm, gm_hbm, q_hbm, w_hbm = [
        pltpu.with_memory_space_constraint(x, pltpu.HBM)
        for x in (
            keys,
            values,
            coarse_keys,
            coarse_values,
            pool_row,
            coarse_mask,
            neighbors,
            grad_mixed,
            queries,
            w_out,
        )
    ]
    across = head
    slots = 1 << levels
    held = (pix // slots + across - 1) // across * 2 * rows
    chunk = width // slots
    segment = chunk + held

    k_own, v_own, send_near, send_far, panel, pool_own, mask_own = call(
        prep_kernel,
        [
            ((tok, width), BF),
            ((tok, width), BF),
            ((2 * RIM, width), BF),
            ((2 * RIM, width), BF),
            ((2 * rows, width), BF),
            ((1, tok), jnp.int32),
            (coarse_mask.shape, jnp.int32),
        ],
        [HBM] * 6,
        scratch=[
            pltpu.VMEM((rows, width), BF),
            pltpu.VMEM((rows, width), BF),
            pltpu.SemaphoreType.DMA((10,)),
        ],
        flops=4 * rows * tok * width,
        bytes_accessed=4 * tok * width * 2,
    )(keys_hbm, values_hbm, ck_hbm, cv_hbm, pool_hbm, mask_hbm)

    grad_early, panel = lax.optimization_barrier((grad_mixed, panel))
    near = exchange(send_near, near_pairs(pix))
    panel = gather_bits(panel, bits[:1])
    first = None
    for at in range(1, len(bits), 2):
        parts = gather_parts(panel, bits[at : at + 2])
        if first is None and len(parts) > 1:
            parts[1], send_far = lax.optimization_barrier((parts[1], send_far))
            first = parts[1]
        panel = jnp.concatenate(parts, 0)
    far = exchange(send_far, far_pairs(pix))

    order = [grad_early]
    index = [0]
    for bit in reversed(head_bits):
        if len(order) > 1:
            order = list(lax.optimization_barrier(tuple(order)))
        order = order + [swap(piece, "head", bit) for piece in order]
        index = index + [i ^ bit for i in index]
    grads = [order[index.index(j)] for j in range(1, head)]
    grad_attn, gm_own, q_own, w_own = call(
        grad_kernel,
        [((tok, width), BF), ((tok, width), BF), ((tok, width), BF), ((width, d_model), BF)],
        [HBM] * 3 + [VMEM] * (head - 1),
        scratch=[pltpu.SemaphoreType.DMA((3,))],
        flops=2 * tok * width * d_model,
        bytes_accessed=(2 * tok * d_model + width * d_model) * 2,
    )(gm_hbm, q_hbm, w_hbm, *grads)

    keys_each = NBR * BLK + coarse
    tall = heads * BLK
    product = 2 * tall * keys_each * width
    attn, weights, mix_keep, mix_send, gw_keep, gw_send = call(
        functools.partial(forward_kernel, rows, levels),
        [
            ((tok, width), BF),
            ((blocks, tall, keys_each), BF),
            ((head // 2 * tok, width), BF),
            ((head // 2 * tok, width), BF),
            ((slots // 2 * segment, d_model), BF),
            ((slots // 2 * segment, d_model), BF),
        ],
        [HBM] + [VMEM] * (9 + head),
        out_specs=[VMEM, HBM] + [VMEM] * 4,
        scratch=[
            pltpu.SMEM(neighbors.shape, jnp.int32),
            pltpu.VMEM((tok + 2 * RIM, width), BF),
            pltpu.VMEM((tok + 2 * RIM, width), BF),
            pltpu.VMEM((width, d_model), BF),
            pltpu.VMEM((blocks, tall, keys_each), BF),
            pltpu.SemaphoreType.DMA,
            pltpu.SemaphoreType.DMA((blocks,)),
        ],
        flops=2 * blocks * product + 4 * tok * width * d_model,
        bytes_accessed=10_000_000,
    )(
        nbr_hbm, mask_own, q_own, k_own, v_own, near, far, panel, w_own, grad_attn, gm_own, *grads
    )

    grad_queries, own, to_near, to_far = call(
        functools.partial(backward_kernel, rows),
        [
            ((tok, width), BF),
            ((2 * tok, width), F32),
            ((2 * RIM, width), BF),
            ((2 * RIM, width), BF),
        ],
        [HBM] + [VMEM] * 8 + [HBM],
        scratch=[
            pltpu.SMEM(neighbors.shape, jnp.int32),
            pltpu.VMEM((tok + 2 * RIM, width), BF),
            pltpu.VMEM((tok + 2 * RIM, width), BF),
            pltpu.VMEM((tok + 2 * RIM, width), F32),
            pltpu.VMEM((tok + 2 * RIM, width), F32),
            pltpu.VMEM((blocks, tall, keys_each), BF),
            pltpu.SemaphoreType.DMA,
            pltpu.SemaphoreType.DMA((blocks,)),
        ],
        flops=4 * blocks * product,
        bytes_accessed=10_000_000,
    )(nbr_hbm, q_own, k_own, v_own, near, far, panel, grad_attn, attn, pltpu.with_memory_space_constraint(weights, pltpu.HBM))

    kept, sent = gw_keep, gw_send
    for level in range(levels):
        got = swap(sent, "pix", bits[level])
        if level == 0:
            got, to_near, to_far = lax.optimization_barrier((got, to_near, to_far))
        total = kept.astype(F32) + got.astype(F32)
        half = total.shape[0] // 2
        if level + 1 < levels:
            kept, sent = total[:half], total[half:].astype(BF)
            sent, to_near, to_far = lax.optimization_barrier((sent, to_near, to_far))
    whole = total
    cells = cut(whole[chunk:], 2 * rows, width, pix // slots)
    part = whole[:chunk]
    for bit in bits[levels:]:
        got = swap(whole.astype(BF), "pix", bit).astype(F32)
        part = part + got[:chunk]
        other = cut(got[chunk:], 2 * rows, width, len(cells))
        cells = [cells[t] + other[t ^ 1] for t in range(0, len(cells), 2)]
        if len(cells) > 1:
            empty = [jnp.zeros_like(cells[0])] * (-len(cells) % across)
            full = cells + empty
            lines = [
                jnp.concatenate(full[t : t + across], 1) for t in range(0, len(full), across)
            ]
            whole = jnp.concatenate([part] + lines, 0)
    coarse_grads = cells[0]
    part = part.astype(BF)
    gathered_parts = [part]
    for bit in reversed(bits[:levels]):
        gathered_parts = gathered_parts + [swap(p, "pix", bit) for p in gathered_parts]
    (grad_w_out,) = call(
        functools.partial(gw_kernel, levels, (tok * pix) ** (-0.5)),
        [((width, d_model), F32)],
        [VMEM] * slots,
        flops=0,
        bytes_accessed=6 * width * d_model,
    )(*gathered_parts)

    kept, sent = mix_keep, mix_send
    for bit in head_bits:
        total = kept.astype(F32) + swap(sent, "head", bit).astype(F32)
        if kept.shape[0] > tok:
            half = kept.shape[0] // 2
            kept, sent = total[:half], total[half:].astype(BF)
    mixed = total.astype(BF)

    got_near = exchange(to_near, near_pairs(pix))
    got_far = exchange(to_far, far_pairs(pix))
    grad_keys, grad_values, grad_ck, grad_cv = call(
        finish_kernel,
        [((tok, width), BF), ((tok, width), BF), ((rows, width), F32), ((rows, width), F32)],
        [VMEM] * 5,
        scratch=[pltpu.VMEM((tok, width), F32)],
        flops=8 * rows * tok * width,
        bytes_accessed=16 * tok * width,
    )(own, got_near, got_far, coarse_grads, pool_own)
    return (mixed, grad_queries, grad_keys, grad_values, grad_ck, grad_cv, grad_w_out)


def solution(mesh):
    in_specs = (
        P("pix", "head"),
        P("pix", "head"),
        P("pix", "head"),
        P("pix", "head"),
        P("pix", "head"),
        P("pix", None),
        P("pix"),
        P("pix", None),
        P("head", None),
        P("pix", "head"),
    )
    out_specs = (
        P("pix", "head"),
        P("pix", "head"),
        P("pix", "head"),
        P("pix", "head"),
        P("pix", "head"),
        P("pix", "head"),
        P("head", None),
    )
    return jax.shard_map(
        on_device, mesh=mesh, in_specs=in_specs, out_specs=out_specs, check_vma=False
    )
```

time: 90.1 us -> 69.6 us (0.77)
  starting transfers between devices: 32.3 us -> 20.1 us
  local copies, waits for them, and re-layouts: 8.33 us -> 0.06 us
  Pallas kernels: 13.8 us -> 17.6 us
  waiting for transfers between devices: 33.2 us -> 29.8 us
    unnamed x29 -> x4, local copies, waits for them, and re-layouts: 8.27 us -> 0.01 us
    ppermute x16 -> x15, starting transfers between devices: 23.3 us -> 16 us  [swap(): lax.ppermute(value, axis, [(i, i ^ bit) for i in range(lax.axis_size(axis...]
    ppermute x4, starting transfers between devices: 9.01 us -> 4.07 us  [exchange(): return lax.ppermute(value, 'pix', pairs + [(b, a) for a, b in pairs])]
    pallas_call x3, Pallas kernels: 5.97 us -> 9.67 us  [the longest x1 6.7 us: on_device(): call(functools.partial(forward_kernel, rows, levels), [((tok, width), BF)...]
    ppermute x16 -> x15, waiting for transfers between devices: 33.2 us -> 29.8 us  [swap(): lax.ppermute(value, axis, [(i, i ^ bit) for i in range(lax.axis_size(axis...]
  transfers between devices with their start and end apart: 20 -> 19, of which waited for: 9 -> 9; matrix products, arithmetic and copies ran while one was open for 1% -> 2% of each run, Pallas kernels for 8% -> 12%
where the time goes in v2:
time: 69.6 us; the launch traced here: 69.4 us
  waiting for transfers between devices  29.8 us (43%)
  starting transfers between devices  20.1 us (29%)
  Pallas kernels  17.6 us (25%)
  other arithmetic  1.09 us (2%)
  between operations  0.79 us (1%)
    ppermute x15, waiting for transfers between devices, swap(): lax.ppermute(value, axis, [(i, i ^ bit) for i in range(lax.axis_size(axis...  29.8 us
    ppermute x15, starting transfers between devices, swap(): lax.ppermute(value, axis, [(i, i ^ bit) for i in range(lax.axis_size(axis...  16 us
    pallas_call x1, Pallas kernels, on_device(): call(functools.partial(forward_kernel, rows, levels), [((tok, width), BF)...  6.7 us
    pallas_call x1, Pallas kernels, on_device(): call(functools.partial(backward_kernel, rows), [((tok, width), BF), ((2 *...  5.33 us
    ppermute x4, starting transfers between devices, exchange(): return lax.ppermute(value, 'pix', pairs + [(b, a) for a, b in pairs])  4.07 us
    pallas_call x1, Pallas kernels, on_device(): call(grad_kernel, [((tok, width), BF), ((tok, width), BF), ((tok, width),...  1.62 us
    pallas_call x1, Pallas kernels, on_device(): call(finish_kernel, [((tok, width), BF), ((tok, width), BF), ((rows, widt...  1.51 us
  transfers between devices with their start and end apart: 19, of which 9 were waited for; matrix products, arithmetic and copies ran while one was open for 2% of the time, Pallas kernels for 12%

profile of v2, /device:TPU:0, one launch (start us, length us, event | category | flops | bytes accessed | tf_op | source)
XLA Modules:
  0.0 69.4 jit_solution(11460793337885100381)
XLA Ops:
  0.6 1.3 %shard_map.153 = (bf16[512,256]{1,0:T(8,128)(2,1)S(1)}, bf16[512,256]{1,0:T(8,128)(2,1)S(1)}, bf16[512,256]{1,0:T(8,128)(2,1)S(1)}, bf16[512,256]{1,0:T(8,128)(2...) custom-call(bf16[512,256]{1,0:T(8,128)(2,1)} %k_hbm.1, bf16[512,256]{1,0:T(8,128)(2,1)} %v_hbm.1, ...), custom_call_target="tpu_custom_call" | custom-call | flops 4194304 | bytes 1048576 | tf_op jit(solution)/shard_map/pallas_call | solution.py:444
  2.0 3.0 %collective-permute-start = (bf16[512,256]{1,0:T(8,128)(2,1)}, bf16[512,256]{1,0:T(8,128)(2,1)S(1)}, u32[]{:S(2)}, u32[]{:S(2)}) collective-permute-start(bf16[512,256]{1,0:T(8,128)(2,1)} %gm_hbm.1), channel_id=1, source_target_pairs={{0,2},{1,3},{2,0},{3,1},{4,6},{5,7},{6,4},{7,5},{8,10},{9,11},{10,... | collective-permute-start | bytes 786440 | tf_op jit(solution)/shard_map/ppermute | solution.py:42
  5.0 1.5 %collective-permute-start.4 = (bf16[16,256]{1,0:T(8,128)(2,1)S(1)}, bf16[16,256]{1,0:T(8,128)(2,1)S(1)}, u32[]{:S(2)}, u32[]{:S(2)}) collective-permute-start(bf16[16,256]{1,0:T(8,128)(2,1)S(1)} %get-tuple-element.53), channel_id=1, source_target_pairs={{0,4},{4,0},{8,12},{12,8},{16,20},{20,16},{24,28},{28,24},{1,5},{5... | collective-permute-start | bytes 24584 | tf_op jit(solution)/shard_map/ppermute | solution.py:42
  6.5 2.1 %collective-permute-done.4 = bf16[16,256]{1,0:T(8,128)(2,1)S(1)} collective-permute-done((bf16[16,256]{1,0:T(8,128)(2,1)S(1)}, bf16[16,256]{1,0:T(8,128)(2,1)S(1)}, u32[]{:S(2)}, u32[]{:S(2)}) %collective-permute-start.4) | collective-permute-done | bytes 8224 | tf_op jit(solution)/shard_map/ppermute | solution.py:42
  8.6 1.6 %collective-permute-start.5 = (bf16[32,256]{1,0:T(8,128)(2,1)S(1)}, bf16[32,256]{1,0:T(8,128)(2,1)S(1)}, u32[]{:S(2)}, u32[]{:S(2)}) collective-permute-start(bf16[32,256]{1,0:T(8,128)(2,1)S(1)} %get-tuple-element.84), channel_id=1, source_target_pairs={{0,8},{4,12},{8,0},{12,4},{16,24},{20,28},{24,16},{28,20},{1,9},{5... | collective-permute-start | bytes 49160 | tf_op jit(solution)/shard_map/ppermute | solution.py:42
  10.2 1.5 %collective-permute-start.3 = (bf16[512,256]{1,0:T(8,128)(2,1)S(1)}, bf16[512,256]{1,0:T(8,128)(2,1)S(1)}, u32[]{:S(2)}, u32[]{:S(2)}) collective-permute-start(bf16[512,256]{1,0:T(8,128)(2,1)S(1)} %get-tuple-element.52), channel_id=1, source_target_pairs={{0,4},{8,12},{16,20},{24,28},{4,0},{12,8},{20,16},{28,24},{1,5},{9... | collective-permute-start | bytes 786440 | tf_op jit(solution)/shard_map/ppermute | solution.py:46
  11.7 2.6 %collective-permute-start.7 = (bf16[32,256]{1,0:T(8,128)(2,1)S(1)}, bf16[32,256]{1,0:T(8,128)(2,1)S(1)}, u32[]{:S(2)}, u32[]{:S(2)}) collective-permute-start(bf16[32,256]{1,0:T(8,128)(2,1)S(1)} %get-tuple-element.84), channel_id=1, source_target_pairs={{0,16},{4,20},{8,24},{12,28},{16,0},{20,4},{24,8},{28,12},{1,17},{... | collective-permute-start | bytes 49160 | tf_op jit(solution)/shard_map/ppermute | solution.py:42
  14.3 0.0 collective-permute-done.5
  14.3 0.7 collective-permute-start.6
  15.0 0.0 collective-permute-done.refs_1_.refs_12_
  15.0 0.1 collective-permute-start.1
  15.1 0.5 collective-permute-start.2
  15.6 0.9 %collective-permute-done.7 = bf16[32,256]{1,0:T(8,128)(2,1)S(1)} collective-permute-done((bf16[32,256]{1,0:T(8,128)(2,1)S(1)}, bf16[32,256]{1,0:T(8,128)(2,1)S(1)}, u32[]{:S(2)}, u32[]{:S(2)}) %collective-permute-start.7) | collective-permute-done | bytes 16416 | tf_op jit(solution)/shard_map/ppermute | solution.py:42
  16.5 3.4 %collective-permute-start.8 = (bf16[32,256]{1,0:T(8,128)(2,1)S(1)}, bf16[32,256]{1,0:T(8,128)(2,1)S(1)}, u32[]{:S(2)}, u32[]{:S(2)}) collective-permute-start(bf16[32,256]{1,0:T(8,128)(2,1)S(1)} %get-tuple-element.84), channel_id=1, source_target_pairs={{0,24},{4,28},{8,16},{12,20},{16,8},{20,12},{24,0},{28,4},{1,25},{... | collective-permute-start | bytes 49160 | tf_op jit(solution)/shard_map/ppermute | solution.py:42
  19.9 4.1 %collective-permute-done.8 = bf16[32,256]{1,0:T(8,128)(2,1)S(1)} collective-permute-done((bf16[32,256]{1,0:T(8,128)(2,1)S(1)}, bf16[32,256]{1,0:T(8,128)(2,1)S(1)}, u32[]{:S(2)}, u32[]{:S(2)}) %collective-permute-start.8) | collective-permute-done | bytes 16416 | tf_op jit(solution)/shard_map/ppermute | solution.py:42
  24.0 0.0 collective-permute-done.1.refs_0_.refs_11_
  24.0 0.0 collective-permute-done.2.refs_2_.refs_13_
  24.0 1.6 %shard_map.154 = (bf16[512,256]{1,0:T(8,128)(2,1)S(1)}, bf16[512,256]{1,0:T(8,128)(2,1)S(1)}, bf16[512,256]{1,0:T(8,128)(2,1)S(1)}, bf16[256,1024]{1,0:T(8,128)(2,1)S(1)}) custom-call(bf16[512,256]{1,0:T(8,128)(2,1)} %gm_hbm.1, bf16[512,256]{1,0:T(8,128)(2,1)} %q_hbm.1, bf16[256,1024]{1,0:T(8,128)(2,1)} %w_hbm.1, ...), custom_call_target="tpu_custom_call" | custom-call | flops 268435456 | bytes 2621440 | tf_op jit(solution)/shard_map/pallas_call | solution.py:485
  25.6 0.0 collective-permute-done.3.refs_5_.refs_4_
  25.6 0.0 collective-permute-done.6.refs_6_.refs_5_
  25.6 6.7 %shard_map.155 = (bf16[512,256]{1,0:T(8,128)(2,1)S(1)}, bf16[4,512,576]{2,1,0:T(8,128)(2,1)}, bf16[1024,256]{1,0:T(8,128)(2,1)S(1)}, bf16[1024,256]{1,0:T(8,128)...) custom-call(s32[4,4]{1,0:T(4,128)} %refs_0_.3, s32[4,8]{1,0:T(4,128)S(1)} %get-tuple-element.44.refs_1_, ...), custom_call_target="tpu_custom_call" | custom-call | flops 1744830464 | bytes 10000000 | tf_op jit(solution)/shard_map/pallas_call | solution.py:497
  32.3 0.4 collective-permute-start.11
  32.7 0.0 collective-permute-start.9
  32.7 5.3 %shard_map.156 = (bf16[512,256]{1,0:T(8,128)(2,1)}, f32[1024,256]{1,0:T(8,128)S(1)}, bf16[512,256]{1,0:T(8,128)(2,1)S(1)}, bf16[512,256]{1,0:T(8,128)(2,1)S(1)}) custom-call(s32[4,4]{1,0:T(4,128)} %refs_0_.3, bf16[512,256]{1,0:T(8,128)(2,1)S(1)} %get-tuple-element.49.refs_2_.refs_1_, bf16[512,256]{1,0:T(8,128)(2,1)S(1)} %get-tuple-element.50.refs_3_.refs_2_, ...), custom_call_target="tpu_custom_call" | custom-call | flops 2415919104 | bytes 10000000 | tf_op jit(solution)/shard_map/pallas_call | solution.py:524
  38.1 1.5 %collective-permute-done.11 = bf16[160,1024]{1,0:T(8,128)(2,1)S(1)} collective-permute-done((bf16[160,1024]{1,0:T(8,128)(2,1)S(1)}, bf16[160,1024]{1,0:T(8,128)(2,1)S(1)}, u32[]{:S(2)}, u32[]{:S(2)}) %collective-permute-start.11) | collective-permute-done | bytes 327712 | tf_op jit(solution)/shard_map/ppermute | solution.py:42
  39.5 0.1 convert_add_fusion.1
  39.6 0.7 collective-permute-start.14
  40.3 1.2 %collective-permute-start.12 = (bf16[512,256]{1,0:T(8,128)(2,1)S(1)}, bf16[512,256]{1,0:T(8,128)(2,1)S(1)}, u32[]{:S(2)}, u32[]{:S(2)}) collective-permute-start(bf16[512,256]{1,0:T(8,128)(2,1)S(1)} %get-tuple-element.73), channel_id=1, source_target_pairs={{0,4},{8,12},{16,20},{24,28},{4,0},{12,8},{20,16},{28,24},{1,5},{9... | collective-permute-start | bytes 786440 | tf_op jit(solution)/shard_map/ppermute | solution.py:46
  41.5 0.7 collective-permute-start.13
  42.2 3.1 %collective-permute-done.14 = bf16[80,1024]{1,0:T(8,128)(2,1)S(1)} collective-permute-done((bf16[80,1024]{1,0:T(8,128)(2,1)S(1)}, bf16[80,1024]{1,0:T(8,128)(2,1)S(1)}, u32[]{:S(2)}, u32[]{:S(2)}) %collective-permute-start.14) | collective-permute-done | bytes 163872 | tf_op jit(solution)/shard_map/ppermute | solution.py:42
  45.3 1.3 %collective-permute-start.15 = (bf16[80,1024]{1,0:T(8,128)(2,1)S(1)}, bf16[80,1024]{1,0:T(8,128)(2,1)S(1)}, u32[]{:S(2)}, u32[]{:S(2)}) collective-permute-start(bf16[80,1024]{1,0:T(8,128)(2,1)S(1)} %get-tuple-element.81), channel_id=1, source_target_pairs={{0,16},{4,20},{8,24},{12,28},{16,0},{20,4},{24,8},{28,12},{1,17},{... | collective-permute-start | bytes 491528 | tf_op jit(solution)/shard_map/ppermute | solution.py:42
  46.7 0.0 collective-permute-done.9
  46.7 0.1 convert_add_fusion
  46.9 0.6 collective-permute-start.10
  47.5 10.8 %collective-permute-done.15 = bf16[80,1024]{1,0:T(8,128)(2,1)S(1)} collective-permute-done((bf16[80,1024]{1,0:T(8,128)(2,1)S(1)}, bf16[80,1024]{1,0:T(8,128)(2,1)S(1)}, u32[]{:S(2)}, u32[]{:S(2)}) %collective-permute-start.15) | collective-permute-done | bytes 163872 | tf_op jit(solution)/shard_map/ppermute | solution.py:42
  58.4 0.1 collective-permute-start.16
  58.4 0.3 collective-permute-start.17
  58.8 0.0 collective-permute-done.12.near_ref
  58.8 0.0 collective-permute-done.13.far_ref
  58.8 1.5 %shard_map.157 = (bf16[512,256]{1,0:T(8,128)(2,1)}, bf16[512,256]{1,0:T(8,128)(2,1)}, f32[8,256]{1,0:T(8,128)}, f32[8,256]{1,0:T(8,128)}) custom-call(f32[1024,256]{1,0:T(8,128)S(1)} %get-tuple-element.65.own_ref, bf16[512,256]{1,0:T(8,128)(2,1)S(1)} %collective-permute-done.12.near_ref, bf16[512,256]{1,0:T(8,128)(2,1)S(1)} %collective-permute-done.13.far_ref, ...), custom_call_target="tpu_custom_call" | custom-call | flops 8388608 | bytes 2097152 | tf_op jit(solution)/shard_map/pallas_call | solution.py:595
  60.3 3.1 %collective-permute-done.16.refs_1_ = bf16[64,1024]{1,0:T(8,128)(2,1)S(1)} collective-permute-done((bf16[64,1024]{1,0:T(8,128)(2,1)S(1)}, bf16[64,1024]{1,0:T(8,128)(2,1)S(1)}, u32[]{:S(2)}, u32[]{:S(2)}) %collective-permute-start.16) | collective-permute-done | bytes 131104 | tf_op jit(solution)/shard_map/ppermute | solution.py:42
  63.4 0.0 collective-permute-start.18
  63.4 0.0 collective-permute-done.10
  63.4 0.8 %fusion = bf16[512,256]{1,0:T(8,128)(2,1)} fusion(f32[1024,256]{1,0:T(8,128)S(1)} %convert_add_fusion, bf16[512,256]{1,0:T(8,128)(2,1)S(1)} %collective-permute-done.10), kind=kLoop, calls=%fused_computation.4 | loop fusion | flops 393216 | bytes 1048576 | tf_op jit(solution)/shard_map/convert_element_type | solution.py:591
  64.2 0.6 collective-permute-done.17.refs_2_
  64.8 3.6 %collective-permute-done.18.refs_3_ = bf16[64,1024]{1,0:T(8,128)(2,1)S(1)} collective-permute-done((bf16[64,1024]{1,0:T(8,128)(2,1)S(1)}, bf16[64,1024]{1,0:T(8,128)(2,1)S(1)}, u32[]{:S(2)}, u32[]{:S(2)}) %collective-permute-start.18) | collective-permute-done | bytes 131104 | tf_op jit(solution)/shard_map/ppermute | solution.py:42
  68.4 1.1 %shard_map.158 = f32[256,1024]{1,0:T(8,128)} custom-call(bf16[64,1024]{1,0:T(8,128)(2,1)S(1)} %fusion.1.refs_0_, bf16[64,1024]{1,0:T(8,128)(2,1)S(1)} %collective-permute-done.16.refs_1_, bf16[64,1024]{1,0:T(8,128)(2,1)S(1)} %collective-permute-done.17.refs_2_, bf16[64,1024]{1,0:T(8,128)(2,1)S(1)} %collective-permute-done.18.refs_3_), custom_call_target="tpu_custom_call" | custom-call | bytes 1572864 | tf_op jit(solution)/shard_map/pallas_call | solution.py:577
  (11 shorter events, 0.2 us)
Async XLA Ops:
  2.0 13.0 %collective-permute-start = (bf16[512,256]{1,0:T(8,128)(2,1)}, bf16[512,256]{1,0:T(8,128)(2,1)S(1)}, u32[]{:S(2)}, u32[]{:S(2)}) collective-permute-start(bf16[512,256]{1,0:T(8,128)(2,1)} %gm_hbm.1), channel_id=1, source_target_pairs={{0,2},{1,3},{2,0},{3,1},{4,6},{5,7},{6,4},{7,5},{8,10},{9,11},{10,... | collective-permute-start | bytes 786440 | tf_op jit(solution)/shard_map/ppermute | solution.py:42
  5.0 3.7 %collective-permute-start.4 = (bf16[16,256]{1,0:T(8,128)(2,1)S(1)}, bf16[16,256]{1,0:T(8,128)(2,1)S(1)}, u32[]{:S(2)}, u32[]{:S(2)}) collective-permute-start(bf16[16,256]{1,0:T(8,128)(2,1)S(1)} %get-tuple-element.53), channel_id=1, source_target_pairs={{0,4},{4,0},{8,12},{12,8},{16,20},{20,16},{24,28},{28,24},{1,5},{5... | collective-permute-start | bytes 24584 | tf_op jit(solution)/shard_map/ppermute | solution.py:42
  8.6 5.7 %collective-permute-start.5 = (bf16[32,256]{1,0:T(8,128)(2,1)S(1)}, bf16[32,256]{1,0:T(8,128)(2,1)S(1)}, u32[]{:S(2)}, u32[]{:S(2)}) collective-permute-start(bf16[32,256]{1,0:T(8,128)(2,1)S(1)} %get-tuple-element.84), channel_id=1, source_target_pairs={{0,8},{4,12},{8,0},{12,4},{16,24},{20,28},{24,16},{28,20},{1,9},{5... | collective-permute-start | bytes 49160 | tf_op jit(solution)/shard_map/ppermute | solution.py:42
  10.2 15.4 %collective-permute-start.3 = (bf16[512,256]{1,0:T(8,128)(2,1)S(1)}, bf16[512,256]{1,0:T(8,128)(2,1)S(1)}, u32[]{:S(2)}, u32[]{:S(2)}) collective-permute-start(bf16[512,256]{1,0:T(8,128)(2,1)S(1)} %get-tuple-element.52), channel_id=1, source_target_pairs={{0,4},{8,12},{16,20},{24,28},{4,0},{12,8},{20,16},{28,24},{1,5},{9... | collective-permute-start | bytes 786440 | tf_op jit(solution)/shard_map/ppermute | solution.py:46
  11.7 4.8 %collective-permute-start.7 = (bf16[32,256]{1,0:T(8,128)(2,1)S(1)}, bf16[32,256]{1,0:T(8,128)(2,1)S(1)}, u32[]{:S(2)}, u32[]{:S(2)}) collective-permute-start(bf16[32,256]{1,0:T(8,128)(2,1)S(1)} %get-tuple-element.84), channel_id=1, source_target_pairs={{0,16},{4,20},{8,24},{12,28},{16,0},{20,4},{24,8},{28,12},{1,17},{... | collective-permute-start | bytes 49160 | tf_op jit(solution)/shard_map/ppermute | solution.py:42
  14.3 11.3 %collective-permute-start.6 = (bf16[512,256]{1,0:T(8,128)(2,1)S(1)}, bf16[512,256]{1,0:T(8,128)(2,1)S(1)}, u32[]{:S(2)}, u32[]{:S(2)}) collective-permute-start(bf16[512,256]{1,0:T(8,128)(2,1)S(1)} %get-tuple-element.55), channel_id=1, source_target_pairs={{4,8},{12,16},{20,24},{8,4},{16,12},{24,20},{5,9},{13,17},{21,25},... | collective-permute-start | bytes 786440 | tf_op jit(solution)/shard_map/ppermute | solution.py:46
  15.0 9.0 %collective-permute-start.1 = (bf16[512,256]{1,0:T(8,128)(2,1)}, bf16[512,256]{1,0:T(8,128)(2,1)S(1)}, u32[]{:S(2)}, u32[]{:S(2)}) collective-permute-start(bf16[512,256]{1,0:T(8,128)(2,1)} %gm_hbm.1), channel_id=1, source_target_pairs={{0,1},{1,0},{2,3},{3,2},{4,5},{5,4},{6,7},{7,6},{8,9},{9,8},{10,11... | collective-permute-start | bytes 786440 | tf_op jit(solution)/shard_map/ppermute | solution.py:42
  15.1 8.9 %collective-permute-start.2 = (bf16[512,256]{1,0:T(8,128)(2,1)S(1)}, bf16[512,256]{1,0:T(8,128)(2,1)S(1)}, u32[]{:S(2)}, u32[]{:S(2)}) collective-permute-start(bf16[512,256]{1,0:T(8,128)(2,1)S(1)} %collective-permute-done.refs_1_.refs_12_), channel_id=1, source_target_pairs={{0,1},{1,0},{2,3},{3,2},{4,5},{5,4},{6,7},{7,6},{8,9},{9,8},{10,11... | collective-permute-start | bytes 786440 | tf_op jit(solution)/shard_map/ppermute | solution.py:42
  16.5 7.5 %collective-permute-start.8 = (bf16[32,256]{1,0:T(8,128)(2,1)S(1)}, bf16[32,256]{1,0:T(8,128)(2,1)S(1)}, u32[]{:S(2)}, u32[]{:S(2)}) collective-permute-start(bf16[32,256]{1,0:T(8,128)(2,1)S(1)} %get-tuple-element.84), channel_id=1, source_target_pairs={{0,24},{4,28},{8,16},{12,20},{16,8},{20,12},{24,0},{28,4},{1,25},{... | collective-permute-start | bytes 49160 | tf_op jit(solution)/shard_map/ppermute | solution.py:42
  32.3 7.2 %collective-permute-start.11 = (bf16[160,1024]{1,0:T(8,128)(2,1)S(1)}, bf16[160,1024]{1,0:T(8,128)(2,1)S(1)}, u32[]{:S(2)}, u32[]{:S(2)}) collective-permute-start(bf16[160,1024]{1,0:T(8,128)(2,1)S(1)} %get-tuple-element.67), channel_id=1, source_target_pairs={{0,4},{4,0},{8,12},{12,8},{16,20},{20,16},{24,28},{28,24},{1,5},{5... | collective-permute-start | bytes 983048 | tf_op jit(solution)/shard_map/ppermute | solution.py:42
  32.7 14.0 %collective-permute-start.9 = (bf16[1024,256]{1,0:T(8,128)(2,1)S(1)}, bf16[1024,256]{1,0:T(8,128)(2,1)S(1)}, u32[]{:S(2)}, u32[]{:S(2)}) collective-permute-start(bf16[1024,256]{1,0:T(8,128)(2,1)S(1)} %get-tuple-element.61), channel_id=1, source_target_pairs={{0,1},{1,0},{2,3},{3,2},{4,5},{5,4},{6,7},{7,6},{8,9},{9,8},{10,11... | collective-permute-start | bytes 1572872 | tf_op jit(solution)/shard_map/ppermute | solution.py:42
  39.6 5.7 %collective-permute-start.14 = (bf16[80,1024]{1,0:T(8,128)(2,1)S(1)}, bf16[80,1024]{1,0:T(8,128)(2,1)S(1)}, u32[]{:S(2)}, u32[]{:S(2)}) collective-permute-start(bf16[80,1024]{1,0:T(8,128)(2,1)S(1)} %slice.59), channel_id=1, source_target_pairs={{0,8},{4,12},{8,0},{12,4},{16,24},{20,28},{24,16},{28,20},{1,9},{5... | collective-permute-start | bytes 491528 | tf_op jit(solution)/shard_map/ppermute | solution.py:42
  40.3 18.5 %collective-permute-start.12 = (bf16[512,256]{1,0:T(8,128)(2,1)S(1)}, bf16[512,256]{1,0:T(8,128)(2,1)S(1)}, u32[]{:S(2)}, u32[]{:S(2)}) collective-permute-start(bf16[512,256]{1,0:T(8,128)(2,1)S(1)} %get-tuple-element.73), channel_id=1, source_target_pairs={{0,4},{8,12},{16,20},{24,28},{4,0},{12,8},{20,16},{28,24},{1,5},{9... | collective-permute-start | bytes 786440 | tf_op jit(solution)/shard_map/ppermute | solution.py:46
  41.5 17.3 %collective-permute-start.13 = (bf16[512,256]{1,0:T(8,128)(2,1)S(1)}, bf16[512,256]{1,0:T(8,128)(2,1)S(1)}, u32[]{:S(2)}, u32[]{:S(2)}) collective-permute-start(bf16[512,256]{1,0:T(8,128)(2,1)S(1)} %get-tuple-element.74), channel_id=1, source_target_pairs={{4,8},{12,16},{20,24},{8,4},{16,12},{24,20},{5,9},{13,17},{21,25},... | collective-permute-start | bytes 786440 | tf_op jit(solution)/shard_map/ppermute | solution.py:46
  45.3 12.9 %collective-permute-start.15 = (bf16[80,1024]{1,0:T(8,128)(2,1)S(1)}, bf16[80,1024]{1,0:T(8,128)(2,1)S(1)}, u32[]{:S(2)}, u32[]{:S(2)}) collective-permute-start(bf16[80,1024]{1,0:T(8,128)(2,1)S(1)} %get-tuple-element.81), channel_id=1, source_target_pairs={{0,16},{4,20},{8,24},{12,28},{16,0},{20,4},{24,8},{28,12},{1,17},{... | collective-permute-start | bytes 491528 | tf_op jit(solution)/shard_map/ppermute | solution.py:42
  46.9 16.5 %collective-permute-start.10 = (bf16[512,256]{1,0:T(8,128)(2,1)S(1)}, bf16[512,256]{1,0:T(8,128)(2,1)S(1)}, u32[]{:S(2)}, u32[]{:S(2)}) collective-permute-start(bf16[512,256]{1,0:T(8,128)(2,1)S(1)} %slice.58), channel_id=1, source_target_pairs={{0,2},{1,3},{2,0},{3,1},{4,6},{5,7},{6,4},{7,5},{8,10},{9,11},{10,... | collective-permute-start | bytes 786440 | tf_op jit(solution)/shard_map/ppermute | solution.py:42
  58.4 5.0 %collective-permute-start.16 = (bf16[64,1024]{1,0:T(8,128)(2,1)S(1)}, bf16[64,1024]{1,0:T(8,128)(2,1)S(1)}, u32[]{:S(2)}, u32[]{:S(2)}) collective-permute-start(bf16[64,1024]{1,0:T(8,128)(2,1)S(1)} %fusion.1.refs_0_), channel_id=1, source_target_pairs={{0,8},{4,12},{8,0},{12,4},{16,24},{20,28},{24,16},{28,20},{1,9},{5... | collective-permute-start | bytes 393224 | tf_op jit(solution)/shard_map/ppermute | solution.py:42
  58.4 6.3 %collective-permute-start.17 = (bf16[64,1024]{1,0:T(8,128)(2,1)S(1)}, bf16[64,1024]{1,0:T(8,128)(2,1)S(1)}, u32[]{:S(2)}, u32[]{:S(2)}) collective-permute-start(bf16[64,1024]{1,0:T(8,128)(2,1)S(1)} %fusion.1.refs_0_), channel_id=1, source_target_pairs={{0,4},{4,0},{8,12},{12,8},{16,20},{20,16},{24,28},{28,24},{1,5},{5... | collective-permute-start | bytes 393224 | tf_op jit(solution)/shard_map/ppermute | solution.py:42
  63.4 5.0 %collective-permute-start.18 = (bf16[64,1024]{1,0:T(8,128)(2,1)S(1)}, bf16[64,1024]{1,0:T(8,128)(2,1)S(1)}, u32[]{:S(2)}, u32[]{:S(2)}) collective-permute-start(bf16[64,1024]{1,0:T(8,128)(2,1)S(1)} %collective-permute-done.16.refs_1_), channel_id=1, source_target_pairs={{0,4},{4,0},{8,12},{12,8},{16,20},{20,16},{24,28},{28,24},{1,5},{5... | collective-permute-start | bytes 393224 | tf_op jit(solution)/shard_map/ppermute | solution.py:42

commit v3 on v2

--- a/solution.py
+++ b/solution.py
@@ -103,30 +103,21 @@
 
 
 def prep_kernel(
-    k_hbm, v_hbm, ck_hbm, cv_hbm, pool_hbm, mask_hbm,
-    k_ref, v_ref, near_ref, far_ref, panel_ref, pool_ref, mask_ref,
+    k_hbm, v_hbm, ck_hbm, cv_hbm, pool_hbm,
+    k_ref, v_ref, panel_ref, pool_ref,
     ck_ref, cv_ref, sems,
 ):
-    tok = k_ref.shape[0]
-    odd = lax.axis_index("pix") & 1
-    near = pl.ds(pl.multiple_of((1 - odd) * (tok - RIM), RIM), RIM)
-    far = pl.ds(pl.multiple_of(odd * (tok - RIM), RIM), RIM)
     pairs = [
         (pool_hbm, pool_ref),
         (k_hbm, k_ref),
         (v_hbm, v_ref),
         (ck_hbm, ck_ref),
         (cv_hbm, cv_ref),
-        (k_hbm.at[near], near_ref.at[pl.ds(0, RIM)]),
-        (v_hbm.at[near], near_ref.at[pl.ds(RIM, RIM)]),
-        (k_hbm.at[far], far_ref.at[pl.ds(0, RIM)]),
-        (v_hbm.at[far], far_ref.at[pl.ds(RIM, RIM)]),
-        (mask_hbm, mask_ref),
     ]
     copies = [pltpu.make_async_copy(x, y, sems.at[i]) for i, (x, y) in enumerate(pairs)]
     for copy in copies:
         copy.start()
-    for copy in copies[:5]:
+    for copy in copies:
         copy.wait()
     member = membership(pool_ref, ck_ref.shape[0]).astype(F32)
     counts = jnp.sum(member, axis=1, keepdims=True)
@@ -134,30 +125,41 @@
     panel_k = mm(member, k_ref[...]) / counts + ck_ref[...].astype(F32)
     panel_v = mm(member, v_ref[...]) / counts + cv_ref[...].astype(F32)
     panel_ref[...] = jnp.concatenate([panel_k, panel_v], 0).astype(BF)
-    for copy in copies[5:]:
-        copy.wait()
-
-
-def grad_kernel(gm_hbm, q_hbm, w_hbm, *refs):
-    pieces = refs[:-5]
-    go_ref, gm_ref, q_ref, w_ref, sems = refs[-5:]
+
+
+def rim_kernel(k_ref, v_ref, panel_ref, near_ref, far_ref):
+    tok = k_ref.shape[0]
+    odd = lax.axis_index("pix") & 1
+    near = pl.ds(pl.multiple_of((1 - odd) * (tok - RIM), RIM), RIM)
+    far = pl.ds(pl.multiple_of(odd * (tok - RIM), RIM), RIM)
+    near_ref[0:RIM] = k_ref[near, :]
+    near_ref[RIM:] = v_ref[near, :]
+    far_ref[0:RIM] = k_ref[far, :]
+    far_ref[RIM:] = v_ref[far, :]
+
+
+def load_kernel(*refs):
+    count = len(refs) // 2
+    sems = refs[-1]
     copies = [
-        pltpu.make_async_copy(x, y, sems.at[i])
-        for i, (x, y) in enumerate([(w_hbm, w_ref), (gm_hbm, gm_ref), (q_hbm, q_ref)])
+        pltpu.make_async_copy(refs[i], refs[count + i], sems.at[i]) for i in range(count)
     ]
     for copy in copies:
         copy.start()
+    for copy in copies:
+        copy.wait()
+
+
+def grad_kernel(w_ref, *refs):
+    pieces, go_ref = refs[:-1], refs[-1]
     me = lax.axis_index("head")
     width = w_ref.shape[0]
-    copies[0].wait()
-    copies[1].wait()
     total = None
-    for j, ref in enumerate((gm_ref,) + pieces):
+    for j, ref in enumerate(pieces):
         w = w_ref[:, pl.ds(pl.multiple_of((me ^ j) * width, width), width)]
         part = mm_t(ref[...], w)
         total = part if total is None else total + part
     go_ref[...] = total.astype(BF)
-    copies[2].wait()
 
 
 def head_masks(width, rows):
@@ -356,8 +358,12 @@
     far = pl.ds(pl.multiple_of(odd * (tok + RIM), RIM), RIM)
     to_near[0:RIM] = sum_k[near, :].astype(BF)
     to_near[RIM:] = sum_v[near, :].astype(BF)
-    to_far[0:RIM] = sum_k[far, :].astype(BF)
-    to_far[RIM:] = sum_v[far, :].astype(BF)
+    to_far[0:RIM] = sum_k[far, :]
+    to_far[RIM:] = sum_v[far, :]
+
+
+def round_kernel(wide_ref, after_ref, out_ref):
+    out_ref[...] = wide_ref[...].astype(BF)
 
 
 def finish_kernel(
@@ -420,7 +426,8 @@
     levels = min(2, len(bits))
     heads = width // HDIM
     pool_row = pool_map.reshape(1, tok)
-    keys_hbm, values_hbm, ck_hbm, cv_hbm, pool_hbm, mask_hbm, nbr_hbm, gm_hbm, q_hbm, w_hbm = [
+    q_in, gm_in, w_in, mask_in = queries, grad_mixed, w_out, coarse_mask
+    keys_hbm, values_hbm, ck_hbm, cv_hbm, pool_hbm, nbr_hbm = [
         pltpu.with_memory_space_constraint(x, pltpu.HBM)
         for x in (
             keys,
@@ -428,11 +435,7 @@
             coarse_keys,
             coarse_values,
             pool_row,
-            coarse_mask,
             neighbors,
-            grad_mixed,
-            queries,
-            w_out,
         )
     ]
     across = head
@@ -441,55 +444,63 @@
     chunk = width // slots
     segment = chunk + held
 
-    k_own, v_own, send_near, send_far, panel, pool_own, mask_own = call(
+    k_own, v_own, panel, pool_own = call(
         prep_kernel,
+        [((tok, width), BF), ((tok, width), BF), ((2 * rows, width), BF), ((1, tok), jnp.int32)],
+        [HBM] * 5,
+        scratch=[
+            pltpu.VMEM((rows, width), BF),
+            pltpu.VMEM((rows, width), BF),
+            pltpu.SemaphoreType.DMA((5,)),
+        ],
+    )(keys_hbm, values_hbm, ck_hbm, cv_hbm, pool_hbm)
+    grad_early, panel = lax.optimization_barrier((grad_mixed, panel))
+    panel = gather_bits(panel, bits[:1])
+    send_near, send_far = call(
+        rim_kernel,
+        [((2 * RIM, width), BF), ((2 * RIM, width), BF)],
+        [VMEM] * 3,
+        flops=3_000_000_000,
+        bytes_accessed=4_000_000,
+    )(k_own, v_own, panel)
+    near = exchange(send_near, near_pairs(pix))
+    late = (q_in, gm_in, w_in, mask_in)
+    first = True
+    for at in range(1, len(bits), 2):
+        parts = gather_parts(panel, bits[at : at + 2])
+        if first and len(parts) > 1:
+            parts[1], send_far, *late = lax.optimization_barrier((parts[1], send_far, *late))
+            first = False
+        panel = jnp.concatenate(parts, 0)
+    far = exchange(send_far, far_pairs(pix))
+    q_own, gm_own, w_own, mask_own = call(
+        load_kernel,
         [
             ((tok, width), BF),
             ((tok, width), BF),
-            ((2 * RIM, width), BF),
-            ((2 * RIM, width), BF),
-            ((2 * rows, width), BF),
-            ((1, tok), jnp.int32),
+            ((width, d_model), BF),
             (coarse_mask.shape, jnp.int32),
         ],
-        [HBM] * 6,
-        scratch=[
-            pltpu.VMEM((rows, width), BF),
-            pltpu.VMEM((rows, width), BF),
-            pltpu.SemaphoreType.DMA((10,)),
-        ],
-        flops=4 * rows * tok * width,
-        bytes_accessed=4 * tok * width * 2,
-    )(keys_hbm, values_hbm, ck_hbm, cv_hbm, pool_hbm, mask_hbm)
-
-    grad_early, panel = lax.optimization_barrier((grad_mixed, panel))
-    near = exchange(send_near, near_pairs(pix))
-    panel = gather_bits(panel, bits[:1])
-    first = None
-    for at in range(1, len(bits), 2):
-        parts = gather_parts(panel, bits[at : at + 2])
-        if first is None and len(parts) > 1:
-            parts[1], send_far = lax.optimization_barrier((parts[1], send_far))
-            first = parts[1]
-        panel = jnp.concatenate(parts, 0)
-    far = exchange(send_far, far_pairs(pix))
+        [HBM] * 4,
+        scratch=[pltpu.SemaphoreType.DMA((4,))],
+        bytes_accessed=0,
+    )(*[pltpu.with_memory_space_constraint(x, pltpu.HBM) for x in late])
 
     order = [grad_early]
     index = [0]
     for bit in reversed(head_bits):
         if len(order) > 1:
-            order = list(lax.optimization_barrier(tuple(order)))
+            *order, near = lax.optimization_barrier((*order, near))
         order = order + [swap(piece, "head", bit) for piece in order]
         index = index + [i ^ bit for i in index]
     grads = [order[index.index(j)] for j in range(1, head)]
-    grad_attn, gm_own, q_own, w_own = call(
+    (grad_attn,) = call(
         grad_kernel,
-        [((tok, width), BF), ((tok, width), BF), ((tok, width), BF), ((width, d_model), BF)],
-        [HBM] * 3 + [VMEM] * (head - 1),
-        scratch=[pltpu.SemaphoreType.DMA((3,))],
-        flops=2 * tok * width * d_model,
-        bytes_accessed=(2 * tok * d_model + width * d_model) * 2,
-    )(gm_hbm, q_hbm, w_hbm, *grads)
+        [((tok, width), BF)],
+        [VMEM] * (1 + head),
+        flops=0,
+        bytes_accessed=0,
+    )(w_own, gm_own, *grads)
 
     keys_each = NBR * BLK + coarse
     tall = heads * BLK
@@ -527,7 +538,7 @@
             ((tok, width), BF),
             ((2 * tok, width), F32),
             ((2 * RIM, width), BF),
-            ((2 * RIM, width), BF),
+            ((2 * RIM, width), F32),
         ],
         [HBM] + [VMEM] * 8 + [HBM],
         scratch=[
@@ -553,12 +564,20 @@
         half = total.shape[0] // 2
         if level + 1 < levels:
             kept, sent = total[:half], total[half:].astype(BF)
-            sent, to_near, to_far = lax.optimization_barrier((sent, to_near, to_far))
+            sent, to_near = lax.optimization_barrier((sent, to_near))
     whole = total
+    sent = lax.optimization_barrier(whole.astype(BF))
+    (to_far,) = call(
+        round_kernel,
+        [((2 * RIM, width), BF)],
+        [VMEM] * 2,
+        flops=3_000_000_000,
+        bytes_accessed=4_000_000,
+    )(to_far, sent)
     cells = cut(whole[chunk:], 2 * rows, width, pix // slots)
     part = whole[:chunk]
     for bit in bits[levels:]:
-        got = swap(whole.astype(BF), "pix", bit).astype(F32)
+        got = swap(sent, "pix", bit).astype(F32)
         part = part + got[:chunk]
         other = cut(got[chunk:], 2 * rows, width, len(cells))
         cells = [cells[t] + other[t ^ 1] for t in range(0, len(cells), 2)]
@@ -568,12 +587,16 @@
             lines = [
                 jnp.concatenate(full[t : t + across], 1) for t in range(0, len(full), across)
             ]
-            whole = jnp.concatenate([part] + lines, 0)
+            sent = jnp.concatenate([part] + lines, 0).astype(BF)
     coarse_grads = cells[0]
     part = part.astype(BF)
     gathered_parts = [part]
     for bit in reversed(bits[:levels]):
         gathered_parts = gathered_parts + [swap(p, "pix", bit) for p in gathered_parts]
+        if len(gathered_parts) == 2:
+            gathered_parts[1], coarse_grads = lax.optimization_barrier(
+                (gathered_parts[1], coarse_grads)
+            )
     (grad_w_out,) = call(
         functools.partial(gw_kernel, levels, (tok * pix) ** (-0.5)),
         [((width, d_model), F32)],
@@ -597,7 +620,7 @@
         [((tok, width), BF), ((tok, width), BF), ((rows, width), F32), ((rows, width), F32)],
         [VMEM] * 5,
         scratch=[pltpu.VMEM((tok, width), F32)],
-        flops=8 * rows * tok * width,
+        flops=3_000_000_000,
         bytes_accessed=16 * tok * width,
     )(own, got_near, got_far, coarse_grads, pool_own)
     return (mixed, grad_queries, grad_keys, grad_values, grad_ck, grad_cv, grad_w_out)

time: 69.6 us -> 62.7 us (0.901)
  waiting for transfers between devices: 29.8 us -> 17 us
  starting transfers between devices: 20.1 us -> 25.9 us
    ppermute x15, waiting for transfers between devices: 29.8 us -> 16.7 us  [swap(): lax.ppermute(value, axis, [(i, i ^ bit) for i in range(lax.axis_size(axis...]
    ppermute x15, starting transfers between devices: 16 us -> 21.6 us  [swap(): lax.ppermute(value, axis, [(i, i ^ bit) for i in range(lax.axis_size(axis...]
    pallas_call x2 -> x5, Pallas kernels: 2.97 us -> 3.07 us  [the longest x1 1.29 us: on_device(): call(prep_kernel, [((tok, width), BF), ((tok, width), BF), ((2 * rows, wi...]
  transfers between devices with their start and end apart: 19 -> 19, of which waited for: 9 -> 8; matrix products, arithmetic and copies ran while one was open for 2% -> 2% of each run, Pallas kernels for 12% -> 14%
where the time goes in v3:
time: 62.7 us; the launch traced here: 62.5 us
  starting transfers between devices  25.9 us (41%)
  Pallas kernels  17.7 us (28%)
  waiting for transfers between devices  17 us (27%)
  other arithmetic  1.09 us (2%)
  between operations  0.79 us (1%)
    ppermute x15, starting transfers between devices, swap(): lax.ppermute(value, axis, [(i, i ^ bit) for i in range(lax.axis_size(axis...  21.6 us
    ppermute x15, waiting for transfers between devices, swap(): lax.ppermute(value, axis, [(i, i ^ bit) for i in range(lax.axis_size(axis...  16.7 us
    pallas_call x1, Pallas kernels, on_device(): call(functools.partial(forward_kernel, rows, levels), [((tok, width), BF)...  6.72 us
    pallas_call x1, Pallas kernels, on_device(): call(functools.partial(backward_kernel, rows), [((tok, width), BF), ((2 *...  5.34 us
    ppermute x4, starting transfers between devices, exchange(): return lax.ppermute(value, 'pix', pairs + [(b, a) for a, b in pairs])  4.3 us
    pallas_call x1, Pallas kernels, on_device(): call(finish_kernel, [((tok, width), BF), ((tok, width), BF), ((rows, widt...  1.52 us
    pallas_call x1, Pallas kernels, on_device(): call(prep_kernel, [((tok, width), BF), ((tok, width), BF), ((2 * rows, wi...  1.29 us
  transfers between devices with their start and end apart: 19, of which 8 were waited for; matrix products, arithmetic and copies ran while one was open for 2% of the time, Pallas kernels for 14%

profile of v3, /device:TPU:0, one launch (start us, length us, event | category | flops | bytes accessed | tf_op | source)
XLA Modules:
  0.0 62.5 jit_solution(6479859768518579280)
XLA Ops:
  0.6 1.3 %shard_map.153 = (bf16[512,256]{1,0:T(8,128)(2,1)S(1)}, bf16[512,256]{1,0:T(8,128)(2,1)S(1)}, bf16[16,256]{1,0:T(8,128)(2,1)S(1)}, s32[1,512]{1,0:T(1,128)S(1)}) custom-call(bf16[512,256]{1,0:T(8,128)(2,1)} %k_hbm.1, bf16[512,256]{1,0:T(8,128)(2,1)} %v_hbm.1, bf16[8,256]{1,0:T(8,128)(2,1)} %ck_hbm.1, bf16[8,256]{1,0:T(8,128)(2,1)} %cv_hbm.1, s32[1,512]{1,0:T(1,128)} %bitcast.1), custom_call_target="tpu_custom_call" | custom-call | tf_op jit(solution)/shard_map/pallas_call | solution.py:447
  1.9 3.0 %collective-permute-start = (bf16[16,256]{1,0:T(8,128)(2,1)S(1)}, bf16[16,256]{1,0:T(8,128)(2,1)S(1)}, u32[]{:S(2)}, u32[]{:S(2)}) collective-permute-start(bf16[16,256]{1,0:T(8,128)(2,1)S(1)} %get-tuple-element.50), channel_id=1, source_target_pairs={{0,4},{4,0},{8,12},{12,8},{16,20},{20,16},{24,28},{28,24},{1,5},{5... | collective-permute-start | bytes 24584 | tf_op jit(solution)/shard_map/ppermute | solution.py:42
  5.0 1.5 %collective-permute-start.2 = (bf16[512,256]{1,0:T(8,128)(2,1)}, bf16[512,256]{1,0:T(8,128)(2,1)S(1)}, u32[]{:S(2)}, u32[]{:S(2)}) collective-permute-start(bf16[512,256]{1,0:T(8,128)(2,1)} %refs_1_), channel_id=1, source_target_pairs={{0,2},{1,3},{2,0},{3,1},{4,6},{5,7},{6,4},{7,5},{8,10},{9,11},{10,... | collective-permute-start | bytes 786440 | tf_op jit(solution)/shard_map/ppermute | solution.py:42
  6.5 0.1 collective-permute-done
  6.6 2.1 %collective-permute-start.3 = (bf16[512,256]{1,0:T(8,128)(2,1)S(1)}, bf16[512,256]{1,0:T(8,128)(2,1)S(1)}, u32[]{:S(2)}, u32[]{:S(2)}) collective-permute-start(bf16[512,256]{1,0:T(8,128)(2,1)S(1)} %get-tuple-element.61), channel_id=1, source_target_pairs={{0,4},{8,12},{16,20},{24,28},{4,0},{12,8},{20,16},{28,24},{1,5},{9... | collective-permute-start | bytes 786440 | tf_op jit(solution)/shard_map/ppermute | solution.py:46
  8.7 1.6 %collective-permute-start.1 = (bf16[32,256]{1,0:T(8,128)(2,1)S(1)}, bf16[32,256]{1,0:T(8,128)(2,1)S(1)}, u32[]{:S(2)}, u32[]{:S(2)}) collective-permute-start(bf16[32,256]{1,0:T(8,128)(2,1)S(1)} %get-tuple-element.94.panel_ref), channel_id=1, source_target_pairs={{0,8},{4,12},{8,0},{12,4},{16,24},{20,28},{24,16},{28,20},{1,9},{5... | collective-permute-start | bytes 49160 | tf_op jit(solution)/shard_map/ppermute | solution.py:42
  10.3 2.6 %collective-permute-start.5 = (bf16[32,256]{1,0:T(8,128)(2,1)S(1)}, bf16[32,256]{1,0:T(8,128)(2,1)S(1)}, u32[]{:S(2)}, u32[]{:S(2)}) collective-permute-start(bf16[32,256]{1,0:T(8,128)(2,1)S(1)} %get-tuple-element.94.panel_ref), channel_id=1, source_target_pairs={{0,16},{4,20},{8,24},{12,28},{16,0},{20,4},{24,8},{28,12},{1,17},{... | collective-permute-start | bytes 49160 | tf_op jit(solution)/shard_map/ppermute | solution.py:42
  12.9 0.2 collective-permute-start.6
  13.1 0.0 collective-permute-done.1
  13.1 0.7 %collective-permute-start.4 = (bf16[512,256]{1,0:T(8,128)(2,1)S(1)}, bf16[512,256]{1,0:T(8,128)(2,1)S(1)}, u32[]{:S(2)}, u32[]{:S(2)}) collective-permute-start(bf16[512,256]{1,0:T(8,128)(2,1)S(1)} %get-tuple-element.63), channel_id=1, source_target_pairs={{4,8},{12,16},{20,24},{8,4},{16,12},{24,20},{5,9},{13,17},{21,25},... | collective-permute-start | bytes 786440 | tf_op jit(solution)/shard_map/ppermute | solution.py:46
  13.8 0.0 collective-permute-done.2.refs_2_.refs_12_
  13.8 0.3 collective-permute-done.3.refs_5_.refs_4_
  14.1 0.0 collective-permute-start.7
  14.1 0.5 collective-permute-start.8
  14.6 0.4 collective-permute-done.5
  15.0 1.2 %shard_map.155 = (bf16[512,256]{1,0:T(8,128)(2,1)S(1)}, bf16[512,256]{1,0:T(8,128)(2,1)S(1)}, bf16[256,1024]{1,0:T(8,128)(2,1)S(1)}, s32[4,8]{1,0:T(4,128)S(1)}) custom-call(bf16[512,256]{1,0:T(8,128)(2,1)} %refs_0_.2, bf16[512,256]{1,0:T(8,128)(2,1)} %refs_1_, bf16[256,1024]{1,0:T(8,128)(2,1)} %refs_2_, s32[4,8]{1,0:T(4,128)} %refs_3_), custom_call_target="tpu_custom_call" | custom-call | tf_op jit(solution)/shard_map/pallas_call | solution.py:476
  16.2 2.5 %collective-permute-done.6 = bf16[32,256]{1,0:T(8,128)(2,1)S(1)} collective-permute-done((bf16[32,256]{1,0:T(8,128)(2,1)S(1)}, bf16[32,256]{1,0:T(8,128)(2,1)S(1)}, u32[]{:S(2)}, u32[]{:S(2)}) %collective-permute-start.6) | collective-permute-done | bytes 16416 | tf_op jit(solution)/shard_map/ppermute | solution.py:42
  18.7 0.0 collective-permute-done.7.refs_1_.refs_11_
  18.7 0.0 collective-permute-done.8.refs_3_.refs_13_
  18.7 0.5 shard_map.156.refs_9_.refs_7_
  19.2 0.0 collective-permute-done.4.refs_6_.refs_5_
  19.2 6.7 %shard_map.157 = (bf16[512,256]{1,0:T(8,128)(2,1)S(1)}, bf16[4,512,576]{2,1,0:T(8,128)(2,1)}, bf16[1024,256]{1,0:T(8,128)(2,1)S(1)}, bf16[1024,256]{1,0:T(8,128)...) custom-call(s32[4,4]{1,0:T(4,128)} %refs_0_.4, s32[4,8]{1,0:T(4,128)S(1)} %get-tuple-element.58.refs_1_, ...), custom_call_target="tpu_custom_call" | custom-call | flops 1744830464 | bytes 10000000 | tf_op jit(solution)/shard_map/pallas_call | solution.py:508
  25.9 3.6 %collective-permute-start.11 = (bf16[160,1024]{1,0:T(8,128)(2,1)S(1)}, bf16[160,1024]{1,0:T(8,128)(2,1)S(1)}, u32[]{:S(2)}, u32[]{:S(2)}) collective-permute-start(bf16[160,1024]{1,0:T(8,128)(2,1)S(1)} %get-tuple-element.76), channel_id=1, source_target_pairs={{0,4},{4,0},{8,12},{12,8},{16,20},{20,16},{24,28},{28,24},{1,5},{5... | collective-permute-start | bytes 983048 | tf_op jit(solution)/shard_map/ppermute | solution.py:42
  29.5 5.3 %shard_map.158 = (bf16[512,256]{1,0:T(8,128)(2,1)}, f32[1024,256]{1,0:T(8,128)S(1)}, bf16[512,256]{1,0:T(8,128)(2,1)S(1)}, f32[512,256]{1,0:T(8,128)S(1)}) custom-call(s32[4,4]{1,0:T(4,128)} %refs_0_.4, bf16[512,256]{1,0:T(8,128)(2,1)S(1)} %get-tuple-element.59.refs_2_.refs_1_, bf16[512,256]{1,0:T(8,128)(2,1)S(1)} %get-tuple-element.51.k_ref.refs_3_.refs_2_, ...), custom_call_target="tpu_custom_call" | custom-call | flops 2415919104 | bytes 10000000 | tf_op jit(solution)/shard_map/pallas_call | solution.py:535
  34.9 0.0 collective-permute-done.11
  34.9 0.1 convert_add_fusion.1
  35.0 2.3 %collective-permute-start.13 = (bf16[80,1024]{1,0:T(8,128)(2,1)S(1)}, bf16[80,1024]{1,0:T(8,128)(2,1)S(1)}, u32[]{:S(2)}, u32[]{:S(2)}) collective-permute-start(bf16[80,1024]{1,0:T(8,128)(2,1)S(1)} %slice.59), channel_id=1, source_target_pairs={{0,8},{4,12},{8,0},{12,4},{16,24},{20,28},{24,16},{28,20},{1,9},{5... | collective-permute-start | bytes 491528 | tf_op jit(solution)/shard_map/ppermute | solution.py:42
  37.3 0.0 collective-permute-start.9
  37.3 0.9 %collective-permute-start.12 = (bf16[512,256]{1,0:T(8,128)(2,1)S(1)}, bf16[512,256]{1,0:T(8,128)(2,1)S(1)}, u32[]{:S(2)}, u32[]{:S(2)}) collective-permute-start(bf16[512,256]{1,0:T(8,128)(2,1)S(1)} %get-tuple-element.81), channel_id=1, source_target_pairs={{0,4},{8,12},{16,20},{24,28},{4,0},{12,8},{20,16},{28,24},{1,5},{9... | collective-permute-start | bytes 786440 | tf_op jit(solution)/shard_map/ppermute | solution.py:46
  38.2 2.4 %collective-permute-done.13 = bf16[80,1024]{1,0:T(8,128)(2,1)S(1)} collective-permute-done((bf16[80,1024]{1,0:T(8,128)(2,1)S(1)}, bf16[80,1024]{1,0:T(8,128)(2,1)S(1)}, u32[]{:S(2)}, u32[]{:S(2)}) %collective-permute-start.13) | collective-permute-done | bytes 163872 | tf_op jit(solution)/shard_map/ppermute | solution.py:42
  40.7 3.9 %collective-permute-start.15 = (bf16[80,1024]{1,0:T(8,128)(2,1)S(1)}, bf16[80,1024]{1,0:T(8,128)(2,1)S(1)}, u32[]{:S(2)}, u32[]{:S(2)}) collective-permute-start(bf16[80,1024]{1,0:T(8,128)(2,1)S(1)} %get-tuple-element.91.after_ref), channel_id=1, source_target_pairs={{0,16},{4,20},{8,24},{12,28},{16,0},{20,4},{24,8},{28,12},{1,17},{... | collective-permute-start | bytes 491528 | tf_op jit(solution)/shard_map/ppermute | solution.py:42
  44.6 0.7 %collective-permute-start.14 = (bf16[512,256]{1,0:T(8,128)(2,1)S(1)}, bf16[512,256]{1,0:T(8,128)(2,1)S(1)}, u32[]{:S(2)}, u32[]{:S(2)}) collective-permute-start(bf16[512,256]{1,0:T(8,128)(2,1)S(1)} %shard_map.159), channel_id=1, source_target_pairs={{4,8},{12,16},{20,24},{8,4},{16,12},{24,20},{5,9},{13,17},{21,25},... | collective-permute-start | bytes 786440 | tf_op jit(solution)/shard_map/ppermute | solution.py:46
  45.3 0.0 collective-permute-done.9
  45.3 0.1 convert_add_fusion
  45.5 1.6 %collective-permute-start.10 = (bf16[512,256]{1,0:T(8,128)(2,1)S(1)}, bf16[512,256]{1,0:T(8,128)(2,1)S(1)}, u32[]{:S(2)}, u32[]{:S(2)}) collective-permute-start(bf16[512,256]{1,0:T(8,128)(2,1)S(1)} %slice.58), channel_id=1, source_target_pairs={{0,2},{1,3},{2,0},{3,1},{4,6},{5,7},{6,4},{7,5},{8,10},{9,11},{10,... | collective-permute-start | bytes 786440 | tf_op jit(solution)/shard_map/ppermute | solution.py:42
  47.0 4.3 %collective-permute-done.15 = bf16[80,1024]{1,0:T(8,128)(2,1)S(1)} collective-permute-done((bf16[80,1024]{1,0:T(8,128)(2,1)S(1)}, bf16[80,1024]{1,0:T(8,128)(2,1)S(1)}, u32[]{:S(2)}, u32[]{:S(2)}) %collective-permute-start.15) | collective-permute-done | bytes 163872 | tf_op jit(solution)/shard_map/ppermute | solution.py:42
  51.4 0.6 %collective-permute-start.16 = (bf16[64,1024]{1,0:T(8,128)(2,1)S(1)}, bf16[64,1024]{1,0:T(8,128)(2,1)S(1)}, u32[]{:S(2)}, u32[]{:S(2)}) collective-permute-start(bf16[64,1024]{1,0:T(8,128)(2,1)S(1)} %fusion.1.refs_0_), channel_id=1, source_target_pairs={{0,8},{4,12},{8,0},{12,4},{16,24},{20,28},{24,16},{28,20},{1,9},{5... | collective-permute-start | bytes 393224 | tf_op jit(solution)/shard_map/ppermute | solution.py:42
  52.1 0.1 collective-permute-start.17
  52.2 4.3 %collective-permute-done.16.refs_1_ = bf16[64,1024]{1,0:T(8,128)(2,1)S(1)} collective-permute-done((bf16[64,1024]{1,0:T(8,128)(2,1)S(1)}, bf16[64,1024]{1,0:T(8,128)(2,1)S(1)}, u32[]{:S(2)}, u32[]{:S(2)}) %collective-permute-start.16) | collective-permute-done | bytes 131104 | tf_op jit(solution)/shard_map/ppermute | solution.py:42
  56.5 0.0 collective-permute-start.18
  56.5 0.0 collective-permute-done.12.near_ref
  56.5 0.0 collective-permute-done.14.far_ref
  56.5 1.5 %shard_map.160 = (bf16[512,256]{1,0:T(8,128)(2,1)}, bf16[512,256]{1,0:T(8,128)(2,1)}, f32[8,256]{1,0:T(8,128)}, f32[8,256]{1,0:T(8,128)}) custom-call(f32[1024,256]{1,0:T(8,128)S(1)} %get-tuple-element.74.own_ref, bf16[512,256]{1,0:T(8,128)(2,1)S(1)} %collective-permute-done.12.near_ref, bf16[512,256]{1,0:T(8,128)(2,1)S(1)} %collective-permute-done.14.far_ref, ...), custom_call_target="tpu_custom_call" | custom-call | flops 3000000000 | bytes 2097152 | tf_op jit(solution)/shard_map/pallas_call | solution.py:618
  58.1 0.0 collective-permute-done.10
  58.1 0.8 %fusion = bf16[512,256]{1,0:T(8,128)(2,1)} fusion(f32[1024,256]{1,0:T(8,128)S(1)} %convert_add_fusion, bf16[512,256]{1,0:T(8,128)(2,1)S(1)} %collective-permute-done.10), kind=kLoop, calls=%fused_computation.4 | loop fusion | flops 393216 | bytes 1048576 | tf_op jit(solution)/shard_map/convert_element_type | solution.py:614
  58.8 0.0 collective-permute-done.17.refs_2_
  58.8 2.6 %collective-permute-done.18.refs_3_ = bf16[64,1024]{1,0:T(8,128)(2,1)S(1)} collective-permute-done((bf16[64,1024]{1,0:T(8,128)(2,1)S(1)}, bf16[64,1024]{1,0:T(8,128)(2,1)S(1)}, u32[]{:S(2)}, u32[]{:S(2)}) %collective-permute-start.18) | collective-permute-done | bytes 131104 | tf_op jit(solution)/shard_map/ppermute | solution.py:42
  61.5 1.1 %shard_map.161 = f32[256,1024]{1,0:T(8,128)} custom-call(bf16[64,1024]{1,0:T(8,128)(2,1)S(1)} %fusion.1.refs_0_, bf16[64,1024]{1,0:T(8,128)(2,1)S(1)} %collective-permute-done.16.refs_1_, bf16[64,1024]{1,0:T(8,128)(2,1)S(1)} %collective-permute-done.17.refs_2_, bf16[64,1024]{1,0:T(8,128)(2,1)S(1)} %collective-permute-done.18.refs_3_), custom_call_target="tpu_custom_call" | custom-call | bytes 1572864 | tf_op jit(solution)/shard_map/pallas_call | solution.py:600
  (15 shorter events, 0.2 us)
Async XLA Ops:
  1.9 4.7 %collective-permute-start = (bf16[16,256]{1,0:T(8,128)(2,1)S(1)}, bf16[16,256]{1,0:T(8,128)(2,1)S(1)}, u32[]{:S(2)}, u32[]{:S(2)}) collective-permute-start(bf16[16,256]{1,0:T(8,128)(2,1)S(1)} %get-tuple-element.50), channel_id=1, source_target_pairs={{0,4},{4,0},{8,12},{12,8},{16,20},{20,16},{24,28},{28,24},{1,5},{5... | collective-permute-start | bytes 24584 | tf_op jit(solution)/shard_map/ppermute | solution.py:42
  5.0 8.8 %collective-permute-start.2 = (bf16[512,256]{1,0:T(8,128)(2,1)}, bf16[512,256]{1,0:T(8,128)(2,1)S(1)}, u32[]{:S(2)}, u32[]{:S(2)}) collective-permute-start(bf16[512,256]{1,0:T(8,128)(2,1)} %refs_1_), channel_id=1, source_target_pairs={{0,2},{1,3},{2,0},{3,1},{4,6},{5,7},{6,4},{7,5},{8,10},{9,11},{10,... | collective-permute-start | bytes 786440 | tf_op jit(solution)/shard_map/ppermute | solution.py:42
  6.6 7.5 %copy-start = (bf16[512,256]{1,0:T(8,128)(2,1)S(1)}, bf16[512,256]{1,0:T(8,128)(2,1)}, u32[]{:S(2)}) copy-start(bf16[512,256]{1,0:T(8,128)(2,1)} %refs_1_) | copy-start | bytes 786436
  6.6 7.4 %collective-permute-start.3 = (bf16[512,256]{1,0:T(8,128)(2,1)S(1)}, bf16[512,256]{1,0:T(8,128)(2,1)S(1)}, u32[]{:S(2)}, u32[]{:S(2)}) collective-permute-start(bf16[512,256]{1,0:T(8,128)(2,1)S(1)} %get-tuple-element.61), channel_id=1, source_target_pairs={{0,4},{8,12},{16,20},{24,28},{4,0},{12,8},{20,16},{28,24},{1,5},{9... | collective-permute-start | bytes 786440 | tf_op jit(solution)/shard_map/ppermute | solution.py:46
  8.7 4.4 %collective-permute-start.1 = (bf16[32,256]{1,0:T(8,128)(2,1)S(1)}, bf16[32,256]{1,0:T(8,128)(2,1)S(1)}, u32[]{:S(2)}, u32[]{:S(2)}) collective-permute-start(bf16[32,256]{1,0:T(8,128)(2,1)S(1)} %get-tuple-element.94.panel_ref), channel_id=1, source_target_pairs={{0,8},{4,12},{8,0},{12,4},{16,24},{20,28},{24,16},{28,20},{1,9},{5... | collective-permute-start | bytes 49160 | tf_op jit(solution)/shard_map/ppermute | solution.py:42
  10.3 4.7 %collective-permute-start.5 = (bf16[32,256]{1,0:T(8,128)(2,1)S(1)}, bf16[32,256]{1,0:T(8,128)(2,1)S(1)}, u32[]{:S(2)}, u32[]{:S(2)}) collective-permute-start(bf16[32,256]{1,0:T(8,128)(2,1)S(1)} %get-tuple-element.94.panel_ref), channel_id=1, source_target_pairs={{0,16},{4,20},{8,24},{12,28},{16,0},{20,4},{24,8},{28,12},{1,17},{... | collective-permute-start | bytes 49160 | tf_op jit(solution)/shard_map/ppermute | solution.py:42
  12.9 5.8 %collective-permute-start.6 = (bf16[32,256]{1,0:T(8,128)(2,1)S(1)}, bf16[32,256]{1,0:T(8,128)(2,1)S(1)}, u32[]{:S(2)}, u32[]{:S(2)}) collective-permute-start(bf16[32,256]{1,0:T(8,128)(2,1)S(1)} %get-tuple-element.94.panel_ref), channel_id=1, source_target_pairs={{0,24},{4,28},{8,16},{12,20},{16,8},{20,12},{24,0},{28,4},{1,25},{... | collective-permute-start | bytes 49160 | tf_op jit(solution)/shard_map/ppermute | solution.py:42
  13.1 6.1 %collective-permute-start.4 = (bf16[512,256]{1,0:T(8,128)(2,1)S(1)}, bf16[512,256]{1,0:T(8,128)(2,1)S(1)}, u32[]{:S(2)}, u32[]{:S(2)}) collective-permute-start(bf16[512,256]{1,0:T(8,128)(2,1)S(1)} %get-tuple-element.63), channel_id=1, source_target_pairs={{4,8},{12,16},{20,24},{8,4},{16,12},{24,20},{5,9},{13,17},{21,25},... | collective-permute-start | bytes 786440 | tf_op jit(solution)/shard_map/ppermute | solution.py:46
  14.1 4.6 %collective-permute-start.7 = (bf16[512,256]{1,0:T(8,128)(2,1)S(1)}, bf16[512,256]{1,0:T(8,128)(2,1)S(1)}, u32[]{:S(2)}, u32[]{:S(2)}) collective-permute-start(bf16[512,256]{1,0:T(8,128)(2,1)S(1)} %copy-done), channel_id=1, source_target_pairs={{0,1},{1,0},{2,3},{3,2},{4,5},{5,4},{6,7},{7,6},{8,9},{9,8},{10,11... | collective-permute-start | bytes 786440 | tf_op jit(solution)/shard_map/ppermute | solution.py:42
  14.1 4.6 %collective-permute-start.8 = (bf16[512,256]{1,0:T(8,128)(2,1)S(1)}, bf16[512,256]{1,0:T(8,128)(2,1)S(1)}, u32[]{:S(2)}, u32[]{:S(2)}) collective-permute-start(bf16[512,256]{1,0:T(8,128)(2,1)S(1)} %collective-permute-done.2.refs_2_.refs_12_), channel_id=1, source_target_pairs={{0,1},{1,0},{2,3},{3,2},{4,5},{5,4},{6,7},{7,6},{8,9},{9,8},{10,11... | collective-permute-start | bytes 786440 | tf_op jit(solution)/shard_map/ppermute | solution.py:42
  25.9 8.9 %collective-permute-start.11 = (bf16[160,1024]{1,0:T(8,128)(2,1)S(1)}, bf16[160,1024]{1,0:T(8,128)(2,1)S(1)}, u32[]{:S(2)}, u32[]{:S(2)}) collective-permute-start(bf16[160,1024]{1,0:T(8,128)(2,1)S(1)} %get-tuple-element.76), channel_id=1, source_target_pairs={{0,4},{4,0},{8,12},{12,8},{16,20},{20,16},{24,28},{28,24},{1,5},{5... | collective-permute-start | bytes 983048 | tf_op jit(solution)/shard_map/ppermute | solution.py:42
  35.0 5.6 %collective-permute-start.13 = (bf16[80,1024]{1,0:T(8,128)(2,1)S(1)}, bf16[80,1024]{1,0:T(8,128)(2,1)S(1)}, u32[]{:S(2)}, u32[]{:S(2)}) collective-permute-start(bf16[80,1024]{1,0:T(8,128)(2,1)S(1)} %slice.59), channel_id=1, source_target_pairs={{0,8},{4,12},{8,0},{12,4},{16,24},{20,28},{24,16},{28,20},{1,9},{5... | collective-permute-start | bytes 491528 | tf_op jit(solution)/shard_map/ppermute | solution.py:42
  37.3 7.9 %collective-permute-start.9 = (bf16[1024,256]{1,0:T(8,128)(2,1)S(1)}, bf16[1024,256]{1,0:T(8,128)(2,1)S(1)}, u32[]{:S(2)}, u32[]{:S(2)}) collective-permute-start(bf16[1024,256]{1,0:T(8,128)(2,1)S(1)} %get-tuple-element.70), channel_id=1, source_target_pairs={{0,1},{1,0},{2,3},{3,2},{4,5},{5,4},{6,7},{7,6},{8,9},{9,8},{10,11... | collective-permute-start | bytes 1572872 | tf_op jit(solution)/shard_map/ppermute | solution.py:42
  37.3 19.2 %collective-permute-start.12 = (bf16[512,256]{1,0:T(8,128)(2,1)S(1)}, bf16[512,256]{1,0:T(8,128)(2,1)S(1)}, u32[]{:S(2)}, u32[]{:S(2)}) collective-permute-start(bf16[512,256]{1,0:T(8,128)(2,1)S(1)} %get-tuple-element.81), channel_id=1, source_target_pairs={{0,4},{8,12},{16,20},{24,28},{4,0},{12,8},{20,16},{28,24},{1,5},{9... | collective-permute-start | bytes 786440 | tf_op jit(solution)/shard_map/ppermute | solution.py:46
  40.7 10.7 %collective-permute-start.15 = (bf16[80,1024]{1,0:T(8,128)(2,1)S(1)}, bf16[80,1024]{1,0:T(8,128)(2,1)S(1)}, u32[]{:S(2)}, u32[]{:S(2)}) collective-permute-start(bf16[80,1024]{1,0:T(8,128)(2,1)S(1)} %get-tuple-element.91.after_ref), channel_id=1, source_target_pairs={{0,16},{4,20},{8,24},{12,28},{16,0},{20,4},{24,8},{28,12},{1,17},{... | collective-permute-start | bytes 491528 | tf_op jit(solution)/shard_map/ppermute | solution.py:42
  44.6 12.0 %collective-permute-start.14 = (bf16[512,256]{1,0:T(8,128)(2,1)S(1)}, bf16[512,256]{1,0:T(8,128)(2,1)S(1)}, u32[]{:S(2)}, u32[]{:S(2)}) collective-permute-start(bf16[512,256]{1,0:T(8,128)(2,1)S(1)} %shard_map.159), channel_id=1, source_target_pairs={{4,8},{12,16},{20,24},{8,4},{16,12},{24,20},{5,9},{13,17},{21,25},... | collective-permute-start | bytes 786440 | tf_op jit(solution)/shard_map/ppermute | solution.py:46
  45.5 12.6 %collective-permute-start.10 = (bf16[512,256]{1,0:T(8,128)(2,1)S(1)}, bf16[512,256]{1,0:T(8,128)(2,1)S(1)}, u32[]{:S(2)}, u32[]{:S(2)}) collective-permute-start(bf16[512,256]{1,0:T(8,128)(2,1)S(1)} %slice.58), channel_id=1, source_target_pairs={{0,2},{1,3},{2,0},{3,1},{4,6},{5,7},{6,4},{7,5},{8,10},{9,11},{10,... | collective-permute-start | bytes 786440 | tf_op jit(solution)/shard_map/ppermute | solution.py:42
  51.4 5.1 %collective-permute-start.16 = (bf16[64,1024]{1,0:T(8,128)(2,1)S(1)}, bf16[64,1024]{1,0:T(8,128)(2,1)S(1)}, u32[]{:S(2)}, u32[]{:S(2)}) collective-permute-start(bf16[64,1024]{1,0:T(8,128)(2,1)S(1)} %fusion.1.refs_0_), channel_id=1, source_target_pairs={{0,8},{4,12},{8,0},{12,4},{16,24},{20,28},{24,16},{28,20},{1,9},{5... | collective-permute-start | bytes 393224 | tf_op jit(solution)/shard_map/ppermute | solution.py:42
  52.1 6.8 %collective-permute-start.17 = (bf16[64,1024]{1,0:T(8,128)(2,1)S(1)}, bf16[64,1024]{1,0:T(8,128)(2,1)S(1)}, u32[]{:S(2)}, u32[]{:S(2)}) collective-permute-start(bf16[64,1024]{1,0:T(8,128)(2,1)S(1)} %fusion.1.refs_0_), channel_id=1, source_target_pairs={{0,4},{4,0},{8,12},{12,8},{16,20},{20,16},{24,28},{28,24},{1,5},{5... | collective-permute-start | bytes 393224 | tf_op jit(solution)/shard_map/ppermute | solution.py:42
  56.5 5.0 %collective-permute-start.18 = (bf16[64,1024]{1,0:T(8,128)(2,1)S(1)}, bf16[64,1024]{1,0:T(8,128)(2,1)S(1)}, u32[]{:S(2)}, u32[]{:S(2)}) collective-permute-start(bf16[64,1024]{1,0:T(8,128)(2,1)S(1)} %collective-permute-done.16.refs_1_), channel_id=1, source_target_pairs={{0,4},{4,0},{8,12},{12,8},{16,20},{20,16},{24,28},{28,24},{1,5},{5... | collective-permute-start | bytes 393224 | tf_op jit(solution)/shard_map/ppermute | solution.py:42

commit v4 on v3

--- a/solution.py
+++ b/solution.py
@@ -74,13 +74,6 @@
     return cells
 
 
-def reversed_bits(index, levels):
-    out = 0
-    for level in range(levels):
-        out = out * 2 + ((index >> level) & 1)
-    return out
-
-
 def call(body, outs, specs, out_specs=None, scratch=(), flops=0, bytes_accessed=0):
     return pl.pallas_call(
         body,
@@ -88,7 +81,7 @@
         in_specs=list(specs),
         out_specs=[VMEM] * len(outs) if out_specs is None else list(out_specs),
         scratch_shapes=list(scratch),
-        compiler_params=pltpu.CompilerParams(vmem_limit_bytes=48 * 1024 * 1024),
+        compiler_params=pltpu.CompilerParams(vmem_limit_bytes=24 * 1024 * 1024),
         cost_estimate=pl.CostEstimate(
             flops=flops, bytes_accessed=bytes_accessed, transcendentals=0
         ),
@@ -219,10 +212,12 @@
     (nbr_hbm, mask_ref, q_ref, k_ref, v_ref, near_ref, far_ref, panel_ref, w_ref, go_ref) = refs[
         :10
     ]
-    outs = len(refs) - 13
+    outs = len(refs) - 12 - (1 << levels)
     pieces = refs[10:outs]
-    (attn_ref, p_hbm, mix_keep, mix_send, gw_keep, gw_send) = refs[outs : outs + 6]
-    (nbr_ref, ext_k, ext_v, gw_all, p_ref, nbr_sem, p_sems) = refs[outs + 6 :]
+    (e_ref, q_all, g_all, d_all, ext_k, ext_v) = refs[outs : outs + 6]
+    (mix_keep, mix_send) = refs[outs + 6 : outs + 8]
+    segments = refs[outs + 8 : outs + 8 + (1 << levels)]
+    (nbr_ref, attn_ref, gw_all, nbr_sem) = refs[outs + 8 + (1 << levels) :]
     tok, width = q_ref.shape
     blocks = tok // BLK
     fetch = pltpu.make_async_copy(nbr_hbm, nbr_ref, nbr_sem)
@@ -242,11 +237,11 @@
     coarse_k = jnp.zeros((coarse, width), F32)
     coarse_v = jnp.zeros((coarse, width), F32)
     fetch.wait()
-    stores = []
     for b in range(blocks):
         span = slice(b * BLK, (b + 1) * BLK)
         starts = picks(nbr_ref, b, blocks)
         q_tall = stacked(q_ref[span], masks)
+        q_all[b] = q_tall
         scores = mm_t(q_tall, gathered(ext_k, starts, panel_k)) * (SCALE * LOG2E)
         fine = scores[:, : NBR * BLK]
         lo = jnp.where(allowed[b : b + 1] > 0.5, scores[:, NBR * BLK :], -jnp.inf)
@@ -257,108 +252,90 @@
         lo = jnp.exp2(lo - top)
         total = jnp.sum(fine, axis=1, keepdims=True) + jnp.sum(lo, axis=1, keepdims=True)
         scale = 1.0 / total
-        coarse_w = (lo * scale).astype(BF)
-        weights = jnp.concatenate([(fine * scale).astype(BF), coarse_w], 1)
-        p_ref[b] = weights
-        store = pltpu.make_async_copy(p_ref.at[b], p_hbm.at[b], p_sems.at[b])
-        store.start()
-        stores.append(store)
-        attn = unstacked(mm(weights, gathered(ext_v, starts, panel_v)), masks).astype(BF)
+        coarse_e = lo.astype(BF)
+        weights = jnp.concatenate([fine.astype(BF), coarse_e], 1)
+        e_ref[b] = weights
+        out = mm(weights, gathered(ext_v, starts, panel_v)) * scale
+        attn = unstacked(out, masks).astype(BF)
         attn_ref[span] = attn
-        g_tall = stacked(go_ref[span], masks)
-        dterm = row_terms(g_tall, attn, heads)
-        coarse_ds = coarse_w.astype(F32) * (mm_t(g_tall, panel_v) - dterm)
-        coarse_k = coarse_k + t_mm(coarse_ds.astype(BF), q_tall)
-        coarse_v = coarse_v + t_mm(coarse_w, g_tall)
-    coarse_k = coarse_k * SCALE
+        g_tall = stacked(go_ref[span], masks).astype(F32) * scale
+        dterm = jnp.sum(
+            g_tall * jnp.concatenate([attn.astype(F32)] * heads, 0), axis=1, keepdims=True
+        )
+        g_tall = g_tall.astype(BF)
+        g_all[b] = g_tall
+        d_all[b] = dterm
+    tall_g = g_all[...].reshape(blocks * heads * BLK, width)
+    tall_q = q_all[...].reshape(blocks * heads * BLK, width)
+    tall_d = d_all[...].reshape(blocks * heads * BLK, 1)
+    tall_e = e_ref[:, :, NBR * BLK :].reshape(blocks * heads * BLK, coarse)
+    coarse_ds = tall_e.astype(F32) * (mm_t(tall_g, panel_v) - tall_d)
+    coarse_k = SCALE * t_mm(coarse_ds.astype(BF), tall_q)
+    coarse_v = t_mm(tall_e, tall_g)
     attn = attn_ref[...]
-    for j, piece in enumerate(pieces):
-        lanes = pl.ds(pl.multiple_of((me_head ^ j) * width, width), width)
-        part = mm(attn, w_ref[:, lanes]).astype(BF)
-        target = mix_send if j & 1 else mix_keep
-        target[(j >> 1) * tok : ((j >> 1) + 1) * tok] = part
     chunk = width >> levels
-    mine = reversed_bits(me, levels)
+    mine = me & ((1 << levels) - 1)
     for j, piece in enumerate(pieces):
         part = t_mm(attn, piece[...]).astype(BF)
         lanes = pl.ds(pl.multiple_of((me_head ^ j) * width, width), width)
         for c in range(1 << levels):
             place = pl.ds(pl.multiple_of((c ^ mine) * chunk, chunk), chunk)
             gw_all[place, lanes] = part[c * chunk : (c + 1) * chunk]
-    segment = gw_keep.shape[0] * 2 >> levels
+    for j, piece in enumerate(pieces):
+        lanes = pl.ds(pl.multiple_of((me_head ^ j) * width, width), width)
+        part = mm(attn, w_ref[:, lanes]).astype(BF)
+        target = mix_send if j & 1 else mix_keep
+        target[(j >> 1) * tok : ((j >> 1) + 1) * tok] = part
     across = gw_all.shape[1] // width
-    if (coarse // rows) >> levels < across:
-        for target in (gw_keep, gw_send):
-            target[...] = jnp.zeros_like(target)
-    for s in range(1 << levels):
-        target = gw_keep if s < (1 << levels) // 2 else gw_send
-        base = (s % ((1 << levels) // 2)) * segment
-        target[base : base + chunk] = gw_all[s * chunk : (s + 1) * chunk]
+    for m, target in enumerate(segments):
+        target[:chunk] = gw_all[m * chunk : (m + 1) * chunk]
+        if (coarse // rows) >> levels < across:
+            target[chunk:] = jnp.zeros_like(target[chunk:])
     for j in range(coarse // rows):
-        s = reversed_bits(j, levels)
         t = j >> levels
-        target = gw_keep if s < (1 << levels) // 2 else gw_send
-        base = (s % ((1 << levels) // 2)) * segment + chunk + (t // across) * 2 * rows
+        base = chunk + (t // across) * 2 * rows
         lanes = slice((t % across) * width, (t % across + 1) * width)
         both = [coarse_k[j * rows : (j + 1) * rows], coarse_v[j * rows : (j + 1) * rows]]
+        target = segments[j & ((1 << levels) - 1)]
         target[base : base + 2 * rows, lanes] = jnp.concatenate(both, 0).astype(BF)
-    for store in stores:
-        store.wait()
-
-
-def row_terms(g_tall, attn, heads):
-    tall = jnp.concatenate([attn.astype(F32)] * heads, 0)
-    return jnp.sum(g_tall.astype(F32) * tall, axis=1, keepdims=True)
 
 
 def backward_kernel(rows, *refs):
-    (nbr_hbm, q_ref, k_ref, v_ref, near_ref, far_ref, panel_ref, go_ref, attn_ref, p_hbm) = refs[
-        :10
-    ]
-    (dq_ref, own_ref, to_near, to_far) = refs[10:14]
-    (nbr_ref, ext_k, ext_v, sum_k, sum_v, p_ref, nbr_sem, p_sems) = refs[14:]
-    tok, width = q_ref.shape
+    (nbr_hbm, panel_ref, e_ref, q_all, g_all, d_all, ext_k, ext_v) = refs[:8]
+    (dq_ref, own_ref, to_near, to_far) = refs[8:12]
+    (nbr_ref, sum_k, sum_v, nbr_sem) = refs[12:]
+    tok, width = dq_ref.shape
     blocks = tok // BLK
     fetch = pltpu.make_async_copy(nbr_hbm, nbr_ref, nbr_sem)
     fetch.start()
-    loads = [
-        pltpu.make_async_copy(p_hbm.at[b], p_ref.at[b], p_sems.at[b]) for b in range(blocks)
-    ]
-    for load in loads:
-        load.start()
     odd = lax.axis_index("pix") & 1
-    extend(ext_k, ext_v, k_ref, v_ref, near_ref, far_ref)
     panel_k, panel_v = panel_parts(panel_ref, rows)
     masks = head_masks(width, BLK)
     sum_k[...] = jnp.zeros_like(sum_k)
     sum_v[...] = jnp.zeros_like(sum_v)
-    heads = len(masks)
     fetch.wait()
     for b in range(blocks):
         span = slice(b * BLK, (b + 1) * BLK)
         starts = picks(nbr_ref, b, blocks)
-        q_tall = stacked(q_ref[span], masks)
-        g_tall = stacked(go_ref[span], masks)
-        dterm = row_terms(g_tall, attn_ref[span], heads)
+        g_tall = g_all[b]
+        weights = e_ref[b]
+        dv = t_mm(weights[:, : NBR * BLK], g_tall)
         slope = mm_t(g_tall, gathered(ext_v, starts, panel_v))
-        loads[b].wait()
-        weights = p_ref[b]
-        ds = (weights.astype(F32) * (slope - dterm)).astype(BF)
+        ds = (weights.astype(F32) * (slope - d_all[b])).astype(BF)
         dq = unstacked(mm(ds, gathered(ext_k, starts, panel_k)), masks)
         dq_ref[span] = (SCALE * dq).astype(BF)
-        dk = SCALE * t_mm(ds[:, : NBR * BLK], q_tall)
-        dv = t_mm(weights[:, : NBR * BLK], g_tall)
+        dk = t_mm(ds[:, : NBR * BLK], q_all[b])
         for n in range(NBR):
             place = pl.ds(starts[n], BLK)
             sum_k[place, :] += dk[n * BLK : (n + 1) * BLK]
             sum_v[place, :] += dv[n * BLK : (n + 1) * BLK]
-    own_ref[0:tok] = sum_k[RIM : RIM + tok]
+    own_ref[0:tok] = SCALE * sum_k[RIM : RIM + tok]
     own_ref[tok:] = sum_v[RIM : RIM + tok]
     near = pl.ds(pl.multiple_of((1 - odd) * (tok + RIM), RIM), RIM)
     far = pl.ds(pl.multiple_of(odd * (tok + RIM), RIM), RIM)
-    to_near[0:RIM] = sum_k[near, :].astype(BF)
+    to_near[0:RIM] = (SCALE * sum_k[near, :]).astype(BF)
     to_near[RIM:] = sum_v[near, :].astype(BF)
-    to_far[0:RIM] = sum_k[far, :]
+    to_far[0:RIM] = SCALE * sum_k[far, :]
     to_far[RIM:] = sum_v[far, :]
 
 
@@ -396,10 +373,66 @@
     out_ref = refs[-1]
     me = lax.axis_index("pix")
     chunk = out_ref.shape[0] >> levels
-    mine = reversed_bits(me, levels)
+    mine = me & ((1 << levels) - 1)
     for slot, ref in enumerate(refs[:-1]):
         place = pl.ds(pl.multiple_of((slot ^ mine) * chunk, chunk), chunk)
         out_ref[place, :] = ref[...].astype(F32) * factor
+
+
+def run_forward(rows, coarse, levels, segment, args, pieces):
+    tok, width = args[2].shape
+    d_model = args[8].shape[1]
+    head = len(pieces)
+    blocks = tok // BLK
+    keys_each = NBR * BLK + coarse
+    tall = width // HDIM * BLK
+    kept = [
+        ((blocks, tall, keys_each), BF),
+        ((blocks, tall, width), BF),
+        ((blocks, tall, width), BF),
+        ((blocks, tall, 1), F32),
+        ((tok + 2 * RIM, width), BF),
+        ((tok + 2 * RIM, width), BF),
+    ]
+    outs = call(
+        functools.partial(forward_kernel, rows, levels),
+        kept
+        + [((head // 2 * tok, width), BF)] * 2
+        + [((segment, d_model), BF)] * (1 << levels),
+        [HBM] + [VMEM] * (9 + head),
+        scratch=[
+            pltpu.SMEM(args[0].shape, jnp.int32),
+            pltpu.VMEM((tok, width), BF),
+            pltpu.VMEM((width, d_model), BF),
+            pltpu.SemaphoreType.DMA,
+        ],
+        flops=4 * blocks * tall * keys_each * width + 4 * tok * width * d_model,
+        bytes_accessed=10_000_000,
+    )(*args, *pieces)
+    return outs[: len(kept)], outs[len(kept) :]
+
+
+def run_backward(rows, neighbors, panel, saved):
+    blocks, tall, width = saved[1].shape
+    tok = blocks * BLK
+    return call(
+        functools.partial(backward_kernel, rows),
+        [
+            ((tok, width), BF),
+            ((2 * tok, width), F32),
+            ((2 * RIM, width), BF),
+            ((2 * RIM, width), F32),
+        ],
+        [HBM] + [VMEM] * 7,
+        scratch=[
+            pltpu.SMEM(neighbors.shape, jnp.int32),
+            pltpu.VMEM((tok + 2 * RIM, width), F32),
+            pltpu.VMEM((tok + 2 * RIM, width), F32),
+            pltpu.SemaphoreType.DMA,
+        ],
+        flops=8 * blocks * tall * saved[0].shape[2] * width,
+        bytes_accessed=10_000_000,
+    )(neighbors, panel, *saved)
 
 
 def on_device(
@@ -424,7 +457,6 @@
     bits = bit_list(pix)
     head_bits = bit_list(head)
     levels = min(2, len(bits))
-    heads = width // HDIM
     pool_row = pool_map.reshape(1, tok)
     q_in, gm_in, w_in, mask_in = queries, grad_mixed, w_out, coarse_mask
     keys_hbm, values_hbm, ck_hbm, cv_hbm, pool_hbm, nbr_hbm = [
@@ -490,6 +522,7 @@
     index = [0]
     for bit in reversed(head_bits):
         if len(order) > 1:
+            order[0] = gm_own
             *order, near = lax.optimization_barrier((*order, near))
         order = order + [swap(piece, "head", bit) for piece in order]
         index = index + [i ^ bit for i in index]
@@ -502,69 +535,21 @@
         bytes_accessed=0,
     )(w_own, gm_own, *grads)
 
-    keys_each = NBR * BLK + coarse
-    tall = heads * BLK
-    product = 2 * tall * keys_each * width
-    attn, weights, mix_keep, mix_send, gw_keep, gw_send = call(
-        functools.partial(forward_kernel, rows, levels),
-        [
-            ((tok, width), BF),
-            ((blocks, tall, keys_each), BF),
-            ((head // 2 * tok, width), BF),
-            ((head // 2 * tok, width), BF),
-            ((slots // 2 * segment, d_model), BF),
-            ((slots // 2 * segment, d_model), BF),
-        ],
-        [HBM] + [VMEM] * (9 + head),
-        out_specs=[VMEM, HBM] + [VMEM] * 4,
-        scratch=[
-            pltpu.SMEM(neighbors.shape, jnp.int32),
-            pltpu.VMEM((tok + 2 * RIM, width), BF),
-            pltpu.VMEM((tok + 2 * RIM, width), BF),
-            pltpu.VMEM((width, d_model), BF),
-            pltpu.VMEM((blocks, tall, keys_each), BF),
-            pltpu.SemaphoreType.DMA,
-            pltpu.SemaphoreType.DMA((blocks,)),
-        ],
-        flops=2 * blocks * product + 4 * tok * width * d_model,
-        bytes_accessed=10_000_000,
-    )(
-        nbr_hbm, mask_own, q_own, k_own, v_own, near, far, panel, w_own, grad_attn, gm_own, *grads
+    saved, (mix_keep, mix_send, *segments) = run_forward(
+        rows,
+        coarse,
+        levels,
+        segment,
+        (nbr_hbm, mask_own, q_own, k_own, v_own, near, far, panel, w_own, grad_attn),
+        (gm_own, *grads),
     )
-
-    grad_queries, own, to_near, to_far = call(
-        functools.partial(backward_kernel, rows),
-        [
-            ((tok, width), BF),
-            ((2 * tok, width), F32),
-            ((2 * RIM, width), BF),
-            ((2 * RIM, width), F32),
-        ],
-        [HBM] + [VMEM] * 8 + [HBM],
-        scratch=[
-            pltpu.SMEM(neighbors.shape, jnp.int32),
-            pltpu.VMEM((tok + 2 * RIM, width), BF),
-            pltpu.VMEM((tok + 2 * RIM, width), BF),
-            pltpu.VMEM((tok + 2 * RIM, width), F32),
-            pltpu.VMEM((tok + 2 * RIM, width), F32),
-            pltpu.VMEM((blocks, tall, keys_each), BF),
-            pltpu.SemaphoreType.DMA,
-            pltpu.SemaphoreType.DMA((blocks,)),
-        ],
-        flops=4 * blocks * product,
-        bytes_accessed=10_000_000,
-    )(nbr_hbm, q_own, k_own, v_own, near, far, panel, grad_attn, attn, pltpu.with_memory_space_constraint(weights, pltpu.HBM))
-
-    kept, sent = gw_keep, gw_send
-    for level in range(levels):
-        got = swap(sent, "pix", bits[level])
-        if level == 0:
-            got, to_near, to_far = lax.optimization_barrier((got, to_near, to_far))
-        total = kept.astype(F32) + got.astype(F32)
-        half = total.shape[0] // 2
-        if level + 1 < levels:
-            kept, sent = total[:half], total[half:].astype(BF)
-            sent, to_near = lax.optimization_barrier((sent, to_near))
+    grad_queries, own, to_near, to_far = run_backward(rows, nbr_hbm, panel, saved)
+
+    got = [swap(segments[m], "pix", m) for m in range(1, slots)]
+    *got, to_near = lax.optimization_barrier((*got, to_near))
+    total = segments[0].astype(F32)
+    for piece in got:
+        total = total + piece.astype(F32)
     whole = total
     sent = lax.optimization_barrier(whole.astype(BF))
     (to_far,) = call(
@@ -590,13 +575,8 @@
             sent = jnp.concatenate([part] + lines, 0).astype(BF)
     coarse_grads = cells[0]
     part = part.astype(BF)
-    gathered_parts = [part]
-    for bit in reversed(bits[:levels]):
-        gathered_parts = gathered_parts + [swap(p, "pix", bit) for p in gathered_parts]
-        if len(gathered_parts) == 2:
-            gathered_parts[1], coarse_grads = lax.optimization_barrier(
-                (gathered_parts[1], coarse_grads)
-            )
+    part, coarse_grads = lax.optimization_barrier((part, coarse_grads))
+    gathered_parts = [part] + [swap(part, "pix", m) for m in range(1, slots)]
     (grad_w_out,) = call(
         functools.partial(gw_kernel, levels, (tok * pix) ** (-0.5)),
         [((width, d_model), F32)],

time: 62.7 us -> 59.5 us (0.949)
  waiting for transfers between devices: 17 us -> 14.1 us
  Pallas kernels: 17.7 us -> 15.4 us
  starting transfers between devices: 25.9 us -> 27.9 us
    ppermute x15 -> x16, waiting for transfers between devices: 16.7 us -> 14.1 us  [swap(): lax.ppermute(value, axis, [(i, i ^ bit) for i in range(lax.axis_size(axis...]
    pallas_call x2, Pallas kernels: 12.1 us -> 9.73 us  [the longest x1 4.99 us: run_forward(): call(functools.partial(forward_kernel, rows, levels), kept + [((head // 2...]
    ppermute x15 -> x16, starting transfers between devices: 21.6 us -> 23.5 us  [swap(): lax.ppermute(value, axis, [(i, i ^ bit) for i in range(lax.axis_size(axis...]
  transfers between devices with their start and end apart: 19 -> 20, of which waited for: 8 -> 6; matrix products, arithmetic and copies ran while one was open for 2% -> 1% of each run, Pallas kernels for 14% -> 15%
where the time goes in v4:
time: 59.5 us; the launch traced here: 59.3 us
  starting transfers between devices  27.9 us (47%)
  Pallas kernels  15.4 us (26%)
  waiting for transfers between devices  14.1 us (24%)
  other arithmetic  1.04 us (2%)
  between operations  0.82 us (1%)
    ppermute x16, starting transfers between devices, swap(): lax.ppermute(value, axis, [(i, i ^ bit) for i in range(lax.axis_size(axis...  23.5 us
    ppermute x16, waiting for transfers between devices, swap(): lax.ppermute(value, axis, [(i, i ^ bit) for i in range(lax.axis_size(axis...  14.1 us
    pallas_call x1, Pallas kernels, run_forward(): call(functools.partial(forward_kernel, rows, levels), kept + [((head // 2...  4.99 us
    pallas_call x1, Pallas kernels, run_backward(): call(functools.partial(backward_kernel, rows), [((tok, width), BF), ((2 *...  4.74 us
    ppermute x4, starting transfers between devices, exchange(): return lax.ppermute(value, 'pix', pairs + [(b, a) for a, b in pairs])  4.46 us
    pallas_call x1, Pallas kernels, on_device(): call(finish_kernel, [((tok, width), BF), ((tok, width), BF), ((rows, widt...  1.52 us
    pallas_call x1, Pallas kernels, on_device(): call(prep_kernel, [((tok, width), BF), ((tok, width), BF), ((2 * rows, wi...  1.28 us
    pallas_call x1, Pallas kernels, on_device(): call(load_kernel, [((tok, width), BF), ((tok, width), BF), ((width, d_mod...  1.24 us
  transfers between devices with their start and end apart: 20, of which 6 were waited for; matrix products, arithmetic and copies ran while one was open for 1% of the time, Pallas kernels for 15%

profile of v4, /device:TPU:0, one launch (start us, length us, event | category | flops | bytes accessed | tf_op | source)
XLA Modules:
  0.0 59.3 jit_solution(1659562438449809828)
XLA Ops:
  0.6 1.3 %shard_map.153 = (bf16[512,256]{1,0:T(8,128)(2,1)S(1)}, bf16[512,256]{1,0:T(8,128)(2,1)S(1)}, bf16[16,256]{1,0:T(8,128)(2,1)S(1)}, s32[1,512]{1,0:T(1,128)S(1)}) custom-call(bf16[512,256]{1,0:T(8,128)(2,1)} %k_hbm.1, bf16[512,256]{1,0:T(8,128)(2,1)} %v_hbm.1, bf16[8,256]{1,0:T(8,128)(2,1)} %ck_hbm.1, bf16[8,256]{1,0:T(8,128)(2,1)} %cv_hbm.1, s32[1,512]{1,0:T(1,128)} %bitcast.1), custom_call_target="tpu_custom_call" | custom-call | tf_op jit(solution)/shard_map/pallas_call | solution.py:479
  1.9 3.0 %collective-permute-start = (bf16[16,256]{1,0:T(8,128)(2,1)S(1)}, bf16[16,256]{1,0:T(8,128)(2,1)S(1)}, u32[]{:S(2)}, u32[]{:S(2)}) collective-permute-start(bf16[16,256]{1,0:T(8,128)(2,1)S(1)} %get-tuple-element.55), channel_id=1, source_target_pairs={{0,4},{4,0},{8,12},{12,8},{16,20},{20,16},{24,28},{28,24},{1,5},{5... | collective-permute-start | bytes 24584 | tf_op jit(solution)/shard_map/ppermute | solution.py:42
  5.0 1.5 %collective-permute-start.2 = (bf16[512,256]{1,0:T(8,128)(2,1)}, bf16[512,256]{1,0:T(8,128)(2,1)S(1)}, u32[]{:S(2)}, u32[]{:S(2)}) collective-permute-start(bf16[512,256]{1,0:T(8,128)(2,1)} %refs_1_), channel_id=1, source_target_pairs={{0,2},{1,3},{2,0},{3,1},{4,6},{5,7},{6,4},{7,5},{8,10},{9,11},{10,... | collective-permute-start | bytes 786440 | tf_op jit(solution)/shard_map/ppermute | solution.py:42
  6.4 0.1 collective-permute-done
  6.6 2.1 %collective-permute-start.3 = (bf16[512,256]{1,0:T(8,128)(2,1)S(1)}, bf16[512,256]{1,0:T(8,128)(2,1)S(1)}, u32[]{:S(2)}, u32[]{:S(2)}) collective-permute-start(bf16[512,256]{1,0:T(8,128)(2,1)S(1)} %get-tuple-element.67), channel_id=1, source_target_pairs={{0,4},{8,12},{16,20},{24,28},{4,0},{12,8},{20,16},{28,24},{1,5},{9... | collective-permute-start | bytes 786440 | tf_op jit(solution)/shard_map/ppermute | solution.py:46
  8.7 1.6 %collective-permute-start.1 = (bf16[32,256]{1,0:T(8,128)(2,1)S(1)}, bf16[32,256]{1,0:T(8,128)(2,1)S(1)}, u32[]{:S(2)}, u32[]{:S(2)}) collective-permute-start(bf16[32,256]{1,0:T(8,128)(2,1)S(1)} %get-tuple-element.104.panel_ref), channel_id=1, source_target_pairs={{0,8},{4,12},{8,0},{12,4},{16,24},{20,28},{24,16},{28,20},{1,9},{5... | collective-permute-start | bytes 49160 | tf_op jit(solution)/shard_map/ppermute | solution.py:42
  10.3 2.5 %collective-permute-start.6 = (bf16[32,256]{1,0:T(8,128)(2,1)S(1)}, bf16[32,256]{1,0:T(8,128)(2,1)S(1)}, u32[]{:S(2)}, u32[]{:S(2)}) collective-permute-start(bf16[32,256]{1,0:T(8,128)(2,1)S(1)} %get-tuple-element.104.panel_ref), channel_id=1, source_target_pairs={{0,24},{4,28},{8,16},{12,20},{16,8},{20,12},{24,0},{28,4},{1,25},{... | collective-permute-start | bytes 49160 | tf_op jit(solution)/shard_map/ppermute | solution.py:42
  12.8 0.1 collective-permute-start.5
  12.9 0.0 collective-permute-done.1
  12.9 0.7 %collective-permute-start.4 = (bf16[512,256]{1,0:T(8,128)(2,1)S(1)}, bf16[512,256]{1,0:T(8,128)(2,1)S(1)}, u32[]{:S(2)}, u32[]{:S(2)}) collective-permute-start(bf16[512,256]{1,0:T(8,128)(2,1)S(1)} %get-tuple-element.69), channel_id=1, source_target_pairs={{4,8},{12,16},{20,24},{8,4},{16,12},{24,20},{5,9},{13,17},{21,25},... | collective-permute-start | bytes 786440 | tf_op jit(solution)/shard_map/ppermute | solution.py:46
  13.6 1.2 %shard_map.155 = (bf16[512,256]{1,0:T(8,128)(2,1)S(1)}, bf16[512,256]{1,0:T(8,128)(2,1)S(1)}, bf16[256,1024]{1,0:T(8,128)(2,1)S(1)}, s32[4,8]{1,0:T(4,128)S(1)}) custom-call(bf16[512,256]{1,0:T(8,128)(2,1)} %refs_0_.2, bf16[512,256]{1,0:T(8,128)(2,1)} %refs_1_, bf16[256,1024]{1,0:T(8,128)(2,1)} %refs_2_, s32[4,8]{1,0:T(4,128)} %refs_3_), custom_call_target="tpu_custom_call" | custom-call | tf_op jit(solution)/shard_map/pallas_call | solution.py:508
  14.8 0.0 collective-permute-done.2.refs_2_.refs_12_
  14.8 0.0 collective-permute-done.3.refs_5_
  14.8 0.1 collective-permute-start.7
  14.9 0.5 collective-permute-start.8
  15.4 2.4 %collective-permute-done.5 = bf16[32,256]{1,0:T(8,128)(2,1)S(1)} collective-permute-done((bf16[32,256]{1,0:T(8,128)(2,1)S(1)}, bf16[32,256]{1,0:T(8,128)(2,1)S(1)}, u32[]{:S(2)}, u32[]{:S(2)}) %collective-permute-start.5) | collective-permute-done | bytes 16416 | tf_op jit(solution)/shard_map/ppermute | solution.py:42
  17.8 0.0 collective-permute-done.6
  17.8 0.0 collective-permute-done.7.refs_1_.refs_11_
  17.8 0.0 collective-permute-done.8.refs_3_.refs_13_
  17.8 0.5 shard_map.156.refs_9_
  18.3 0.0 collective-permute-done.4.refs_6_
  18.3 5.0 %shard_map.157 = (bf16[4,512,576]{2,1,0:T(8,128)(2,1)S(1)}, bf16[4,512,256]{2,1,0:T(8,128)(2,1)S(1)}, bf16[4,512,256]{2,1,0:T(8,128)(2,1)S(1)}, f32[4,512,1]{2,1...) custom-call(s32[4,4]{1,0:T(4,128)} %refs_0_.4, ...), custom_call_target="tpu_custom_call" | custom-call | flops 1744830464 | bytes 10000000 | tf_op jit(solution)/shard_map/pallas_call | solution.py:397
  23.3 4.3 %collective-permute-start.11 = (bf16[80,1024]{1,0:T(8,128)(2,1)S(1)}, bf16[80,1024]{1,0:T(8,128)(2,1)S(1)}, u32[]{:S(2)}, u32[]{:S(2)}) collective-permute-start(bf16[80,1024]{1,0:T(8,128)(2,1)S(1)} %get-tuple-element.84), channel_id=1, source_target_pairs={{0,4},{4,0},{8,12},{12,8},{16,20},{20,16},{24,28},{28,24},{1,5},{5... | collective-permute-start | bytes 491528 | tf_op jit(solution)/shard_map/ppermute | solution.py:42
  27.6 1.8 %collective-permute-start.12 = (bf16[80,1024]{1,0:T(8,128)(2,1)S(1)}, bf16[80,1024]{1,0:T(8,128)(2,1)S(1)}, u32[]{:S(2)}, u32[]{:S(2)}) collective-permute-start(bf16[80,1024]{1,0:T(8,128)(2,1)S(1)} %get-tuple-element.85), channel_id=1, source_target_pairs={{0,8},{4,12},{8,0},{12,4},{16,24},{20,28},{24,16},{28,20},{1,9},{5... | collective-permute-start | bytes 491528 | tf_op jit(solution)/shard_map/ppermute | solution.py:42
  29.4 1.0 %collective-permute-start.13 = (bf16[80,1024]{1,0:T(8,128)(2,1)S(1)}, bf16[80,1024]{1,0:T(8,128)(2,1)S(1)}, u32[]{:S(2)}, u32[]{:S(2)}) collective-permute-start(bf16[80,1024]{1,0:T(8,128)(2,1)S(1)} %get-tuple-element.86), channel_id=1, source_target_pairs={{0,12},{4,8},{8,4},{12,0},{16,28},{20,24},{24,20},{28,16},{1,13},{... | collective-permute-start | bytes 491528 | tf_op jit(solution)/shard_map/ppermute | solution.py:42
  30.3 0.0 collective-permute-start.9
  30.4 4.7 %shard_map.158 = (bf16[512,256]{1,0:T(8,128)(2,1)}, f32[1024,256]{1,0:T(8,128)S(1)}, bf16[512,256]{1,0:T(8,128)(2,1)S(1)}, f32[512,256]{1,0:T(8,128)S(1)}) custom-call(s32[4,4]{1,0:T(4,128)} %refs_0_.4, bf16[128,256]{1,0:T(8,128)(2,1)S(1)} %constant_dynamic-update-slice_fusion.2.refs_7_.refs_1_, bf16[4,512,576]{2,1,0:T(8,128)(2,1)S(1)} %get-tuple-element.76.refs_2_, ...), custom_call_target="tpu_custom_call" | custom-call | flops 2415919104 | bytes 10000000 | tf_op jit(solution)/shard_map/pallas_call | solution.py:418
  35.1 0.0 collective-permute-done.11
  35.1 0.0 collective-permute-done.12
  35.1 1.6 %collective-permute-done.13 = bf16[80,1024]{1,0:T(8,128)(2,1)S(1)} collective-permute-done((bf16[80,1024]{1,0:T(8,128)(2,1)S(1)}, bf16[80,1024]{1,0:T(8,128)(2,1)S(1)}, u32[]{:S(2)}, u32[]{:S(2)}) %collective-permute-start.13) | collective-permute-done | bytes 163872 | tf_op jit(solution)/shard_map/ppermute | solution.py:42
  36.8 1.0 %collective-permute-start.14 = (bf16[512,256]{1,0:T(8,128)(2,1)S(1)}, bf16[512,256]{1,0:T(8,128)(2,1)S(1)}, u32[]{:S(2)}, u32[]{:S(2)}) collective-permute-start(bf16[512,256]{1,0:T(8,128)(2,1)S(1)} %get-tuple-element.88), channel_id=1, source_target_pairs={{0,4},{8,12},{16,20},{24,28},{4,0},{12,8},{20,16},{28,24},{1,5},{9... | collective-permute-start | bytes 786440 | tf_op jit(solution)/shard_map/ppermute | solution.py:46
  37.8 0.1 fusion.2
  37.9 2.0 %collective-permute-start.16 = (bf16[80,1024]{1,0:T(8,128)(2,1)S(1)}, bf16[80,1024]{1,0:T(8,128)(2,1)S(1)}, u32[]{:S(2)}, u32[]{:S(2)}) collective-permute-start(bf16[80,1024]{1,0:T(8,128)(2,1)S(1)} %get-tuple-element.101.after_ref), channel_id=1, source_target_pairs={{0,16},{4,20},{8,24},{12,28},{16,0},{20,4},{24,8},{28,12},{1,17},{... | collective-permute-start | bytes 491528 | tf_op jit(solution)/shard_map/ppermute | solution.py:42
  40.0 0.7 %collective-permute-start.15 = (bf16[512,256]{1,0:T(8,128)(2,1)S(1)}, bf16[512,256]{1,0:T(8,128)(2,1)S(1)}, u32[]{:S(2)}, u32[]{:S(2)}) collective-permute-start(bf16[512,256]{1,0:T(8,128)(2,1)S(1)} %shard_map.159), channel_id=1, source_target_pairs={{4,8},{12,16},{20,24},{8,4},{16,12},{24,20},{5,9},{13,17},{21,25},... | collective-permute-start | bytes 786440 | tf_op jit(solution)/shard_map/ppermute | solution.py:46
  40.6 7.6 %collective-permute-done.16 = bf16[80,1024]{1,0:T(8,128)(2,1)S(1)} collective-permute-done((bf16[80,1024]{1,0:T(8,128)(2,1)S(1)}, bf16[80,1024]{1,0:T(8,128)(2,1)S(1)}, u32[]{:S(2)}, u32[]{:S(2)}) %collective-permute-start.16) | collective-permute-done | bytes 163872 | tf_op jit(solution)/shard_map/ppermute | solution.py:42
  48.3 0.6 %collective-permute-start.19 = (bf16[64,1024]{1,0:T(8,128)(2,1)S(1)}, bf16[64,1024]{1,0:T(8,128)(2,1)S(1)}, u32[]{:S(2)}, u32[]{:S(2)}) collective-permute-start(bf16[64,1024]{1,0:T(8,128)(2,1)S(1)} %fusion.1.refs_0_), channel_id=1, source_target_pairs={{0,12},{4,8},{8,4},{12,0},{16,28},{20,24},{24,20},{28,16},{1,13},{... | collective-permute-start | bytes 393224 | tf_op jit(solution)/shard_map/ppermute | solution.py:42
  49.0 1.2 %collective-permute-start.18 = (bf16[64,1024]{1,0:T(8,128)(2,1)S(1)}, bf16[64,1024]{1,0:T(8,128)(2,1)S(1)}, u32[]{:S(2)}, u32[]{:S(2)}) collective-permute-start(bf16[64,1024]{1,0:T(8,128)(2,1)S(1)} %fusion.1.refs_0_), channel_id=1, source_target_pairs={{0,8},{4,12},{8,0},{12,4},{16,24},{20,28},{24,16},{28,20},{1,9},{5... | collective-permute-start | bytes 393224 | tf_op jit(solution)/shard_map/ppermute | solution.py:42
  50.1 1.7 %collective-permute-start.17 = (bf16[64,1024]{1,0:T(8,128)(2,1)S(1)}, bf16[64,1024]{1,0:T(8,128)(2,1)S(1)}, u32[]{:S(2)}, u32[]{:S(2)}) collective-permute-start(bf16[64,1024]{1,0:T(8,128)(2,1)S(1)} %fusion.1.refs_0_), channel_id=1, source_target_pairs={{0,4},{4,0},{8,12},{12,8},{16,20},{20,16},{24,28},{28,24},{1,5},{5... | collective-permute-start | bytes 393224 | tf_op jit(solution)/shard_map/ppermute | solution.py:42
  51.9 0.1 convert_add_fusion
  52.0 0.0 collective-permute-done.14.near_ref
  52.1 1.5 %collective-permute-start.10 = (bf16[512,256]{1,0:T(8,128)(2,1)S(1)}, bf16[512,256]{1,0:T(8,128)(2,1)S(1)}, u32[]{:S(2)}, u32[]{:S(2)}) collective-permute-start(bf16[512,256]{1,0:T(8,128)(2,1)S(1)} %slice.45), channel_id=1, source_target_pairs={{0,2},{1,3},{2,0},{3,1},{4,6},{5,7},{6,4},{7,5},{8,10},{9,11},{10,... | collective-permute-start | bytes 786440 | tf_op jit(solution)/shard_map/ppermute | solution.py:42
  53.6 0.0 collective-permute-done.15.far_ref
  53.6 1.5 %shard_map.160 = (bf16[512,256]{1,0:T(8,128)(2,1)}, bf16[512,256]{1,0:T(8,128)(2,1)}, f32[8,256]{1,0:T(8,128)}, f32[8,256]{1,0:T(8,128)}) custom-call(f32[1024,256]{1,0:T(8,128)S(1)} %get-tuple-element.83.own_ref, bf16[512,256]{1,0:T(8,128)(2,1)S(1)} %collective-permute-done.14.near_ref, bf16[512,256]{1,0:T(8,128)(2,1)S(1)} %collective-permute-done.15.far_ref, ...), custom_call_target="tpu_custom_call" | custom-call | flops 3000000000 | bytes 2097152 | tf_op jit(solution)/shard_map/pallas_call | solution.py:598
  55.1 2.1 %collective-permute-done.18.refs_2_ = bf16[64,1024]{1,0:T(8,128)(2,1)S(1)} collective-permute-done((bf16[64,1024]{1,0:T(8,128)(2,1)S(1)}, bf16[64,1024]{1,0:T(8,128)(2,1)S(1)}, u32[]{:S(2)}, u32[]{:S(2)}) %collective-permute-start.18) | collective-permute-done | bytes 131104 | tf_op jit(solution)/shard_map/ppermute | solution.py:42
  57.3 0.0 collective-permute-done.17.refs_1_
  57.3 1.1 %shard_map.161 = f32[256,1024]{1,0:T(8,128)} custom-call(bf16[64,1024]{1,0:T(8,128)(2,1)S(1)} %fusion.1.refs_0_, bf16[64,1024]{1,0:T(8,128)(2,1)S(1)} %collective-permute-done.17.refs_1_, bf16[64,1024]{1,0:T(8,128)(2,1)S(1)} %collective-permute-done.18.refs_2_, bf16[64,1024]{1,0:T(8,128)(2,1)S(1)} %collective-permute-done.19.refs_3_), custom_call_target="tpu_custom_call" | custom-call | bytes 1572864 | tf_op jit(solution)/shard_map/pallas_call | solution.py:580
  58.3 0.2 collective-permute-done.10
  58.5 0.8 %fusion = bf16[512,256]{1,0:T(8,128)(2,1)} fusion(f32[1024,256]{1,0:T(8,128)S(1)} %convert_add_fusion, bf16[512,256]{1,0:T(8,128)(2,1)S(1)} %collective-permute-done.10), kind=kLoop, calls=%fused_computation.3 | loop fusion | flops 393216 | bytes 1048576 | tf_op jit(solution)/shard_map/convert_element_type | solution.py:594
  (13 shorter events, 0.2 us)
Async XLA Ops:
  1.9 4.7 %collective-permute-start = (bf16[16,256]{1,0:T(8,128)(2,1)S(1)}, bf16[16,256]{1,0:T(8,128)(2,1)S(1)}, u32[]{:S(2)}, u32[]{:S(2)}) collective-permute-start(bf16[16,256]{1,0:T(8,128)(2,1)S(1)} %get-tuple-element.55), channel_id=1, source_target_pairs={{0,4},{4,0},{8,12},{12,8},{16,20},{20,16},{24,28},{28,24},{1,5},{5... | collective-permute-start | bytes 24584 | tf_op jit(solution)/shard_map/ppermute | solution.py:42
  5.0 9.9 %collective-permute-start.2 = (bf16[512,256]{1,0:T(8,128)(2,1)}, bf16[512,256]{1,0:T(8,128)(2,1)S(1)}, u32[]{:S(2)}, u32[]{:S(2)}) collective-permute-start(bf16[512,256]{1,0:T(8,128)(2,1)} %refs_1_), channel_id=1, source_target_pairs={{0,2},{1,3},{2,0},{3,1},{4,6},{5,7},{6,4},{7,5},{8,10},{9,11},{10,... | collective-permute-start | bytes 786440 | tf_op jit(solution)/shard_map/ppermute | solution.py:42
  6.6 8.2 %collective-permute-start.3 = (bf16[512,256]{1,0:T(8,128)(2,1)S(1)}, bf16[512,256]{1,0:T(8,128)(2,1)S(1)}, u32[]{:S(2)}, u32[]{:S(2)}) collective-permute-start(bf16[512,256]{1,0:T(8,128)(2,1)S(1)} %get-tuple-element.67), channel_id=1, source_target_pairs={{0,4},{8,12},{16,20},{24,28},{4,0},{12,8},{20,16},{28,24},{1,5},{9... | collective-permute-start | bytes 786440 | tf_op jit(solution)/shard_map/ppermute | solution.py:46
  8.7 4.2 %collective-permute-start.1 = (bf16[32,256]{1,0:T(8,128)(2,1)S(1)}, bf16[32,256]{1,0:T(8,128)(2,1)S(1)}, u32[]{:S(2)}, u32[]{:S(2)}) collective-permute-start(bf16[32,256]{1,0:T(8,128)(2,1)S(1)} %get-tuple-element.104.panel_ref), channel_id=1, source_target_pairs={{0,8},{4,12},{8,0},{12,4},{16,24},{20,28},{24,16},{28,20},{1,9},{5... | collective-permute-start | bytes 49160 | tf_op jit(solution)/shard_map/ppermute | solution.py:42
  10.3 7.5 %collective-permute-start.6 = (bf16[32,256]{1,0:T(8,128)(2,1)S(1)}, bf16[32,256]{1,0:T(8,128)(2,1)S(1)}, u32[]{:S(2)}, u32[]{:S(2)}) collective-permute-start(bf16[32,256]{1,0:T(8,128)(2,1)S(1)} %get-tuple-element.104.panel_ref), channel_id=1, source_target_pairs={{0,24},{4,28},{8,16},{12,20},{16,8},{20,12},{24,0},{28,4},{1,25},{... | collective-permute-start | bytes 49160 | tf_op jit(solution)/shard_map/ppermute | solution.py:42
  12.8 5.0 %collective-permute-start.5 = (bf16[32,256]{1,0:T(8,128)(2,1)S(1)}, bf16[32,256]{1,0:T(8,128)(2,1)S(1)}, u32[]{:S(2)}, u32[]{:S(2)}) collective-permute-start(bf16[32,256]{1,0:T(8,128)(2,1)S(1)} %get-tuple-element.104.panel_ref), channel_id=1, source_target_pairs={{0,16},{4,20},{8,24},{12,28},{16,0},{20,4},{24,8},{28,12},{1,17},{... | collective-permute-start | bytes 49160 | tf_op jit(solution)/shard_map/ppermute | solution.py:42
  12.9 5.4 %collective-permute-start.4 = (bf16[512,256]{1,0:T(8,128)(2,1)S(1)}, bf16[512,256]{1,0:T(8,128)(2,1)S(1)}, u32[]{:S(2)}, u32[]{:S(2)}) collective-permute-start(bf16[512,256]{1,0:T(8,128)(2,1)S(1)} %get-tuple-element.69), channel_id=1, source_target_pairs={{4,8},{12,16},{20,24},{8,4},{16,12},{24,20},{5,9},{13,17},{21,25},... | collective-permute-start | bytes 786440 | tf_op jit(solution)/shard_map/ppermute | solution.py:46
  14.8 3.0 %collective-permute-start.7 = (bf16[512,256]{1,0:T(8,128)(2,1)S(1)}, bf16[512,256]{1,0:T(8,128)(2,1)S(1)}, u32[]{:S(2)}, u32[]{:S(2)}) collective-permute-start(bf16[512,256]{1,0:T(8,128)(2,1)S(1)} %get-tuple-element.72.refs_0_.refs_10_), channel_id=1, source_target_pairs={{0,1},{1,0},{2,3},{3,2},{4,5},{5,4},{6,7},{7,6},{8,9},{9,8},{10,11... | collective-permute-start | bytes 786440 | tf_op jit(solution)/shard_map/ppermute | solution.py:42
  14.9 2.9 %collective-permute-start.8 = (bf16[512,256]{1,0:T(8,128)(2,1)S(1)}, bf16[512,256]{1,0:T(8,128)(2,1)S(1)}, u32[]{:S(2)}, u32[]{:S(2)}) collective-permute-start(bf16[512,256]{1,0:T(8,128)(2,1)S(1)} %collective-permute-done.2.refs_2_.refs_12_), channel_id=1, source_target_pairs={{0,1},{1,0},{2,3},{3,2},{4,5},{5,4},{6,7},{7,6},{8,9},{9,8},{10,11... | collective-permute-start | bytes 786440 | tf_op jit(solution)/shard_map/ppermute | solution.py:42
  23.3 11.8 %collective-permute-start.11 = (bf16[80,1024]{1,0:T(8,128)(2,1)S(1)}, bf16[80,1024]{1,0:T(8,128)(2,1)S(1)}, u32[]{:S(2)}, u32[]{:S(2)}) collective-permute-start(bf16[80,1024]{1,0:T(8,128)(2,1)S(1)} %get-tuple-element.84), channel_id=1, source_target_pairs={{0,4},{4,0},{8,12},{12,8},{16,20},{20,16},{24,28},{28,24},{1,5},{5... | collective-permute-start | bytes 491528 | tf_op jit(solution)/shard_map/ppermute | solution.py:42
  27.6 7.5 %collective-permute-start.12 = (bf16[80,1024]{1,0:T(8,128)(2,1)S(1)}, bf16[80,1024]{1,0:T(8,128)(2,1)S(1)}, u32[]{:S(2)}, u32[]{:S(2)}) collective-permute-start(bf16[80,1024]{1,0:T(8,128)(2,1)S(1)} %get-tuple-element.85), channel_id=1, source_target_pairs={{0,8},{4,12},{8,0},{12,4},{16,24},{20,28},{24,16},{28,20},{1,9},{5... | collective-permute-start | bytes 491528 | tf_op jit(solution)/shard_map/ppermute | solution.py:42
  29.4 7.4 %collective-permute-start.13 = (bf16[80,1024]{1,0:T(8,128)(2,1)S(1)}, bf16[80,1024]{1,0:T(8,128)(2,1)S(1)}, u32[]{:S(2)}, u32[]{:S(2)}) collective-permute-start(bf16[80,1024]{1,0:T(8,128)(2,1)S(1)} %get-tuple-element.86), channel_id=1, source_target_pairs={{0,12},{4,8},{8,4},{12,0},{16,28},{20,24},{24,20},{28,16},{1,13},{... | collective-permute-start | bytes 491528 | tf_op jit(solution)/shard_map/ppermute | solution.py:42
  30.3 19.8 %collective-permute-start.9 = (bf16[1024,256]{1,0:T(8,128)(2,1)S(1)}, bf16[1024,256]{1,0:T(8,128)(2,1)S(1)}, u32[]{:S(2)}, u32[]{:S(2)}) collective-permute-start(bf16[1024,256]{1,0:T(8,128)(2,1)S(1)} %get-tuple-element.75), channel_id=1, source_target_pairs={{0,1},{1,0},{2,3},{3,2},{4,5},{5,4},{6,7},{7,6},{8,9},{9,8},{10,11... | collective-permute-start | bytes 1572872 | tf_op jit(solution)/shard_map/ppermute | solution.py:42
  36.8 15.3 %collective-permute-start.14 = (bf16[512,256]{1,0:T(8,128)(2,1)S(1)}, bf16[512,256]{1,0:T(8,128)(2,1)S(1)}, u32[]{:S(2)}, u32[]{:S(2)}) collective-permute-start(bf16[512,256]{1,0:T(8,128)(2,1)S(1)} %get-tuple-element.88), channel_id=1, source_target_pairs={{0,4},{8,12},{16,20},{24,28},{4,0},{12,8},{20,16},{28,24},{1,5},{9... | collective-permute-start | bytes 786440 | tf_op jit(solution)/shard_map/ppermute | solution.py:46
  37.9 10.4 %collective-permute-start.16 = (bf16[80,1024]{1,0:T(8,128)(2,1)S(1)}, bf16[80,1024]{1,0:T(8,128)(2,1)S(1)}, u32[]{:S(2)}, u32[]{:S(2)}) collective-permute-start(bf16[80,1024]{1,0:T(8,128)(2,1)S(1)} %get-tuple-element.101.after_ref), channel_id=1, source_target_pairs={{0,16},{4,20},{8,24},{12,28},{16,0},{20,4},{24,8},{28,12},{1,17},{... | collective-permute-start | bytes 491528 | tf_op jit(solution)/shard_map/ppermute | solution.py:42
  40.0 13.6 %collective-permute-start.15 = (bf16[512,256]{1,0:T(8,128)(2,1)S(1)}, bf16[512,256]{1,0:T(8,128)(2,1)S(1)}, u32[]{:S(2)}, u32[]{:S(2)}) collective-permute-start(bf16[512,256]{1,0:T(8,128)(2,1)S(1)} %shard_map.159), channel_id=1, source_target_pairs={{4,8},{12,16},{20,24},{8,4},{16,12},{24,20},{5,9},{13,17},{21,25},... | collective-permute-start | bytes 786440 | tf_op jit(solution)/shard_map/ppermute | solution.py:46
  48.3 6.8 %collective-permute-start.19 = (bf16[64,1024]{1,0:T(8,128)(2,1)S(1)}, bf16[64,1024]{1,0:T(8,128)(2,1)S(1)}, u32[]{:S(2)}, u32[]{:S(2)}) collective-permute-start(bf16[64,1024]{1,0:T(8,128)(2,1)S(1)} %fusion.1.refs_0_), channel_id=1, source_target_pairs={{0,12},{4,8},{8,4},{12,0},{16,28},{20,24},{24,20},{28,16},{1,13},{... | collective-permute-start | bytes 393224 | tf_op jit(solution)/shard_map/ppermute | solution.py:42
  49.0 8.3 %collective-permute-start.18 = (bf16[64,1024]{1,0:T(8,128)(2,1)S(1)}, bf16[64,1024]{1,0:T(8,128)(2,1)S(1)}, u32[]{:S(2)}, u32[]{:S(2)}) collective-permute-start(bf16[64,1024]{1,0:T(8,128)(2,1)S(1)} %fusion.1.refs_0_), channel_id=1, source_target_pairs={{0,8},{4,12},{8,0},{12,4},{16,24},{20,28},{24,16},{28,20},{1,9},{5... | collective-permute-start | bytes 393224 | tf_op jit(solution)/shard_map/ppermute | solution.py:42
  50.1 7.1 %collective-permute-start.17 = (bf16[64,1024]{1,0:T(8,128)(2,1)S(1)}, bf16[64,1024]{1,0:T(8,128)(2,1)S(1)}, u32[]{:S(2)}, u32[]{:S(2)}) collective-permute-start(bf16[64,1024]{1,0:T(8,128)(2,1)S(1)} %fusion.1.refs_0_), channel_id=1, source_target_pairs={{0,4},{4,0},{8,12},{12,8},{16,20},{20,16},{24,28},{28,24},{1,5},{5... | collective-permute-start | bytes 393224 | tf_op jit(solution)/shard_map/ppermute | solution.py:42
  52.1 6.4 %collective-permute-start.10 = (bf16[512,256]{1,0:T(8,128)(2,1)S(1)}, bf16[512,256]{1,0:T(8,128)(2,1)S(1)}, u32[]{:S(2)}, u32[]{:S(2)}) collective-permute-start(bf16[512,256]{1,0:T(8,128)(2,1)S(1)} %slice.45), channel_id=1, source_target_pairs={{0,2},{1,3},{2,0},{3,1},{4,6},{5,7},{6,4},{7,5},{8,10},{9,11},{10,... | collective-permute-start | bytes 786440 | tf_op jit(solution)/shard_map/ppermute | solution.py:42

commit v5 on v4

--- a/solution.py
+++ b/solution.py
@@ -286,18 +286,18 @@
         part = mm(attn, w_ref[:, lanes]).astype(BF)
         target = mix_send if j & 1 else mix_keep
         target[(j >> 1) * tok : ((j >> 1) + 1) * tok] = part
-    across = gw_all.shape[1] // width
+    across = gw_all.shape[1] // (2 * width)
     for m, target in enumerate(segments):
-        target[:chunk] = gw_all[m * chunk : (m + 1) * chunk]
-        if (coarse // rows) >> levels < across:
-            target[chunk:] = jnp.zeros_like(target[chunk:])
-    for j in range(coarse // rows):
-        t = j >> levels
-        base = chunk + (t // across) * 2 * rows
-        lanes = slice((t % across) * width, (t % across + 1) * width)
-        both = [coarse_k[j * rows : (j + 1) * rows], coarse_v[j * rows : (j + 1) * rows]]
-        target = segments[j & ((1 << levels) - 1)]
-        target[base : base + 2 * rows, lanes] = jnp.concatenate(both, 0).astype(BF)
+        cells = []
+        for j in range(m, coarse // rows, 1 << levels):
+            span = slice(j * rows, (j + 1) * rows)
+            cells.append(jnp.concatenate([coarse_k[span], coarse_v[span]], 1))
+        cells = cells + [jnp.zeros_like(cells[0])] * (-len(cells) % across)
+        lines = [
+            jnp.concatenate(cells[t : t + across], 1) for t in range(0, len(cells), across)
+        ]
+        own = gw_all[m * chunk : (m + 1) * chunk].astype(F32)
+        target[...] = jnp.concatenate([own] + lines, 0).astype(BF)
 
 
 def backward_kernel(rows, *refs):
@@ -352,13 +352,13 @@
     member = membership(pool_ref, rows).astype(F32)
     counts = jnp.sum(member, axis=1, keepdims=True)
     member = member.astype(BF)
-    ck_ref[...] = coarse_ref[0:rows]
-    cv_ref[...] = coarse_ref[rows:]
+    ck_ref[...] = coarse_ref[:, :width]
+    cv_ref[...] = coarse_ref[:, width:]
     member = jnp.concatenate([member, member], 0)
     near = pl.ds(pl.multiple_of((1 - odd) * (tok - RIM), RIM), RIM)
     far = pl.ds(pl.multiple_of(odd * (tok - RIM), RIM), RIM)
     for which, out in ((0, gk_ref), (1, gv_ref)):
-        per_row = coarse_ref[which * rows : (which + 1) * rows] / counts
+        per_row = coarse_ref[:, which * width : (which + 1) * width] / counts
         high = per_row.astype(BF)
         low = (per_row - high.astype(F32)).astype(BF)
         pooled = t_mm(member, jnp.concatenate([high, low], 0))
@@ -470,9 +470,9 @@
             neighbors,
         )
     ]
-    across = head
+    across = head // 2
     slots = 1 << levels
-    held = (pix // slots + across - 1) // across * 2 * rows
+    held = (pix // slots + across - 1) // across * rows
     chunk = width // slots
     segment = chunk + held
 
@@ -559,12 +559,12 @@
         flops=3_000_000_000,
         bytes_accessed=4_000_000,
     )(to_far, sent)
-    cells = cut(whole[chunk:], 2 * rows, width, pix // slots)
+    cells = cut(whole[chunk:], rows, 2 * width, pix // slots)
     part = whole[:chunk]
     for bit in bits[levels:]:
         got = swap(sent, "pix", bit).astype(F32)
         part = part + got[:chunk]
-        other = cut(got[chunk:], 2 * rows, width, len(cells))
+        other = cut(got[chunk:], rows, 2 * width, len(cells))
         cells = [cells[t] + other[t ^ 1] for t in range(0, len(cells), 2)]
         if len(cells) > 1:
             empty = [jnp.zeros_like(cells[0])] * (-len(cells) % across)

time: 59.5 us -> 59.5 us (level)
  transfers between devices with their start and end apart: 20 -> 20, of which waited for: 6 -> 5; matrix products, arithmetic and copies ran while one was open for 1% -> 1% of each run, Pallas kernels for 15% -> 15%
where the time goes in v5:
time: 59.5 us; the launch traced here: 59.3 us
  starting transfers between devices  27.7 us (47%)
  Pallas kernels  15.4 us (26%)
  waiting for transfers between devices  14.3 us (24%)
  other arithmetic  1.04 us (2%)
  between operations  0.82 us (1%)
    ppermute x16, starting transfers between devices, swap(): lax.ppermute(value, axis, [(i, i ^ bit) for i in range(lax.axis_size(axis...  23.5 us
    ppermute x16, waiting for transfers between devices, swap(): lax.ppermute(value, axis, [(i, i ^ bit) for i in range(lax.axis_size(axis...  14.3 us
    pallas_call x1, Pallas kernels, run_forward(): call(functools.partial(forward_kernel, rows, levels), kept + [((head // 2...  5 us
    pallas_call x1, Pallas kernels, run_backward(): call(functools.partial(backward_kernel, rows), [((tok, width), BF), ((2 *...  4.74 us
    ppermute x4, starting transfers between devices, exchange(): return lax.ppermute(value, 'pix', pairs + [(b, a) for a, b in pairs])  4.27 us
    pallas_call x1, Pallas kernels, on_device(): call(finish_kernel, [((tok, width), BF), ((tok, width), BF), ((rows, widt...  1.52 us
    pallas_call x1, Pallas kernels, on_device(): call(prep_kernel, [((tok, width), BF), ((tok, width), BF), ((2 * rows, wi...  1.28 us
    pallas_call x1, Pallas kernels, on_device(): call(load_kernel, [((tok, width), BF), ((tok, width), BF), ((width, d_mod...  1.24 us
  transfers between devices with their start and end apart: 20, of which 5 were waited for; matrix products, arithmetic and copies ran while one was open for 1% of the time, Pallas kernels for 15%

profile of v5, /device:TPU:0, one launch (start us, length us, event | category | flops | bytes accessed | tf_op | source)
XLA Modules:
  0.0 59.3 jit_solution(3026436275325173038)
XLA Ops:
  0.6 1.3 %shard_map.153 = (bf16[512,256]{1,0:T(8,128)(2,1)S(1)}, bf16[512,256]{1,0:T(8,128)(2,1)S(1)}, bf16[16,256]{1,0:T(8,128)(2,1)S(1)}, s32[1,512]{1,0:T(1,128)S(1)}) custom-call(bf16[512,256]{1,0:T(8,128)(2,1)} %k_hbm.1, bf16[512,256]{1,0:T(8,128)(2,1)} %v_hbm.1, bf16[8,256]{1,0:T(8,128)(2,1)} %ck_hbm.1, bf16[8,256]{1,0:T(8,128)(2,1)} %cv_hbm.1, s32[1,512]{1,0:T(1,128)} %bitcast.1), custom_call_target="tpu_custom_call" | custom-call | tf_op jit(solution)/shard_map/pallas_call | solution.py:479
  1.9 3.0 %collective-permute-start = (bf16[16,256]{1,0:T(8,128)(2,1)S(1)}, bf16[16,256]{1,0:T(8,128)(2,1)S(1)}, u32[]{:S(2)}, u32[]{:S(2)}) collective-permute-start(bf16[16,256]{1,0:T(8,128)(2,1)S(1)} %get-tuple-element.55), channel_id=1, source_target_pairs={{0,4},{4,0},{8,12},{12,8},{16,20},{20,16},{24,28},{28,24},{1,5},{5... | collective-permute-start | bytes 24584 | tf_op jit(solution)/shard_map/ppermute | solution.py:42
  5.0 1.5 %collective-permute-start.2 = (bf16[512,256]{1,0:T(8,128)(2,1)}, bf16[512,256]{1,0:T(8,128)(2,1)S(1)}, u32[]{:S(2)}, u32[]{:S(2)}) collective-permute-start(bf16[512,256]{1,0:T(8,128)(2,1)} %refs_1_), channel_id=1, source_target_pairs={{0,2},{1,3},{2,0},{3,1},{4,6},{5,7},{6,4},{7,5},{8,10},{9,11},{10,... | collective-permute-start | bytes 786440 | tf_op jit(solution)/shard_map/ppermute | solution.py:42
  6.4 0.1 collective-permute-done
  6.6 2.1 %collective-permute-start.3 = (bf16[512,256]{1,0:T(8,128)(2,1)S(1)}, bf16[512,256]{1,0:T(8,128)(2,1)S(1)}, u32[]{:S(2)}, u32[]{:S(2)}) collective-permute-start(bf16[512,256]{1,0:T(8,128)(2,1)S(1)} %get-tuple-element.67), channel_id=1, source_target_pairs={{0,4},{8,12},{16,20},{24,28},{4,0},{12,8},{20,16},{28,24},{1,5},{9... | collective-permute-start | bytes 786440 | tf_op jit(solution)/shard_map/ppermute | solution.py:46
  8.7 1.6 %collective-permute-start.1 = (bf16[32,256]{1,0:T(8,128)(2,1)S(1)}, bf16[32,256]{1,0:T(8,128)(2,1)S(1)}, u32[]{:S(2)}, u32[]{:S(2)}) collective-permute-start(bf16[32,256]{1,0:T(8,128)(2,1)S(1)} %get-tuple-element.104.panel_ref), channel_id=1, source_target_pairs={{0,8},{4,12},{8,0},{12,4},{16,24},{20,28},{24,16},{28,20},{1,9},{5... | collective-permute-start | bytes 49160 | tf_op jit(solution)/shard_map/ppermute | solution.py:42
  10.3 2.5 %collective-permute-start.6 = (bf16[32,256]{1,0:T(8,128)(2,1)S(1)}, bf16[32,256]{1,0:T(8,128)(2,1)S(1)}, u32[]{:S(2)}, u32[]{:S(2)}) collective-permute-start(bf16[32,256]{1,0:T(8,128)(2,1)S(1)} %get-tuple-element.104.panel_ref), channel_id=1, source_target_pairs={{0,24},{4,28},{8,16},{12,20},{16,8},{20,12},{24,0},{28,4},{1,25},{... | collective-permute-start | bytes 49160 | tf_op jit(solution)/shard_map/ppermute | solution.py:42
  12.8 0.1 collective-permute-start.5
  12.9 0.0 collective-permute-done.1
  12.9 0.7 %collective-permute-start.4 = (bf16[512,256]{1,0:T(8,128)(2,1)S(1)}, bf16[512,256]{1,0:T(8,128)(2,1)S(1)}, u32[]{:S(2)}, u32[]{:S(2)}) collective-permute-start(bf16[512,256]{1,0:T(8,128)(2,1)S(1)} %get-tuple-element.69), channel_id=1, source_target_pairs={{4,8},{12,16},{20,24},{8,4},{16,12},{24,20},{5,9},{13,17},{21,25},... | collective-permute-start | bytes 786440 | tf_op jit(solution)/shard_map/ppermute | solution.py:46
  13.6 1.2 %shard_map.155 = (bf16[512,256]{1,0:T(8,128)(2,1)S(1)}, bf16[512,256]{1,0:T(8,128)(2,1)S(1)}, bf16[256,1024]{1,0:T(8,128)(2,1)S(1)}, s32[4,8]{1,0:T(4,128)S(1)}) custom-call(bf16[512,256]{1,0:T(8,128)(2,1)} %refs_0_.2, bf16[512,256]{1,0:T(8,128)(2,1)} %refs_1_, bf16[256,1024]{1,0:T(8,128)(2,1)} %refs_2_, s32[4,8]{1,0:T(4,128)} %refs_3_), custom_call_target="tpu_custom_call" | custom-call | tf_op jit(solution)/shard_map/pallas_call | solution.py:508
  14.8 0.0 collective-permute-done.2.refs_2_.refs_12_
  14.8 0.0 collective-permute-done.3.refs_5_
  14.8 0.1 collective-permute-start.7
  14.9 0.5 collective-permute-start.8
  15.4 2.4 %collective-permute-done.5 = bf16[32,256]{1,0:T(8,128)(2,1)S(1)} collective-permute-done((bf16[32,256]{1,0:T(8,128)(2,1)S(1)}, bf16[32,256]{1,0:T(8,128)(2,1)S(1)}, u32[]{:S(2)}, u32[]{:S(2)}) %collective-permute-start.5) | collective-permute-done | bytes 16416 | tf_op jit(solution)/shard_map/ppermute | solution.py:42
  17.8 0.0 collective-permute-done.6
  17.8 0.0 collective-permute-done.7.refs_1_.refs_11_
  17.8 0.0 collective-permute-done.8.refs_3_.refs_13_
  17.8 0.5 shard_map.156.refs_9_
  18.3 0.0 collective-permute-done.4.refs_6_
  18.3 5.0 %shard_map.157 = (bf16[4,512,576]{2,1,0:T(8,128)(2,1)S(1)}, bf16[4,512,256]{2,1,0:T(8,128)(2,1)S(1)}, bf16[4,512,256]{2,1,0:T(8,128)(2,1)S(1)}, f32[4,512,1]{2,1...) custom-call(s32[4,4]{1,0:T(4,128)} %refs_0_.4, ...), custom_call_target="tpu_custom_call" | custom-call | flops 1744830464 | bytes 10000000 | tf_op jit(solution)/shard_map/pallas_call | solution.py:397
  23.3 4.3 %collective-permute-start.11 = (bf16[72,1024]{1,0:T(8,128)(2,1)S(1)}, bf16[72,1024]{1,0:T(8,128)(2,1)S(1)}, u32[]{:S(2)}, u32[]{:S(2)}) collective-permute-start(bf16[72,1024]{1,0:T(8,128)(2,1)S(1)} %get-tuple-element.84), channel_id=1, source_target_pairs={{0,4},{4,0},{8,12},{12,8},{16,20},{20,16},{24,28},{28,24},{1,5},{5... | collective-permute-start | bytes 442376 | tf_op jit(solution)/shard_map/ppermute | solution.py:42
  27.6 1.8 %collective-permute-start.12 = (bf16[72,1024]{1,0:T(8,128)(2,1)S(1)}, bf16[72,1024]{1,0:T(8,128)(2,1)S(1)}, u32[]{:S(2)}, u32[]{:S(2)}) collective-permute-start(bf16[72,1024]{1,0:T(8,128)(2,1)S(1)} %get-tuple-element.85), channel_id=1, source_target_pairs={{0,8},{4,12},{8,0},{12,4},{16,24},{20,28},{24,16},{28,20},{1,9},{5... | collective-permute-start | bytes 442376 | tf_op jit(solution)/shard_map/ppermute | solution.py:42
  29.4 1.0 %collective-permute-start.13 = (bf16[72,1024]{1,0:T(8,128)(2,1)S(1)}, bf16[72,1024]{1,0:T(8,128)(2,1)S(1)}, u32[]{:S(2)}, u32[]{:S(2)}) collective-permute-start(bf16[72,1024]{1,0:T(8,128)(2,1)S(1)} %get-tuple-element.86), channel_id=1, source_target_pairs={{0,12},{4,8},{8,4},{12,0},{16,28},{20,24},{24,20},{28,16},{1,13},{... | collective-permute-start | bytes 442376 | tf_op jit(solution)/shard_map/ppermute | solution.py:42
  30.4 0.0 collective-permute-start.9
  30.4 4.7 %shard_map.158 = (bf16[512,256]{1,0:T(8,128)(2,1)}, f32[1024,256]{1,0:T(8,128)S(1)}, bf16[512,256]{1,0:T(8,128)(2,1)S(1)}, f32[512,256]{1,0:T(8,128)S(1)}) custom-call(s32[4,4]{1,0:T(4,128)} %refs_0_.4, bf16[128,256]{1,0:T(8,128)(2,1)S(1)} %constant_dynamic-update-slice_fusion.2.refs_7_.refs_1_, bf16[4,512,576]{2,1,0:T(8,128)(2,1)S(1)} %get-tuple-element.76.refs_2_, ...), custom_call_target="tpu_custom_call" | custom-call | flops 2415919104 | bytes 10000000 | tf_op jit(solution)/shard_map/pallas_call | solution.py:418
  35.1 0.0 collective-permute-done.11
  35.1 0.0 collective-permute-done.12
  35.1 1.1 %collective-permute-done.13 = bf16[72,1024]{1,0:T(8,128)(2,1)S(1)} collective-permute-done((bf16[72,1024]{1,0:T(8,128)(2,1)S(1)}, bf16[72,1024]{1,0:T(8,128)(2,1)S(1)}, u32[]{:S(2)}, u32[]{:S(2)}) %collective-permute-start.13) | collective-permute-done | bytes 147488 | tf_op jit(solution)/shard_map/ppermute | solution.py:42
  36.2 0.8 %collective-permute-start.14 = (bf16[512,256]{1,0:T(8,128)(2,1)S(1)}, bf16[512,256]{1,0:T(8,128)(2,1)S(1)}, u32[]{:S(2)}, u32[]{:S(2)}) collective-permute-start(bf16[512,256]{1,0:T(8,128)(2,1)S(1)} %get-tuple-element.88), channel_id=1, source_target_pairs={{0,4},{8,12},{16,20},{24,28},{4,0},{12,8},{20,16},{28,24},{1,5},{9... | collective-permute-start | bytes 786440 | tf_op jit(solution)/shard_map/ppermute | solution.py:46
  37.1 0.1 fusion.2
  37.2 2.0 %collective-permute-start.16 = (bf16[72,1024]{1,0:T(8,128)(2,1)S(1)}, bf16[72,1024]{1,0:T(8,128)(2,1)S(1)}, u32[]{:S(2)}, u32[]{:S(2)}) collective-permute-start(bf16[72,1024]{1,0:T(8,128)(2,1)S(1)} %get-tuple-element.101.after_ref), channel_id=1, source_target_pairs={{0,16},{4,20},{8,24},{12,28},{16,0},{20,4},{24,8},{28,12},{1,17},{... | collective-permute-start | bytes 442376 | tf_op jit(solution)/shard_map/ppermute | solution.py:42
  39.3 0.7 %collective-permute-start.15 = (bf16[512,256]{1,0:T(8,128)(2,1)S(1)}, bf16[512,256]{1,0:T(8,128)(2,1)S(1)}, u32[]{:S(2)}, u32[]{:S(2)}) collective-permute-start(bf16[512,256]{1,0:T(8,128)(2,1)S(1)} %shard_map.159), channel_id=1, source_target_pairs={{4,8},{12,16},{20,24},{8,4},{16,12},{24,20},{5,9},{13,17},{21,25},... | collective-permute-start | bytes 786440 | tf_op jit(solution)/shard_map/ppermute | solution.py:46
  39.9 7.6 %collective-permute-done.16 = bf16[72,1024]{1,0:T(8,128)(2,1)S(1)} collective-permute-done((bf16[72,1024]{1,0:T(8,128)(2,1)S(1)}, bf16[72,1024]{1,0:T(8,128)(2,1)S(1)}, u32[]{:S(2)}, u32[]{:S(2)}) %collective-permute-start.16) | collective-permute-done | bytes 147488 | tf_op jit(solution)/shard_map/ppermute | solution.py:42
  47.6 0.6 %collective-permute-start.19 = (bf16[64,1024]{1,0:T(8,128)(2,1)S(1)}, bf16[64,1024]{1,0:T(8,128)(2,1)S(1)}, u32[]{:S(2)}, u32[]{:S(2)}) collective-permute-start(bf16[64,1024]{1,0:T(8,128)(2,1)S(1)} %fusion.1.refs_0_), channel_id=1, source_target_pairs={{0,12},{4,8},{8,4},{12,0},{16,28},{20,24},{24,20},{28,16},{1,13},{... | collective-permute-start | bytes 393224 | tf_op jit(solution)/shard_map/ppermute | solution.py:42
  48.2 1.2 %collective-permute-start.18 = (bf16[64,1024]{1,0:T(8,128)(2,1)S(1)}, bf16[64,1024]{1,0:T(8,128)(2,1)S(1)}, u32[]{:S(2)}, u32[]{:S(2)}) collective-permute-start(bf16[64,1024]{1,0:T(8,128)(2,1)S(1)} %fusion.1.refs_0_), channel_id=1, source_target_pairs={{0,8},{4,12},{8,0},{12,4},{16,24},{20,28},{24,16},{28,20},{1,9},{5... | collective-permute-start | bytes 393224 | tf_op jit(solution)/shard_map/ppermute | solution.py:42
  49.4 0.0 collective-permute-done.9
  49.4 1.7 %collective-permute-start.17 = (bf16[64,1024]{1,0:T(8,128)(2,1)S(1)}, bf16[64,1024]{1,0:T(8,128)(2,1)S(1)}, u32[]{:S(2)}, u32[]{:S(2)}) collective-permute-start(bf16[64,1024]{1,0:T(8,128)(2,1)S(1)} %fusion.1.refs_0_), channel_id=1, source_target_pairs={{0,4},{4,0},{8,12},{12,8},{16,20},{20,16},{24,28},{28,24},{1,5},{5... | collective-permute-start | bytes 393224 | tf_op jit(solution)/shard_map/ppermute | solution.py:42
  51.2 0.1 convert_add_fusion
  51.3 0.0 collective-permute-done.14.near_ref
  51.3 1.6 %collective-permute-start.10 = (bf16[512,256]{1,0:T(8,128)(2,1)S(1)}, bf16[512,256]{1,0:T(8,128)(2,1)S(1)}, u32[]{:S(2)}, u32[]{:S(2)}) collective-permute-start(bf16[512,256]{1,0:T(8,128)(2,1)S(1)} %slice.45), channel_id=1, source_target_pairs={{0,2},{1,3},{2,0},{3,1},{4,6},{5,7},{6,4},{7,5},{8,10},{9,11},{10,... | collective-permute-start | bytes 786440 | tf_op jit(solution)/shard_map/ppermute | solution.py:42
  52.9 1.5 %shard_map.160 = (bf16[512,256]{1,0:T(8,128)(2,1)}, bf16[512,256]{1,0:T(8,128)(2,1)}, f32[8,256]{1,0:T(8,128)}, f32[8,256]{1,0:T(8,128)}) custom-call(f32[1024,256]{1,0:T(8,128)S(1)} %get-tuple-element.83.own_ref, bf16[512,256]{1,0:T(8,128)(2,1)S(1)} %collective-permute-done.14.near_ref, bf16[512,256]{1,0:T(8,128)(2,1)S(1)} %collective-permute-done.15.far_ref, ...), custom_call_target="tpu_custom_call" | custom-call | flops 3000000000 | bytes 2097152 | tf_op jit(solution)/shard_map/pallas_call | solution.py:598
  54.4 0.0 collective-permute-done.19.refs_3_
  54.4 3.1 %collective-permute-done.18.refs_2_ = bf16[64,1024]{1,0:T(8,128)(2,1)S(1)} collective-permute-done((bf16[64,1024]{1,0:T(8,128)(2,1)S(1)}, bf16[64,1024]{1,0:T(8,128)(2,1)S(1)}, u32[]{:S(2)}, u32[]{:S(2)}) %collective-permute-start.18) | collective-permute-done | bytes 131104 | tf_op jit(solution)/shard_map/ppermute | solution.py:42
  57.5 1.1 %shard_map.161 = f32[256,1024]{1,0:T(8,128)} custom-call(bf16[64,1024]{1,0:T(8,128)(2,1)S(1)} %fusion.1.refs_0_, bf16[64,1024]{1,0:T(8,128)(2,1)S(1)} %collective-permute-done.17.refs_1_, bf16[64,1024]{1,0:T(8,128)(2,1)S(1)} %collective-permute-done.18.refs_2_, bf16[64,1024]{1,0:T(8,128)(2,1)S(1)} %collective-permute-done.19.refs_3_), custom_call_target="tpu_custom_call" | custom-call | bytes 1572864 | tf_op jit(solution)/shard_map/pallas_call | solution.py:580
  58.5 0.0 collective-permute-done.10
  58.5 0.8 %fusion = bf16[512,256]{1,0:T(8,128)(2,1)} fusion(f32[1024,256]{1,0:T(8,128)S(1)} %convert_add_fusion, bf16[512,256]{1,0:T(8,128)(2,1)S(1)} %collective-permute-done.10), kind=kLoop, calls=%fused_computation.3 | loop fusion | flops 393216 | bytes 1048576 | tf_op jit(solution)/shard_map/convert_element_type | solution.py:594
  (13 shorter events, 0.2 us)
Async XLA Ops:
  1.9 4.7 %collective-permute-start = (bf16[16,256]{1,0:T(8,128)(2,1)S(1)}, bf16[16,256]{1,0:T(8,128)(2,1)S(1)}, u32[]{:S(2)}, u32[]{:S(2)}) collective-permute-start(bf16[16,256]{1,0:T(8,128)(2,1)S(1)} %get-tuple-element.55), channel_id=1, source_target_pairs={{0,4},{4,0},{8,12},{12,8},{16,20},{20,16},{24,28},{28,24},{1,5},{5... | collective-permute-start | bytes 24584 | tf_op jit(solution)/shard_map/ppermute | solution.py:42
  5.0 9.9 %collective-permute-start.2 = (bf16[512,256]{1,0:T(8,128)(2,1)}, bf16[512,256]{1,0:T(8,128)(2,1)S(1)}, u32[]{:S(2)}, u32[]{:S(2)}) collective-permute-start(bf16[512,256]{1,0:T(8,128)(2,1)} %refs_1_), channel_id=1, source_target_pairs={{0,2},{1,3},{2,0},{3,1},{4,6},{5,7},{6,4},{7,5},{8,10},{9,11},{10,... | collective-permute-start | bytes 786440 | tf_op jit(solution)/shard_map/ppermute | solution.py:42
  6.6 8.2 %collective-permute-start.3 = (bf16[512,256]{1,0:T(8,128)(2,1)S(1)}, bf16[512,256]{1,0:T(8,128)(2,1)S(1)}, u32[]{:S(2)}, u32[]{:S(2)}) collective-permute-start(bf16[512,256]{1,0:T(8,128)(2,1)S(1)} %get-tuple-element.67), channel_id=1, source_target_pairs={{0,4},{8,12},{16,20},{24,28},{4,0},{12,8},{20,16},{28,24},{1,5},{9... | collective-permute-start | bytes 786440 | tf_op jit(solution)/shard_map/ppermute | solution.py:46
  8.7 4.2 %collective-permute-start.1 = (bf16[32,256]{1,0:T(8,128)(2,1)S(1)}, bf16[32,256]{1,0:T(8,128)(2,1)S(1)}, u32[]{:S(2)}, u32[]{:S(2)}) collective-permute-start(bf16[32,256]{1,0:T(8,128)(2,1)S(1)} %get-tuple-element.104.panel_ref), channel_id=1, source_target_pairs={{0,8},{4,12},{8,0},{12,4},{16,24},{20,28},{24,16},{28,20},{1,9},{5... | collective-permute-start | bytes 49160 | tf_op jit(solution)/shard_map/ppermute | solution.py:42
  10.3 7.5 %collective-permute-start.6 = (bf16[32,256]{1,0:T(8,128)(2,1)S(1)}, bf16[32,256]{1,0:T(8,128)(2,1)S(1)}, u32[]{:S(2)}, u32[]{:S(2)}) collective-permute-start(bf16[32,256]{1,0:T(8,128)(2,1)S(1)} %get-tuple-element.104.panel_ref), channel_id=1, source_target_pairs={{0,24},{4,28},{8,16},{12,20},{16,8},{20,12},{24,0},{28,4},{1,25},{... | collective-permute-start | bytes 49160 | tf_op jit(solution)/shard_map/ppermute | solution.py:42
  12.8 5.0 %collective-permute-start.5 = (bf16[32,256]{1,0:T(8,128)(2,1)S(1)}, bf16[32,256]{1,0:T(8,128)(2,1)S(1)}, u32[]{:S(2)}, u32[]{:S(2)}) collective-permute-start(bf16[32,256]{1,0:T(8,128)(2,1)S(1)} %get-tuple-element.104.panel_ref), channel_id=1, source_target_pairs={{0,16},{4,20},{8,24},{12,28},{16,0},{20,4},{24,8},{28,12},{1,17},{... | collective-permute-start | bytes 49160 | tf_op jit(solution)/shard_map/ppermute | solution.py:42
  12.9 5.4 %collective-permute-start.4 = (bf16[512,256]{1,0:T(8,128)(2,1)S(1)}, bf16[512,256]{1,0:T(8,128)(2,1)S(1)}, u32[]{:S(2)}, u32[]{:S(2)}) collective-permute-start(bf16[512,256]{1,0:T(8,128)(2,1)S(1)} %get-tuple-element.69), channel_id=1, source_target_pairs={{4,8},{12,16},{20,24},{8,4},{16,12},{24,20},{5,9},{13,17},{21,25},... | collective-permute-start | bytes 786440 | tf_op jit(solution)/shard_map/ppermute | solution.py:46
  14.8 3.0 %collective-permute-start.7 = (bf16[512,256]{1,0:T(8,128)(2,1)S(1)}, bf16[512,256]{1,0:T(8,128)(2,1)S(1)}, u32[]{:S(2)}, u32[]{:S(2)}) collective-permute-start(bf16[512,256]{1,0:T(8,128)(2,1)S(1)} %get-tuple-element.72.refs_0_.refs_10_), channel_id=1, source_target_pairs={{0,1},{1,0},{2,3},{3,2},{4,5},{5,4},{6,7},{7,6},{8,9},{9,8},{10,11... | collective-permute-start | bytes 786440 | tf_op jit(solution)/shard_map/ppermute | solution.py:42
  14.9 2.9 %collective-permute-start.8 = (bf16[512,256]{1,0:T(8,128)(2,1)S(1)}, bf16[512,256]{1,0:T(8,128)(2,1)S(1)}, u32[]{:S(2)}, u32[]{:S(2)}) collective-permute-start(bf16[512,256]{1,0:T(8,128)(2,1)S(1)} %collective-permute-done.2.refs_2_.refs_12_), channel_id=1, source_target_pairs={{0,1},{1,0},{2,3},{3,2},{4,5},{5,4},{6,7},{7,6},{8,9},{9,8},{10,11... | collective-permute-start | bytes 786440 | tf_op jit(solution)/shard_map/ppermute | solution.py:42
  23.3 11.8 %collective-permute-start.11 = (bf16[72,1024]{1,0:T(8,128)(2,1)S(1)}, bf16[72,1024]{1,0:T(8,128)(2,1)S(1)}, u32[]{:S(2)}, u32[]{:S(2)}) collective-permute-start(bf16[72,1024]{1,0:T(8,128)(2,1)S(1)} %get-tuple-element.84), channel_id=1, source_target_pairs={{0,4},{4,0},{8,12},{12,8},{16,20},{20,16},{24,28},{28,24},{1,5},{5... | collective-permute-start | bytes 442376 | tf_op jit(solution)/shard_map/ppermute | solution.py:42
  27.6 7.5 %collective-permute-start.12 = (bf16[72,1024]{1,0:T(8,128)(2,1)S(1)}, bf16[72,1024]{1,0:T(8,128)(2,1)S(1)}, u32[]{:S(2)}, u32[]{:S(2)}) collective-permute-start(bf16[72,1024]{1,0:T(8,128)(2,1)S(1)} %get-tuple-element.85), channel_id=1, source_target_pairs={{0,8},{4,12},{8,0},{12,4},{16,24},{20,28},{24,16},{28,20},{1,9},{5... | collective-permute-start | bytes 442376 | tf_op jit(solution)/shard_map/ppermute | solution.py:42
  29.4 6.9 %collective-permute-start.13 = (bf16[72,1024]{1,0:T(8,128)(2,1)S(1)}, bf16[72,1024]{1,0:T(8,128)(2,1)S(1)}, u32[]{:S(2)}, u32[]{:S(2)}) collective-permute-start(bf16[72,1024]{1,0:T(8,128)(2,1)S(1)} %get-tuple-element.86), channel_id=1, source_target_pairs={{0,12},{4,8},{8,4},{12,0},{16,28},{20,24},{24,20},{28,16},{1,13},{... | collective-permute-start | bytes 442376 | tf_op jit(solution)/shard_map/ppermute | solution.py:42
  30.4 19.1 %collective-permute-start.9 = (bf16[1024,256]{1,0:T(8,128)(2,1)S(1)}, bf16[1024,256]{1,0:T(8,128)(2,1)S(1)}, u32[]{:S(2)}, u32[]{:S(2)}) collective-permute-start(bf16[1024,256]{1,0:T(8,128)(2,1)S(1)} %get-tuple-element.75), channel_id=1, source_target_pairs={{0,1},{1,0},{2,3},{3,2},{4,5},{5,4},{6,7},{7,6},{8,9},{9,8},{10,11... | collective-permute-start | bytes 1572872 | tf_op jit(solution)/shard_map/ppermute | solution.py:42
  36.2 15.1 %collective-permute-start.14 = (bf16[512,256]{1,0:T(8,128)(2,1)S(1)}, bf16[512,256]{1,0:T(8,128)(2,1)S(1)}, u32[]{:S(2)}, u32[]{:S(2)}) collective-permute-start(bf16[512,256]{1,0:T(8,128)(2,1)S(1)} %get-tuple-element.88), channel_id=1, source_target_pairs={{0,4},{8,12},{16,20},{24,28},{4,0},{12,8},{20,16},{28,24},{1,5},{9... | collective-permute-start | bytes 786440 | tf_op jit(solution)/shard_map/ppermute | solution.py:46
  37.2 10.3 %collective-permute-start.16 = (bf16[72,1024]{1,0:T(8,128)(2,1)S(1)}, bf16[72,1024]{1,0:T(8,128)(2,1)S(1)}, u32[]{:S(2)}, u32[]{:S(2)}) collective-permute-start(bf16[72,1024]{1,0:T(8,128)(2,1)S(1)} %get-tuple-element.101.after_ref), channel_id=1, source_target_pairs={{0,16},{4,20},{8,24},{12,28},{16,0},{20,4},{24,8},{28,12},{1,17},{... | collective-permute-start | bytes 442376 | tf_op jit(solution)/shard_map/ppermute | solution.py:42
  39.3 13.7 %collective-permute-start.15 = (bf16[512,256]{1,0:T(8,128)(2,1)S(1)}, bf16[512,256]{1,0:T(8,128)(2,1)S(1)}, u32[]{:S(2)}, u32[]{:S(2)}) collective-permute-start(bf16[512,256]{1,0:T(8,128)(2,1)S(1)} %shard_map.159), channel_id=1, source_target_pairs={{4,8},{12,16},{20,24},{8,4},{16,12},{24,20},{5,9},{13,17},{21,25},... | collective-permute-start | bytes 786440 | tf_op jit(solution)/shard_map/ppermute | solution.py:46
  47.6 6.8 %collective-permute-start.19 = (bf16[64,1024]{1,0:T(8,128)(2,1)S(1)}, bf16[64,1024]{1,0:T(8,128)(2,1)S(1)}, u32[]{:S(2)}, u32[]{:S(2)}) collective-permute-start(bf16[64,1024]{1,0:T(8,128)(2,1)S(1)} %fusion.1.refs_0_), channel_id=1, source_target_pairs={{0,12},{4,8},{8,4},{12,0},{16,28},{20,24},{24,20},{28,16},{1,13},{... | collective-permute-start | bytes 393224 | tf_op jit(solution)/shard_map/ppermute | solution.py:42
  48.2 9.3 %collective-permute-start.18 = (bf16[64,1024]{1,0:T(8,128)(2,1)S(1)}, bf16[64,1024]{1,0:T(8,128)(2,1)S(1)}, u32[]{:S(2)}, u32[]{:S(2)}) collective-permute-start(bf16[64,1024]{1,0:T(8,128)(2,1)S(1)} %fusion.1.refs_0_), channel_id=1, source_target_pairs={{0,8},{4,12},{8,0},{12,4},{16,24},{20,28},{24,16},{28,20},{1,9},{5... | collective-permute-start | bytes 393224 | tf_op jit(solution)/shard_map/ppermute | solution.py:42
  49.4 8.1 %collective-permute-start.17 = (bf16[64,1024]{1,0:T(8,128)(2,1)S(1)}, bf16[64,1024]{1,0:T(8,128)(2,1)S(1)}, u32[]{:S(2)}, u32[]{:S(2)}) collective-permute-start(bf16[64,1024]{1,0:T(8,128)(2,1)S(1)} %fusion.1.refs_0_), channel_id=1, source_target_pairs={{0,4},{4,0},{8,12},{12,8},{16,20},{20,16},{24,28},{28,24},{1,5},{5... | collective-permute-start | bytes 393224 | tf_op jit(solution)/shard_map/ppermute | solution.py:42
  51.3 7.2 %collective-permute-start.10 = (bf16[512,256]{1,0:T(8,128)(2,1)S(1)}, bf16[512,256]{1,0:T(8,128)(2,1)S(1)}, u32[]{:S(2)}, u32[]{:S(2)}) collective-permute-start(bf16[512,256]{1,0:T(8,128)(2,1)S(1)} %slice.45), channel_id=1, source_target_pairs={{0,2},{1,3},{2,0},{3,1},{4,6},{5,7},{6,4},{7,5},{8,10},{9,11},{10,... | collective-permute-start | bytes 786440 | tf_op jit(solution)/shard_map/ppermute | solution.py:42
